TPU v7x, 32 devices: a whole 2x2x4 slice. The times are simulated.
32 devices in a mesh: req: 16 (over z, x, core), tp: 2 (over y).
Axes of the slice: x: 2, y: 2, z: 4, core: 2. Of those that a mesh axis runs over, the one named last changes fastest.
Arguments:
- query_new: bfloat16 [64, 2048], P('req', 'tp'), may hold values from -16 to 16
- key_new: bfloat16 [64, 2048], P('req', 'tp'), may hold values from -6 to 6
- value_new: bfloat16 [64, 2048], P('req', 'tp'), may hold values from -6 to 6
- residual: bfloat16 [64, 2048], P('req', 'tp'), may hold values from -3 to 3
- dense_weight: bfloat16 [2048, 2048], P('tp'), may hold values from -1 to 1
- dense_bias: bfloat16 [2048], P('tp'), may hold values from -3 to 3
- key_pool: bfloat16 [384, 128, 2048], P('req', None, 'tp'), may hold values from -8 to 8
- value_pool: bfloat16 [384, 128, 2048], P('req', None, 'tp'), may hold values from -6 to 6
- page_table: int32 [64, 8], P('req'), may hold values from 0 to 23, as said below
- lengths: int32 [64], P('req'), may hold values from 0 to 1023, as said below
- request_slot: int32 [64], P('req'), may hold values from 0 to 63, as said below
- arrival_index: int32 [64], P('req'), may hold values from 0 to 63, as said below
Outputs:
- hidden: bfloat16 [64, 2048], P('req', 'tp')
- appended_keys: bfloat16 [64, 2048], P('req', 'tp')
- appended_values: bfloat16 [64, 2048], P('req', 'tp')
Inputs may be any that keep to these rules, and one draw needn't show every extreme that they name: All entries differ; request_slot[r] is the resident slot of arrival request r, and slot s lies on req device s // 4. arrival_index[s] = r exactly where request_slot[r] = s. `page_table`: the first 2 * ceil((lengths[s] + 1) / 256) entries of a row name pages of its own req device's pool, all different from each other and from those of the other slots of that device; later entries name arbitrary pages of that pool and are not read. The pages that the slots of one req device need, 2 * ceil((lengths[s] + 1) / 256) each, number at most 24 in all.
All inputs are finite; a program needn't handle non-finite values.
Results may differ from a plain program's by a relative error of at most 0.011.
Values may be sent and summed in bfloat16 or wider, within the bound.
No kernel may reach another device: no remote copies, remote signals or barrier semaphores. Data moves between devices by JAX's collectives and lax.ppermute only.
A program may use at most 64 MiB of HBM per device.

v0:
```python
import jax
import jax.numpy as jnp
from jax import lax
from jax.sharding import PartitionSpec as P

HS = 256


def rotate(vectors, positions):
    head_size = vectors.shape[-1]
    rotary_dims = head_size // 4
    half_dims = rotary_dims // 2
    rates = 10000.0 ** (-2.0 * jnp.arange(half_dims, dtype=jnp.float32) / rotary_dims)
    angle = positions.astype(jnp.float32)[:, None] * rates[None, :]
    cosine = jnp.cos(angle)[:, None, :]
    sine = jnp.sin(angle)[:, None, :]
    front_half = vectors[..., :half_dims]
    back_half = vectors[..., half_dims:rotary_dims]
    return jnp.concatenate(
        [
            front_half * cosine - back_half * sine,
            back_half * cosine + front_half * sine,
            vectors[..., rotary_dims:],
        ],
        axis=-1,
    )


def normalize(scores, visible, own_score):
    masked = jnp.where(visible, scores, -jnp.inf)
    top = jnp.maximum(jnp.max(masked, axis=(2, 3)), own_score)
    spread = jnp.exp(masked - top[:, :, None, None])
    own_spread = jnp.exp(own_score - top)
    total = jnp.sum(spread, axis=(2, 3)) + own_spread
    weights = (spread / total[:, :, None, None]).astype(jnp.bfloat16)
    own_weight = (own_spread / total).astype(jnp.bfloat16)
    return (weights, own_weight)


def on_device(
    query_new,
    key_new,
    value_new,
    residual,
    dense_weight,
    dense_bias,
    key_pool,
    value_pool,
    page_table,
    lengths,
    request_slot,
    arrival_index,
):
    rows = query_new.shape[0]
    everyone = rows * lax.axis_size("req")
    width_here = query_new.shape[1]
    heads_here = width_here // HS
    page_rows = key_pool.shape[1]
    table_width = page_table.shape[1]
    scale = HS ** (-0.5)
    pieces = (
        lax.all_gather(query_new, "req", axis=0, tiled=True),
        lax.all_gather(key_new, "req", axis=0, tiled=True),
        lax.all_gather(value_new, "req", axis=0, tiled=True),
    )
    count = pieces[0].shape[0]
    select = (arrival_index[:, None] == jnp.arange(count, dtype=jnp.int32)[None, :]).astype(
        jnp.bfloat16
    )
    moved = tuple((jnp.dot(select, piece, preferred_element_type=jnp.float32) for piece in pieces))
    query = moved[0].astype(jnp.bfloat16)
    own_key = moved[1].astype(jnp.bfloat16)
    appended_values = moved[2].astype(jnp.bfloat16)
    rotated_query = rotate(query.astype(jnp.float32).reshape(rows, heads_here, HS), lengths).astype(
        jnp.bfloat16
    )
    appended_keys = rotate(
        own_key.astype(jnp.float32).reshape(rows, heads_here, HS), lengths
    ).astype(jnp.bfloat16)
    value_heads = appended_values.reshape(rows, heads_here, HS)
    own_score = (
        jnp.einsum("rhd,rhd->rh", rotated_query, appended_keys, preferred_element_type=jnp.float32)
        * scale
    )
    key_pages = key_pool[page_table].reshape(rows, table_width, page_rows, heads_here, HS)
    value_pages = value_pool[page_table].reshape(rows, table_width, page_rows, heads_here, HS)
    scores = (
        jnp.einsum("rhd,rpthd->rhpt", rotated_query, key_pages, preferred_element_type=jnp.float32)
        * scale
    )
    token_place = (
        jnp.arange(table_width, dtype=jnp.int32)[:, None] * page_rows
        + jnp.arange(page_rows, dtype=jnp.int32)[None, :]
    )
    visible = (token_place[None, :, :] < lengths[:, None, None])[:, None, :, :]
    weights, own_weight = normalize(scores, visible, own_score)
    attended = jnp.einsum(
        "rhpt,rpthd->rhd", weights, value_pages, preferred_element_type=jnp.float32
    )
    attended = attended + own_weight.astype(jnp.float32)[:, :, None] * value_heads.astype(
        jnp.float32
    )
    attended = attended.astype(jnp.bfloat16).reshape(rows, width_here)
    partial_terms = jnp.dot(attended, dense_weight, preferred_element_type=jnp.float32)
    projected = lax.psum_scatter(partial_terms, "tp", scatter_dimension=1, tiled=True).astype(
        jnp.bfloat16
    )
    place_back = (jnp.arange(everyone, dtype=jnp.int32)[:, None] == arrival_index[None, :]).astype(
        jnp.bfloat16
    )
    returned = lax.psum_scatter(
        jnp.dot(place_back, projected, preferred_element_type=jnp.float32),
        "req",
        scatter_dimension=0,
        tiled=True,
    )
    hidden = (
        residual.astype(jnp.float32) + dense_bias.astype(jnp.float32)[None, :] + returned
    ).astype(jnp.bfloat16)
    return (hidden, appended_keys.reshape(rows, width_here), appended_values)


def solution(mesh):
    in_specs = (
        P("req", "tp"),
        P("req", "tp"),
        P("req", "tp"),
        P("req", "tp"),
        P("tp", None),
        P("tp"),
        P("req", None, "tp"),
        P("req", None, "tp"),
        P("req", None),
        P("req"),
        P("req"),
        P("req"),
    )
    out_specs = (P("req", "tp"), P("req", "tp"), P("req", "tp"))
    return jax.shard_map(
        on_device, mesh=mesh, in_specs=in_specs, out_specs=out_specs, check_vma=False
    )
```

profile of v0, /device:TPU:0, one launch (start us, length us, event | category | flops | bytes accessed | tf_op | source)
XLA Modules:
  0.0 249.7 jit_solution(7350536747056859989)
XLA Ops:
  7.2 0.0 reduce-scatter.4.cloned.1.call-start
  7.2 23.7 %all-gather = bf16[16,4,1024]{2,1,0:T(4,128)(2,1)S(1)} all-gather(bf16[1,4,1024]{2,1,0:T(4,128)(2,1)} %bitcast.36), channel_id=1, replica_groups=mesh['req'=16,'tp'=2] {'req'}, dimensions={0}, use_global_device_ids=true | all-gather | bytes 139264 | tf_op jit(solution)/shard_map/all_gather | solution.py:62
  30.9 0.8 convolution_convert_fusion.2
  31.8 0.1 slice.31
  31.9 0.7 convert_element_type.58
  32.5 18.0 %all-gather.1 = bf16[16,4,1024]{2,1,0:T(4,128)(2,1)S(1)} all-gather(bf16[1,4,1024]{2,1,0:T(4,128)(2,1)} %bitcast.37), channel_id=1, replica_groups=mesh['req'=16,'tp'=2] {'req'}, dimensions={0}, use_global_device_ids=true | all-gather | bytes 139264 | tf_op jit(solution)/shard_map/all_gather | solution.py:63
  50.6 0.8 fusion.4
  51.5 0.1 slice.34
  51.5 0.1 multiply_cosine_fusion
  51.7 0.1 multiply_subtract_fusion
  51.7 0.1 subtract_convert_fusion
  51.8 0.7 compare_select_fusion
  52.5 0.1 reshape.127
  52.6 7.8 %gather_fusion = bf16[32,128,1024]{2,1,0:T(8,128)(2,1)} fusion(bf16[24,128,1024]{2,1,0:T(8,128)(2,1)} %param.18, s32[1024]{0:T(1024)S(1)} %pad_clamp_fusion), kind=kCustom, calls=%fused_computation | custom fusion | bytes 16777344 | tf_op jit(solution)/shard_map/gather | solution.py:85
  60.4 14.6 %reshape.117 = bf16[4,8,128,4,256]{4,3,2,1,0:T(4,128)(2,1)} reshape(bf16[32,128,1024]{2,1,0:T(8,128)(2,1)} %gather_fusion) | data formatting | bytes 16777216 | tf_op jit(solution)/shard_map/reshape | solution.py:85
  75.0 0.1 iota_add_fusion
  75.1 0.0 copy-done.6
  75.1 0.1 broadcast_compare_fusion
  75.2 0.1 fusion.22
  75.3 5.6 %fusion.2 = f32[4,4,1,8,128]{4,2,3,1,0:T(1,128)S(1)} fusion(bf16[4,8,128,4,256]{4,3,2,1,0:T(4,128)(2,1)} %reshape.117, bf16[4,4,256,1,1]{2,1,0,3,4:T(4,128)(2,1)S(1)} %fusion.22), kind=kOutput, calls=%fused_computation.4 | convolution fusion | flops 8388608 | bytes 8462336 | tf_op jit(solution)/shard_map/rhd,rpthd->rhpt/dot_general | solution.py:88
  80.9 0.1 fusion.6
  81.0 0.2 fusion.12
  81.2 0.2 fusion.7
  81.4 0.1 fusion.8
  81.6 7.8 %gather_fusion.1 = bf16[32,128,1024]{2,1,0:T(8,128)(2,1)} fusion(bf16[24,128,1024]{2,1,0:T(8,128)(2,1)} %param.19, s32[1024]{0:T(1024)S(1)} %pad_clamp_fusion), kind=kCustom, calls=%fused_computation.1 | custom fusion | bytes 16777344 | tf_op jit(solution)/shard_map/gather | solution.py:86
  89.4 14.6 %reshape.120 = bf16[4,8,128,4,256]{4,3,2,1,0:T(4,128)(2,1)} reshape(bf16[32,128,1024]{2,1,0:T(8,128)(2,1)} %gather_fusion.1) | data formatting | bytes 16777216 | tf_op jit(solution)/shard_map/reshape | solution.py:86
  104.0 0.0 copy-done.1
  104.0 19.2 %all-gather.2 = bf16[16,4,1024]{2,1,0:T(4,128)(2,1)S(1)} all-gather(bf16[1,4,1024]{2,1,0:T(4,128)(2,1)S(1)} %bitcast.38), channel_id=1, replica_groups=mesh['req'=16,'tp'=2] {'req'}, dimensions={0}, use_global_device_ids=true | all-gather | bytes 139264 | tf_op jit(solution)/shard_map/all_gather | solution.py:64
  123.3 0.0 copy-done.5
  123.3 0.2 convolution_convert_fusion
  123.5 0.0 copy-start
  123.5 4.7 %fusion = f32[4,4,1,256,1]{3,2,4,1,0:T(1,128)S(1)} fusion(bf16[4,8,128,4,256]{4,3,2,1,0:T(4,128)(2,1)} %reshape.120, bf16[4,4,8,128,1]{3,2,1,0,4:T(8,128)(2,1)S(1)} %fusion.8), kind=kOutput, calls=%fused_computation.2 | convolution fusion | flops 8388608 | bytes 8437760 | tf_op jit(solution)/shard_map/rhpt,rpthd->rhd/dot_general | solution.py:97
  128.2 0.1 fusion.15
  128.3 0.0 copy-done
  128.3 2.7 %convolution_bitcast_fusion = f32[2048,4]{1,0:T(8,128)} fusion(bf16[4,1024]{1,0:T(4,128)(2,1)S(1)} %bitcast.34, bf16[1024,2048]{1,0:T(8,128)(2,1)S(1)} %copy-done), kind=kOutput, calls=%fused_computation.6 | convolution fusion | flops 16777216 | bytes 4235264
  131.1 0.0 reduce-scatter.4.cloned.1.call-update
  131.1 0.0 all-reduce.3.cloned.1.call-start
  131.1 17.7 %reduce-scatter.4.cloned.1.call-done = f32[1024,4]{1,0:T(8,128)} async-done(((f32[2048,4]{1,0:T(8,128)}), f32[1024,4]{1,0:T(8,128)}) %reduce-scatter.4.cloned.1.call-update) | async-done | bytes 16400
  148.9 1.2 copy.26
  150.1 0.9 fusion.9
  151.0 0.0 all-reduce.3.cloned.1.call-update
  151.0 0.0 copy-done.4
  151.0 0.6 copy.28
  151.6 0.6 dynamic-slice
  152.9 88.6 %all-reduce.3.cloned.1.call-done = f32[64,1024]{1,0:T(8,128)} async-done(((f32[64,1024]{1,0:T(8,128)}), f32[64,1024]{1,0:T(8,128)}) %all-reduce.3.cloned.1.call-update) | async-done | bytes 262160
  241.5 0.0 copy-done.3
  241.5 1.4 fusion.10
  242.8 0.0 copy-done.2
  (22 shorter events, 0.2 us)
Async XLA Ops:
  7.2 141.7 %reduce-scatter.4.cloned.1.call-start = ((), (), s32[]{:S(2)}) async-start(), calls=%async_computation.1 | async-start | bytes 1572864
  60.4 14.7 %copy-start.6 = (s32[4]{0:T(128)S(1)}, s32[4]{0:T(128)}, u32[]{:S(2)}) copy-start(s32[4]{0:T(128)} %param.21) | copy-start | bytes 52
  89.4 14.7 %copy-start.1 = (bf16[4,1024]{1,0:T(4,128)(2,1)S(1)}, bf16[4,1024]{1,0:T(4,128)(2,1)}, u32[]{:S(2)}) copy-start(bf16[4,1024]{1,0:T(4,128)(2,1)} %param.14) | copy-start | bytes 24580
  89.4 33.9 %copy-start.5 = (s32[4]{0:T(128)S(1)}, s32[4]{0:T(128)}, u32[]{:S(2)}) copy-start(s32[4]{0:T(128)} %param.22) | copy-start | bytes 52
  104.0 47.0 %copy-start.4 = (bf16[1024]{0:T(1024)(128)(2,1)S(1)}, bf16[1024]{0:T(1024)(128)(2,1)}, u32[]{:S(2)}) copy-start(bf16[1024]{0:T(1024)(128)(2,1)} %param.17) | copy-start | bytes 6148
  104.0 47.6 %copy-start.7 = (u32[32]{0:T(128)S(1)}, u32[32]{0:T(128)}, u32[]{:S(2)}) copy-start(u32[32]{0:T(128)} %constant.32) | copy-start | bytes 388
  104.0 137.4 %copy-start.3 = (bf16[4,1024]{1,0:T(4,128)(2,1)S(1)}, bf16[4,1024]{1,0:T(4,128)(2,1)}, u32[]{:S(2)}) copy-start(bf16[4,1024]{1,0:T(4,128)(2,1)} %param.15) | copy-start | bytes 24580
  123.5 119.3 %copy-start.2 = (bf16[4,1024]{1,0:T(4,128)(2,1)}, bf16[4,1024]{1,0:T(4,128)(2,1)S(1)}, u32[]{:S(2)}) copy-start(bf16[4,1024]{1,0:T(4,128)(2,1)S(1)} %convolution_convert_fusion) | copy-start | bytes 24580
  123.5 4.8 %copy-start = (bf16[1024,2048]{1,0:T(8,128)(2,1)S(1)}, bf16[1024,2048]{1,0:T(8,128)(2,1)}, u32[]{:S(2)}) copy-start(bf16[1024,2048]{1,0:T(8,128)(2,1)} %param.16) | copy-start | bytes 12582916
  131.1 110.4 %all-reduce.3.cloned.1.call-start = ((), (), s32[]{:S(2)}) async-start(), calls=%async_computation.2 | async-start | bytes 524288
Sparse Core Ops, SparseCore 0:
  131.2 17.6 reduce-scatter.3
  152.6 88.7 all-reduce.2
where the time goes:
time: 251 us; the launch traced here: 250 us
  waiting for transfers between devices  106 us (42%)
  blocking collectives  60.9 us (24%)
  local copies, waits for them, and re-layouts  47.7 us (19%)
  matrix products  15.9 us (6%)
  between operations  14.8 us (6%)
  other arithmetic  3.95 us (2%)
    unnamed x4, waiting for transfers between devices  106 us
    all_gather x1, blocking collectives, on_device(): lax.all_gather(query_new, 'req', axis=0, tiled=True)  23.7 us
    all_gather x1, blocking collectives, on_device(): lax.all_gather(value_new, 'req', axis=0, tiled=True)  19.2 us
    all_gather x1, blocking collectives, on_device(): lax.all_gather(key_new, 'req', axis=0, tiled=True)  18 us
    reshape x1, local copies, waits for them, and re-layouts, on_device(): value_pool[page_table].reshape(rows, table_width, page_rows, heads_here, HS)  14.6 us
    reshape x1, local copies, waits for them, and re-layouts, on_device(): key_pool[page_table].reshape(rows, table_width, page_rows, heads_here, HS)  14.6 us
    gather x1, local copies, waits for them, and re-layouts, on_device(): value_pool[page_table].reshape(rows, table_width, page_rows, heads_here, HS)  7.8 us
    gather x1, local copies, waits for them, and re-layouts, on_device(): key_pool[page_table].reshape(rows, table_width, page_rows, heads_here, HS)  7.79 us
  transfers between devices with their start and end apart: 2, of which 2 were waited for; matrix products, arithmetic and copies ran while one was open for 0% of the time, Pallas kernels for 0%

commit v1 on v0

v1 whole, which is shorter than its diff:
```python
import functools

import jax
import jax.numpy as jnp
from jax import lax
from jax.experimental import pallas as pl
from jax.experimental.pallas import tpu as pltpu
from jax.sharding import PartitionSpec as P

HS = 256
BF16 = jnp.bfloat16
F32 = jnp.float32
ANY = pl.BlockSpec(memory_space=pl.ANY)
VMEM = pl.BlockSpec(memory_space=pltpu.VMEM)
SMEM = pl.BlockSpec(memory_space=pltpu.SMEM)


def gather_by_doubling(block, devices):
    held = block[None]
    bit = devices // 2
    while bit:
        pairs = [(i, i ^ bit) for i in range(devices)]
        held = jnp.concatenate([held, lax.ppermute(held, "req", pairs)], axis=0)
        bit //= 2
    return held


def place_of(owner, me, devices):
    apart = owner ^ me
    place = jnp.int32(0)
    bit, weight = devices // 2, 1
    while bit:
        place = place + jnp.where((apart & bit) != 0, weight, 0)
        bit //= 2
        weight *= 2
    return place


def sum_by_halving(kept, sent, parts):
    bit = parts // 2
    while True:
        kept = kept + lax.ppermute(sent, "tp", [(i, i ^ bit) for i in range(parts)])
        if bit == 1:
            return kept[0]
        bit //= 2
        kept, sent = kept[:bit], kept[bit:]


def take_row(block, row):
    block = block.astype(F32)
    rows = lax.broadcasted_iota(jnp.int32, block.shape, 0)
    return jnp.sum(jnp.where(rows == row, block, 0.0), axis=0, keepdims=True)


def rotary_factors(lengths, heads):
    rotary_dims = HS // 4
    half = rotary_dims // 2
    rates = 10000.0 ** (-2.0 * jnp.arange(half, dtype=F32) / rotary_dims)
    angle = lengths.astype(F32)[:, None] * rates[None, :]
    cosine, sine = jnp.cos(angle), jnp.sin(angle)
    rows = lengths.shape[0]
    none = jnp.zeros((rows, half), F32)
    rest = jnp.zeros((rows, HS - rotary_dims), F32)
    same = jnp.concatenate([cosine, cosine, rest + 1.0], axis=1)
    right = jnp.concatenate([-sine, none, rest], axis=1)
    left = jnp.concatenate([none, sine, rest], axis=1)
    return jnp.stack([jnp.tile(f, (1, heads)) for f in (same, right, left)])


def attend(devices, parts, me_ref, arrival_ref, fresh_ref, factors_ref, table_ref, lengths_ref,
           keys_ref, values_ref, weight_ref, kept_out, sent_out, keys_out, values_out, terms_ref):
    me, half = me_ref[0], me_ref[1]
    slots = table_ref.shape[0]
    width = keys_out.shape[1]
    heads = width // HS
    per = fresh_ref.shape[1]
    pages, page = keys_ref.shape[0], keys_ref.shape[1]
    tokens = pages * page
    scale = HS ** (-0.5)

    taken = []
    for s in range(slots):
        arrival = arrival_ref[s]
        block = fresh_ref[place_of(arrival // per, me, devices)]
        taken.append(take_row(block, arrival % per))
    taken = jnp.concatenate(taken, axis=0)
    query, key, value = (taken[:, i * width:(i + 1) * width] for i in range(3))

    def rotate(x):
        right = pltpu.roll(x, width - HS // 8, 1)
        left = pltpu.roll(x, HS // 8, 1)
        return x * factors_ref[0] + right * factors_ref[1] + left * factors_ref[2]

    query = rotate(query).astype(BF16).astype(F32)
    key = rotate(key).astype(BF16)
    keys_out[...] = key
    values_out[...] = value.astype(BF16)

    rows = heads * slots
    row_head = lax.broadcasted_iota(jnp.int32, (rows, width), 0) // slots
    lane_head = lax.broadcasted_iota(jnp.int32, (rows, width), 1) // HS
    mine = row_head == lane_head
    spread_query = jnp.where(mine, jnp.concatenate([query] * heads, axis=0), 0.0)
    own_score = jnp.sum(
        spread_query * jnp.concatenate([key.astype(F32)] * heads, axis=0), axis=1, keepdims=True
    ) * scale

    lane = lax.broadcasted_iota(jnp.int32, (slots, 128), 1)
    visible = jnp.zeros((slots, 128), jnp.int32)
    for i in range(table_ref.shape[1]):
        left_over = jnp.clip(lengths_ref[...] - i * page, 0, page)
        visible = jnp.where((lane == table_ref[:, i:i + 1]) & (left_over > 0), left_over, visible)
    visible = jnp.concatenate([visible] * heads, axis=0)

    scores = lax.dot_general(
        spread_query.astype(BF16), keys_ref[...].reshape(tokens, width),
        (((1,), (1,)), ((), ())), preferred_element_type=F32,
    ) * scale
    place = lax.broadcasted_iota(jnp.int32, (rows, page), 1)
    masked = jnp.concatenate(
        [
            jnp.where(place < visible[:, p:p + 1], scores[:, p * page:(p + 1) * page], -jnp.inf)
            for p in range(pages)
        ],
        axis=1,
    )
    top = jnp.maximum(jnp.max(masked, axis=1, keepdims=True), own_score)
    exps = jnp.exp(masked - top)
    own_exp = jnp.exp(own_score - top)
    total = jnp.sum(exps, axis=1, keepdims=True) + own_exp
    weights = (exps / total).astype(BF16)
    own_weight = (own_exp / total).astype(BF16).astype(F32)
    attended = jnp.dot(weights, values_ref[...].reshape(tokens, width), preferred_element_type=F32)
    attended = attended + own_weight * jnp.concatenate([value] * heads, axis=0)
    attended = jnp.where(mine, attended, 0.0)
    attended = sum(attended[h * slots:(h + 1) * slots] for h in range(heads)).astype(BF16)

    terms = jnp.dot(attended, weight_ref[...], preferred_element_type=F32)
    for part in range(parts):
        terms_ref[part ^ half] = terms[:, part * width:(part + 1) * width]
    kept_out[...] = terms_ref[:parts // 2]
    sent_out[...] = terms_ref[parts // 2:]


def finish(devices, me_ref, slot_ref, held_ref, residual_ref, bias_ref, out_ref):
    me = me_ref[0]
    per = held_ref.shape[1]
    taken = []
    for r in range(out_ref.shape[0]):
        slot = slot_ref[r]
        taken.append(take_row(held_ref[place_of(slot // per, me, devices)], slot % per))
    taken = jnp.concatenate(taken, axis=0)
    out_ref[...] = (residual_ref[...].astype(F32) + bias_ref[...].astype(F32) + taken).astype(BF16)


def on_device(devices, parts, query_new, key_new, value_new, residual, dense_weight, dense_bias,
              key_pool, value_pool, page_table, lengths, request_slot, arrival_index):
    rows, width = query_new.shape
    heads = width // HS
    me = jnp.stack([lax.axis_index("req"), lax.axis_index("tp")]).astype(jnp.int32)
    fresh = gather_by_doubling(jnp.concatenate([query_new, key_new, value_new], axis=1), devices)
    factors = rotary_factors(lengths, heads)
    half_terms = jax.ShapeDtypeStruct((parts // 2, rows, width), F32)
    kept, sent, appended_keys, appended_values = pl.pallas_call(
        functools.partial(attend, devices, parts),
        out_shape=(
            half_terms,
            half_terms,
            jax.ShapeDtypeStruct((rows, width), BF16),
            jax.ShapeDtypeStruct((rows, width), BF16),
        ),
        scratch_shapes=[pltpu.VMEM((parts, rows, width), F32)],
        in_specs=[SMEM, SMEM, VMEM, VMEM, VMEM, VMEM, VMEM, VMEM, VMEM],
        out_specs=(VMEM,) * 4,
        compiler_params=pltpu.CompilerParams(vmem_limit_bytes=32 * 1024 * 1024),
    )(me, arrival_index, fresh, factors, page_table, lengths[:, None], key_pool, value_pool, dense_weight)
    held = gather_by_doubling(sum_by_halving(kept, sent, parts).astype(BF16), devices)
    hidden = pl.pallas_call(
        functools.partial(finish, devices),
        out_shape=jax.ShapeDtypeStruct((rows, width), BF16),
        in_specs=[SMEM, SMEM, VMEM, VMEM, VMEM],
        out_specs=VMEM,
    )(me, request_slot, held, residual, dense_bias[None, :])
    return hidden, appended_keys, appended_values


def solution(mesh):
    rows = P("req", "tp")
    pool = P("req", None, "tp")
    in_specs = (rows,) * 4 + (P("tp", None), P("tp"), pool, pool, P("req", None)) + (P("req"),) * 3
    step = functools.partial(on_device, mesh.shape["req"], mesh.shape["tp"])
    return jax.shard_map(step, mesh=mesh, in_specs=in_specs, out_specs=(rows,) * 3, check_vma=False)
```

time: 251 us -> 52.8 us (0.21)
  waiting for transfers between devices: 106 us -> 16.9 us
  blocking collectives: 60.9 us -> 0 us
  local copies, waits for them, and re-layouts: 47.7 us -> 11.6 us
  matrix products: 15.9 us -> 0 us
  starting transfers between devices: 0.08 us -> 14.2 us
  between operations: 14.8 us -> 0.76 us
  Pallas kernels: 0 us -> 6.11 us
    unnamed x4 -> x0, waiting for transfers between devices: 106 us -> none
    all_gather x3 -> x0, blocking collectives: 60.9 us -> none  [the longest x1 23.7 us: on_device(): lax.all_gather(query_new, 'req', axis=0, tiled=True)]
    reshape x4 -> x0, local copies, waits for them, and re-layouts: 29.3 us -> none  [the longest x1 14.6 us: on_device(): value_pool[page_table].reshape(rows, table_width, page_rows, heads_here, HS)]
    ppermute x0 -> x9, waiting for transfers between devices: none -> 16.9 us  [the longest x8 14.7 us: gather_by_doubling(): held = jnp.concatenate([held, lax.ppermute(held, 'req', pairs)], axis=0)]
    gather x2 -> x0, local copies, waits for them, and re-layouts: 15.6 us -> none  [the longest x1 7.8 us: on_device(): value_pool[page_table].reshape(rows, table_width, page_rows, heads_here, HS)]
    ppermute x0 -> x9, starting transfers between devices: none -> 14.2 us  [the longest x8 12.7 us: gather_by_doubling(): held = jnp.concatenate([held, lax.ppermute(held, 'req', pairs)], axis=0)]
    dot_general x6 -> x0, matrix products: 13.1 us -> none  [the longest x1 5.65 us: on_device(): jnp.einsum('rhd,rpthd->rhpt', rotated_query, key_pages, preferred_element...]
    unnamed x23 -> x22, local copies, waits for them, and re-layouts: 2.56 us -> 9.88 us
  transfers between devices with their start and end apart: 2 -> 9, of which waited for: 2 -> 8; matrix products, arithmetic and copies ran while one was open for 0% -> 7% of each run, Pallas kernels for 0% -> 0%
where the time goes in v1:
time: 52.8 us; the launch traced here: 52.4 us
  waiting for transfers between devices  16.9 us (32%)
  starting transfers between devices  14.2 us (27%)
  local copies, waits for them, and re-layouts  11.6 us (22%)
  Pallas kernels  6.11 us (12%)
  other arithmetic  2.79 us (5%)
  between operations  0.76 us (1%)
    ppermute x8, waiting for transfers between devices, gather_by_doubling(): held = jnp.concatenate([held, lax.ppermute(held, 'req', pairs)], axis=0)  14.7 us
    ppermute x8, starting transfers between devices, gather_by_doubling(): held = jnp.concatenate([held, lax.ppermute(held, 'req', pairs)], axis=0)  12.7 us
    unnamed x22, local copies, waits for them, and re-layouts  9.88 us
    pallas_call x1, Pallas kernels, on_device(): pl.pallas_call(functools.partial(attend, devices, parts), out_shape=(half...  4.51 us
    ppermute x1, waiting for transfers between devices, sum_by_halving(): kept = kept + lax.ppermute(sent, 'tp', [(i, i ^ bit) for i in range(parts)])  2.22 us
    pallas_call x1, Pallas kernels, on_device(): pl.pallas_call(functools.partial(finish, devices), out_shape=jax.ShapeDty...  1.6 us
    ppermute x1, starting transfers between devices, sum_by_halving(): kept = kept + lax.ppermute(sent, 'tp', [(i, i ^ bit) for i in range(parts)])  1.52 us
  transfers between devices with their start and end apart: 9, of which 8 were waited for; matrix products, arithmetic and copies ran while one was open for 7% of the time, Pallas kernels for 0%

profile of v1, /device:TPU:0, one launch (start us, length us, event | category | flops | bytes accessed | tf_op | source)
XLA Modules:
  0.0 52.4 jit_solution(13027493655387425856)
XLA Ops:
  0.6 0.7 %maximum_bitcast_fusion = bf16[1,4,3072]{2,1,0:T(4,128)(2,1)S(1)} fusion(bf16[4,1024]{1,0:T(4,128)(2,1)} %param.14, bf16[4,1024]{1,0:T(4,128)(2,1)} %param.13, bf16[4,1024]{1,0:T(4,128)(2,1)} %param.12), kind=kLoop, calls=%fused_computation.6 | loop fusion | flops 73728 | bytes 49152 | tf_op jit(solution)/shard_map/broadcast_in_dim | solution.py:19
  1.4 4.1 %collective-permute-start = (bf16[1,4,3072]{2,1,0:T(4,128)(2,1)S(1)}, bf16[1,4,3072]{2,1,0:T(4,128)(2,1)S(1)}, u32[]{:S(2)}, u32[]{:S(2)}) collective-permute-start(bf16[1,4,3072]{2,1,0:T(4,128)(2,1)S(1)} %maximum_bitcast_fusion), channel_id=1, source_target_pairs={{0,16},{2,18},{4,20},{6,22},{8,24},{10,26},{12,28},{14,30},{16,0},... | collective-permute-start | bytes 73736 | tf_op jit(solution)/shard_map/ppermute | solution.py:23
  5.5 0.7 %constant_dynamic-update-slice_fusion.4 = bf16[16,4,3072]{2,1,0:T(4,128)(2,1)S(1)} fusion(bf16[4,1024]{1,0:T(4,128)(2,1)} %param.14, bf16[4,1024]{1,0:T(4,128)(2,1)} %param.13, bf16[4,1024]{1,0:T(4,128)(2,1)} %param.12), kind=kLoop, calls=%fused_computation.11 | loop fusion | flops 73727 | bytes 49152
  6.2 0.7 %convert_element_type.7 = f32[4]{0:T(128)S(1)} convert(s32[4]{0:T(128)} %param.21) | non-fusion elementwise | flops 4 | bytes 32 | tf_op jit(solution)/shard_map/convert_element_type | solution.py:59
  6.9 0.1 pad.17.clone
  7.0 0.1 pad.20.clone
  7.1 0.1 multiply_cosine_fusion
  7.2 0.1 maximum_maximum_fusion.1
  7.4 0.1 pad_add_fusion.me_ref
  7.5 0.0 copy-start.4
  7.5 0.7 %copy.15.lengths_ref = s32[4,1]{1,0:T(4,128)S(1)} copy(s32[4,1]{0,1:T(1,128)} %bitcast.7) | data formatting | bytes 32 | tf_op jit(solution)/shard_map/broadcast_in_dim | solution.py:176
  8.2 0.0 collective-permute-done
  8.2 1.6 %collective-permute-start.1 = (bf16[2,4,3072]{2,1,0:T(4,128)(2,1)S(1)}, bf16[2,4,3072]{2,1,0:T(4,128)(2,1)S(1)}, u32[]{:S(2)}, u32[]{:S(2)}) collective-permute-start(bf16[2,4,3072]{2,1,0:T(4,128)(2,1)S(1)} %pad_maximum_fusion.3), channel_id=1, source_target_pairs={{0,8},{2,10},{4,12},{6,14},{8,0},{10,2},{12,4},{14,6},{16,24},{18,... | collective-permute-start | bytes 147464 | tf_op jit(solution)/shard_map/ppermute | solution.py:23
  9.9 2.5 %collective-permute-done.1 = bf16[2,4,3072]{2,1,0:T(4,128)(2,1)S(1)} collective-permute-done((bf16[2,4,3072]{2,1,0:T(4,128)(2,1)S(1)}, bf16[2,4,3072]{2,1,0:T(4,128)(2,1)S(1)}, u32[]{:S(2)}, u32[]{:S(2)}) %collective-permute-start.1) | collective-permute-done | bytes 49184 | tf_op jit(solution)/shard_map/ppermute | solution.py:23
  12.4 0.1 pad_maximum_fusion.1
  12.5 1.6 %collective-permute-start.2 = (bf16[4,4,3072]{2,1,0:T(4,128)(2,1)S(1)}, bf16[4,4,3072]{2,1,0:T(4,128)(2,1)S(1)}, u32[]{:S(2)}, u32[]{:S(2)}) collective-permute-start(bf16[4,4,3072]{2,1,0:T(4,128)(2,1)S(1)} %pad_maximum_fusion.1), channel_id=1, source_target_pairs={{0,4},{2,6},{4,0},{6,2},{8,12},{10,14},{12,8},{14,10},{16,20},{18,... | collective-permute-start | bytes 294920 | tf_op jit(solution)/shard_map/ppermute | solution.py:23
  14.1 3.1 %collective-permute-done.2 = bf16[4,4,3072]{2,1,0:T(4,128)(2,1)S(1)} collective-permute-done((bf16[4,4,3072]{2,1,0:T(4,128)(2,1)S(1)}, bf16[4,4,3072]{2,1,0:T(4,128)(2,1)S(1)}, u32[]{:S(2)}, u32[]{:S(2)}) %collective-permute-start.2) | collective-permute-done | bytes 98336 | tf_op jit(solution)/shard_map/ppermute | solution.py:23
  17.2 0.1 pad_maximum_fusion
  17.3 0.1 collective-permute-start.3
  17.4 1.4 %collective-permute-done.3 = bf16[8,4,3072]{2,1,0:T(4,128)(2,1)S(1)} collective-permute-done((bf16[8,4,3072]{2,1,0:T(4,128)(2,1)S(1)}, bf16[8,4,3072]{2,1,0:T(4,128)(2,1)S(1)}, u32[]{:S(2)}, u32[]{:S(2)}) %collective-permute-start.3) | collective-permute-done | bytes 196640 | tf_op jit(solution)/shard_map/ppermute | solution.py:23
  18.8 0.1 constant_dynamic-update-slice_fusion.fresh_ref
  18.9 0.0 copy-start
  18.9 2.8 %copy-done = bf16[24,128,1024]{2,1,0:T(8,128)(2,1)S(1)} copy-done((bf16[24,128,1024]{2,1,0:T(8,128)(2,1)S(1)}, bf16[24,128,1024]{2,1,0:T(8,128)(2,1)}, u32[]{:S(2)}) %copy-start) | copy-done | bytes 6291480
  21.7 0.0 copy-start.1
  21.7 2.8 %copy-done.1 = bf16[24,128,1024]{2,1,0:T(8,128)(2,1)S(1)} copy-done((bf16[24,128,1024]{2,1,0:T(8,128)(2,1)S(1)}, bf16[24,128,1024]{2,1,0:T(8,128)(2,1)}, u32[]{:S(2)}) %copy-start.1) | copy-done | bytes 6291480
  24.5 0.0 copy-start.2
  24.5 2.2 %copy-done.2 = bf16[1024,2048]{1,0:T(8,128)(2,1)S(1)} copy-done((bf16[1024,2048]{1,0:T(8,128)(2,1)S(1)}, bf16[1024,2048]{1,0:T(8,128)(2,1)}, u32[]{:S(2)}) %copy-start.2) | copy-done | bytes 4194328
  26.7 0.0 copy-start.3
  26.7 0.7 %copy-done.3 = s32[4,8]{1,0:T(4,128)S(1)} copy-done((s32[4,8]{1,0:T(4,128)S(1)}, s32[4,8]{1,0:T(4,128)}, u32[]{:S(2)}) %copy-start.3) | copy-done | bytes 152
  27.4 0.7 %copy-done.5 = s32[4]{0:T(128)S(1)} copy-done((s32[4]{0:T(128)S(1)}, s32[4]{0:T(128)}, u32[]{:S(2)}) %copy-start.5) | copy-done | bytes 40
  28.0 4.5 %shard_map.139 = (f32[1,4,1024]{2,1,0:T(4,128)S(1)}, f32[1,4,1024]{2,1,0:T(4,128)S(1)}, bf16[4,1024]{1,0:T(4,128)(2,1)}, bf16[4,1024]{1,0:T(4,128)(2,1)}) custom-call(s32[2]{0:T(128)S(1)} %pad_add_fusion.me_ref, s32[4]{0:T(128)S(1)} %copy-done.5, bf16[16,4,3072]{2,1,0:T(4,128)(2,1)S(1)} %constant_dynamic-update-slice_fusion.fresh_ref, ...), custom_call_target="tpu_custom_call" | custom-call | tf_op jit(solution)/shard_map/pallas_call | solution.py:164
  32.5 0.0 copy-done.4
  32.5 1.5 %collective-permute-start.4 = (f32[1,4,1024]{2,1,0:T(4,128)S(1)}, f32[1,4,1024]{2,1,0:T(4,128)S(1)}, u32[]{:S(2)}, u32[]{:S(2)}) collective-permute-start(f32[1,4,1024]{2,1,0:T(4,128)S(1)} %get-tuple-element.8), channel_id=1, source_target_pairs={{0,1},{1,0},{2,3},{3,2},{4,5},{5,4},{6,7},{7,6},{8,9},{9,8},{10,11... | collective-permute-start | bytes 49160 | tf_op jit(solution)/shard_map/ppermute | solution.py:42
  34.0 2.2 %collective-permute-done.4 = f32[1,4,1024]{2,1,0:T(4,128)S(1)} collective-permute-done((f32[1,4,1024]{2,1,0:T(4,128)S(1)}, f32[1,4,1024]{2,1,0:T(4,128)S(1)}, u32[]{:S(2)}, u32[]{:S(2)}) %collective-permute-start.4) | collective-permute-done | bytes 16416 | tf_op jit(solution)/shard_map/ppermute | solution.py:42
  36.3 2.1 %collective-permute-start.5 = (bf16[1,4,1024]{2,1,0:T(4,128)(2,1)S(1)}, bf16[1,4,1024]{2,1,0:T(4,128)(2,1)S(1)}, u32[]{:S(2)}, u32[]{:S(2)}) collective-permute-start(bf16[1,4,1024]{2,1,0:T(4,128)(2,1)S(1)} %get-tuple-element.12), channel_id=1, source_target_pairs={{0,16},{2,18},{4,20},{6,22},{8,24},{10,26},{12,28},{14,30},{16,0},... | collective-permute-start | bytes 24584 | tf_op jit(solution)/shard_map/ppermute | solution.py:23
  38.3 0.0 copy-done.7
  38.3 0.6 %broadcast_in_dim.22.bias_ref = bf16[1,1024]{1,0:T(2,128)(2,1)} reshape(bf16[1024]{0:T(1024)(128)(2,1)S(1)} %copy-done.7) | data formatting | bytes 4096 | tf_op jit(solution)/shard_map/broadcast_in_dim | solution.py:183
  38.9 1.9 %collective-permute-done.5 = bf16[1,4,1024]{2,1,0:T(4,128)(2,1)S(1)} collective-permute-done((bf16[1,4,1024]{2,1,0:T(4,128)(2,1)S(1)}, bf16[1,4,1024]{2,1,0:T(4,128)(2,1)S(1)}, u32[]{:S(2)}, u32[]{:S(2)}) %collective-permute-start.5) | collective-permute-done | bytes 8224 | tf_op jit(solution)/shard_map/ppermute | solution.py:23
  40.9 1.6 %collective-permute-start.6 = (bf16[2,4,1024]{2,1,0:T(4,128)(2,1)S(1)}, bf16[2,4,1024]{2,1,0:T(4,128)(2,1)S(1)}, u32[]{:S(2)}, u32[]{:S(2)}) collective-permute-start(bf16[2,4,1024]{2,1,0:T(4,128)(2,1)S(1)} %pad_maximum_fusion.6), channel_id=1, source_target_pairs={{0,8},{2,10},{4,12},{6,14},{8,0},{10,2},{12,4},{14,6},{16,24},{18,... | collective-permute-start | bytes 49160 | tf_op jit(solution)/shard_map/ppermute | solution.py:23
  42.6 2.1 %collective-permute-done.6 = bf16[2,4,1024]{2,1,0:T(4,128)(2,1)S(1)} collective-permute-done((bf16[2,4,1024]{2,1,0:T(4,128)(2,1)S(1)}, bf16[2,4,1024]{2,1,0:T(4,128)(2,1)S(1)}, u32[]{:S(2)}, u32[]{:S(2)}) %collective-permute-start.6) | collective-permute-done | bytes 16416 | tf_op jit(solution)/shard_map/ppermute | solution.py:23
  44.7 1.6 %collective-permute-start.7 = (bf16[4,4,1024]{2,1,0:T(4,128)(2,1)S(1)}, bf16[4,4,1024]{2,1,0:T(4,128)(2,1)S(1)}, u32[]{:S(2)}, u32[]{:S(2)}) collective-permute-start(bf16[4,4,1024]{2,1,0:T(4,128)(2,1)S(1)} %pad_maximum_fusion.5), channel_id=1, source_target_pairs={{0,4},{2,6},{4,0},{6,2},{8,12},{10,14},{12,8},{14,10},{16,20},{18,... | collective-permute-start | bytes 98312 | tf_op jit(solution)/shard_map/ppermute | solution.py:23
  46.3 2.4 %collective-permute-done.7 = bf16[4,4,1024]{2,1,0:T(4,128)(2,1)S(1)} collective-permute-done((bf16[4,4,1024]{2,1,0:T(4,128)(2,1)S(1)}, bf16[4,4,1024]{2,1,0:T(4,128)(2,1)S(1)}, u32[]{:S(2)}, u32[]{:S(2)}) %collective-permute-start.7) | collective-permute-done | bytes 32800 | tf_op jit(solution)/shard_map/ppermute | solution.py:23
  48.7 0.1 pad_maximum_fusion.2
  48.8 0.1 collective-permute-start.8
  48.9 1.2 %collective-permute-done.8 = bf16[8,4,1024]{2,1,0:T(4,128)(2,1)S(1)} collective-permute-done((bf16[8,4,1024]{2,1,0:T(4,128)(2,1)S(1)}, bf16[8,4,1024]{2,1,0:T(4,128)(2,1)S(1)}, u32[]{:S(2)}, u32[]{:S(2)}) %collective-permute-start.8) | collective-permute-done | bytes 65568 | tf_op jit(solution)/shard_map/ppermute | solution.py:23
  50.1 0.0 copy-start.6
  50.1 0.6 %copy-done.6 = bf16[16,4,1024]{2,1,0:T(4,128)(2,1)} copy-done((bf16[16,4,1024]{2,1,0:T(4,128)(2,1)}, bf16[16,4,1024]{2,1,0:T(4,128)(2,1)S(1)}, u32[]{:S(2)}) %copy-start.6) | copy-done | bytes 131096
  50.8 1.6 %shard_map.140 = bf16[4,1024]{1,0:T(4,128)(2,1)} custom-call(s32[2]{0:T(128)} %copy-done.4, s32[4]{0:T(128)} %slot_ref.1, bf16[16,4,1024]{2,1,0:T(4,128)(2,1)} %copy-done.6, bf16[4,1024]{1,0:T(4,128)(2,1)} %residual_ref.1, bf16[1,1024]{1,0:T(2,128)(2,1)} %broadcast_in_dim.22.bias_ref), custom_call_target="tpu_custom_call" | custom-call | tf_op jit(solution)/shard_map/pallas_call | solution.py:178
  (24 shorter events, 0.4 us)
Async XLA Ops:
  1.4 6.8 %collective-permute-start = (bf16[1,4,3072]{2,1,0:T(4,128)(2,1)S(1)}, bf16[1,4,3072]{2,1,0:T(4,128)(2,1)S(1)}, u32[]{:S(2)}, u32[]{:S(2)}) collective-permute-start(bf16[1,4,3072]{2,1,0:T(4,128)(2,1)S(1)} %maximum_bitcast_fusion), channel_id=1, source_target_pairs={{0,16},{2,18},{4,20},{6,22},{8,24},{10,26},{12,28},{14,30},{16,0},... | collective-permute-start | bytes 73736 | tf_op jit(solution)/shard_map/ppermute | solution.py:23
  7.5 25.1 %copy-start.4 = (s32[2]{0:T(128)}, s32[2]{0:T(128)S(1)}, u32[]{:S(2)}) copy-start(s32[2]{0:T(128)S(1)} %pad_add_fusion.me_ref) | copy-start | bytes 28
  8.2 4.2 %collective-permute-start.1 = (bf16[2,4,3072]{2,1,0:T(4,128)(2,1)S(1)}, bf16[2,4,3072]{2,1,0:T(4,128)(2,1)S(1)}, u32[]{:S(2)}, u32[]{:S(2)}) collective-permute-start(bf16[2,4,3072]{2,1,0:T(4,128)(2,1)S(1)} %pad_maximum_fusion.3), channel_id=1, source_target_pairs={{0,8},{2,10},{4,12},{6,14},{8,0},{10,2},{12,4},{14,6},{16,24},{18,... | collective-permute-start | bytes 147464 | tf_op jit(solution)/shard_map/ppermute | solution.py:23
  12.5 4.7 %collective-permute-start.2 = (bf16[4,4,3072]{2,1,0:T(4,128)(2,1)S(1)}, bf16[4,4,3072]{2,1,0:T(4,128)(2,1)S(1)}, u32[]{:S(2)}, u32[]{:S(2)}) collective-permute-start(bf16[4,4,3072]{2,1,0:T(4,128)(2,1)S(1)} %pad_maximum_fusion.1), channel_id=1, source_target_pairs={{0,4},{2,6},{4,0},{6,2},{8,12},{10,14},{12,8},{14,10},{16,20},{18,... | collective-permute-start | bytes 294920 | tf_op jit(solution)/shard_map/ppermute | solution.py:23
  17.3 1.5 %collective-permute-start.3 = (bf16[8,4,3072]{2,1,0:T(4,128)(2,1)S(1)}, bf16[8,4,3072]{2,1,0:T(4,128)(2,1)S(1)}, u32[]{:S(2)}, u32[]{:S(2)}) collective-permute-start(bf16[8,4,3072]{2,1,0:T(4,128)(2,1)S(1)} %pad_maximum_fusion), channel_id=1, source_target_pairs={{0,2},{2,0},{4,6},{6,4},{8,10},{10,8},{12,14},{14,12},{16,18},{18,... | collective-permute-start | bytes 589832 | tf_op jit(solution)/shard_map/ppermute | solution.py:23
  18.9 2.8 %copy-start = (bf16[24,128,1024]{2,1,0:T(8,128)(2,1)S(1)}, bf16[24,128,1024]{2,1,0:T(8,128)(2,1)}, u32[]{:S(2)}) copy-start(bf16[24,128,1024]{2,1,0:T(8,128)(2,1)} %keys_ref.1) | copy-start | bytes 18874372
  21.7 2.8 %copy-start.1 = (bf16[24,128,1024]{2,1,0:T(8,128)(2,1)S(1)}, bf16[24,128,1024]{2,1,0:T(8,128)(2,1)}, u32[]{:S(2)}) copy-start(bf16[24,128,1024]{2,1,0:T(8,128)(2,1)} %values_ref.1) | copy-start | bytes 18874372
  24.5 2.2 %copy-start.2 = (bf16[1024,2048]{1,0:T(8,128)(2,1)S(1)}, bf16[1024,2048]{1,0:T(8,128)(2,1)}, u32[]{:S(2)}) copy-start(bf16[1024,2048]{1,0:T(8,128)(2,1)} %weight_ref.1) | copy-start | bytes 12582916
  26.7 0.7 %copy-start.3 = (s32[4,8]{1,0:T(4,128)S(1)}, s32[4,8]{1,0:T(4,128)}, u32[]{:S(2)}) copy-start(s32[4,8]{1,0:T(4,128)} %table_ref.1) | copy-start | bytes 388
  27.3 0.7 %copy-start.5 = (s32[4]{0:T(128)S(1)}, s32[4]{0:T(128)}, u32[]{:S(2)}) copy-start(s32[4]{0:T(128)} %arrival_ref.1) | copy-start | bytes 52
  28.0 10.3 %copy-start.7 = (bf16[1024]{0:T(1024)(128)(2,1)S(1)}, bf16[1024]{0:T(1024)(128)(2,1)}, u32[]{:S(2)}) copy-start(bf16[1024]{0:T(1024)(128)(2,1)} %param.17) | copy-start | bytes 6148
  32.5 3.7 %collective-permute-start.4 = (f32[1,4,1024]{2,1,0:T(4,128)S(1)}, f32[1,4,1024]{2,1,0:T(4,128)S(1)}, u32[]{:S(2)}, u32[]{:S(2)}) collective-permute-start(f32[1,4,1024]{2,1,0:T(4,128)S(1)} %get-tuple-element.8), channel_id=1, source_target_pairs={{0,1},{1,0},{2,3},{3,2},{4,5},{5,4},{6,7},{7,6},{8,9},{9,8},{10,11... | collective-permute-start | bytes 49160 | tf_op jit(solution)/shard_map/ppermute | solution.py:42
  36.3 4.6 %collective-permute-start.5 = (bf16[1,4,1024]{2,1,0:T(4,128)(2,1)S(1)}, bf16[1,4,1024]{2,1,0:T(4,128)(2,1)S(1)}, u32[]{:S(2)}, u32[]{:S(2)}) collective-permute-start(bf16[1,4,1024]{2,1,0:T(4,128)(2,1)S(1)} %get-tuple-element.12), channel_id=1, source_target_pairs={{0,16},{2,18},{4,20},{6,22},{8,24},{10,26},{12,28},{14,30},{16,0},... | collective-permute-start | bytes 24584 | tf_op jit(solution)/shard_map/ppermute | solution.py:23
  40.9 3.8 %collective-permute-start.6 = (bf16[2,4,1024]{2,1,0:T(4,128)(2,1)S(1)}, bf16[2,4,1024]{2,1,0:T(4,128)(2,1)S(1)}, u32[]{:S(2)}, u32[]{:S(2)}) collective-permute-start(bf16[2,4,1024]{2,1,0:T(4,128)(2,1)S(1)} %pad_maximum_fusion.6), channel_id=1, source_target_pairs={{0,8},{2,10},{4,12},{6,14},{8,0},{10,2},{12,4},{14,6},{16,24},{18,... | collective-permute-start | bytes 49160 | tf_op jit(solution)/shard_map/ppermute | solution.py:23
  44.7 4.0 %collective-permute-start.7 = (bf16[4,4,1024]{2,1,0:T(4,128)(2,1)S(1)}, bf16[4,4,1024]{2,1,0:T(4,128)(2,1)S(1)}, u32[]{:S(2)}, u32[]{:S(2)}) collective-permute-start(bf16[4,4,1024]{2,1,0:T(4,128)(2,1)S(1)} %pad_maximum_fusion.5), channel_id=1, source_target_pairs={{0,4},{2,6},{4,0},{6,2},{8,12},{10,14},{12,8},{14,10},{16,20},{18,... | collective-permute-start | bytes 98312 | tf_op jit(solution)/shard_map/ppermute | solution.py:23
  48.8 1.3 %collective-permute-start.8 = (bf16[8,4,1024]{2,1,0:T(4,128)(2,1)S(1)}, bf16[8,4,1024]{2,1,0:T(4,128)(2,1)S(1)}, u32[]{:S(2)}, u32[]{:S(2)}) collective-permute-start(bf16[8,4,1024]{2,1,0:T(4,128)(2,1)S(1)} %pad_maximum_fusion.2), channel_id=1, source_target_pairs={{0,2},{2,0},{4,6},{6,4},{8,10},{10,8},{12,14},{14,12},{16,18},{18,... | collective-permute-start | bytes 196616 | tf_op jit(solution)/shard_map/ppermute | solution.py:23
  50.1 0.6 %copy-start.6 = (bf16[16,4,1024]{2,1,0:T(4,128)(2,1)}, bf16[16,4,1024]{2,1,0:T(4,128)(2,1)S(1)}, u32[]{:S(2)}) copy-start(bf16[16,4,1024]{2,1,0:T(4,128)(2,1)S(1)} %constant_dynamic-update-slice_fusion.5.held_ref) | copy-start | bytes 393220

commit v2 on v1

v2 whole, which is shorter than its diff:
```python
import functools

import jax
import jax.numpy as jnp
from jax import lax
from jax.experimental import pallas as pl
from jax.experimental.pallas import tpu as pltpu
from jax.sharding import PartitionSpec as P

HS = 256
BF16 = jnp.bfloat16
F32 = jnp.float32
ANY = pl.BlockSpec(memory_space=pl.ANY)
VMEM = pl.BlockSpec(memory_space=pltpu.VMEM)


def joined(own_ref, other_ref, out_ref):
    count = own_ref.shape[0]
    out_ref[:count] = own_ref[...]
    out_ref[count:] = other_ref[...]


def join(own, other, work):
    return pl.pallas_call(
        joined,
        out_shape=jax.ShapeDtypeStruct((2 * own.shape[0],) + own.shape[1:], own.dtype),
        in_specs=[VMEM, VMEM],
        out_specs=VMEM,
        cost_estimate=pl.CostEstimate(flops=work, bytes_accessed=work >> 14, transcendentals=0),
        compiler_params=pltpu.CompilerParams(vmem_limit_bytes=1 << 20),
    )(own, other)


def gather_by_doubling(block, devices, works):
    held = block[None]
    bit = devices // 2
    while True:
        other = lax.ppermute(held, "req", [(i, i ^ bit) for i in range(devices)])
        if bit == 1:
            return held, other
        held = join(held, other, works.pop(0) if works else 0)
        bit //= 2


def places(rows, per, devices):
    apart = (rows // per) ^ lax.axis_index("req").astype(jnp.int32)
    place = jnp.zeros_like(rows)
    bit, weight = devices // 2, 1
    while bit:
        place = place + jnp.where((apart & bit) != 0, weight, 0)
        bit //= 2
        weight *= 2
    return jnp.stack([place, rows % per, jnp.full_like(rows, lax.axis_index("tp"))])


def take_rows(places_ref, near_ref, far_ref):
    count, per, width = near_ref.shape
    rows = lax.broadcasted_iota(jnp.int32, (per, width), 0)
    taken = []
    table = places_ref[...]
    for i in range(table.shape[1]):
        place, row = table[0, i], table[1, i]
        near = near_ref[jnp.minimum(place, count - 1)].astype(F32)
        far = far_ref[jnp.maximum(place - count, 0)].astype(F32)
        block = jnp.where(place < count, near, far)
        taken.append(jnp.sum(jnp.where(rows == row, block, 0.0), axis=0, keepdims=True))
    return jnp.concatenate(taken, axis=0)


def sum_by_halving(kept, sent, parts):
    bit = parts // 2
    while True:
        kept = kept + lax.ppermute(sent, "tp", [(i, i ^ bit) for i in range(parts)])
        if bit == 1:
            return kept[0]
        bit //= 2
        kept, sent = kept[:bit], kept[bit:]


def rotary_factors(lengths, heads):
    rotary_dims = HS // 4
    half = rotary_dims // 2
    rates = 10000.0 ** (-2.0 * jnp.arange(half, dtype=F32) / rotary_dims)
    angle = lengths.astype(F32)[:, None] * rates[None, :]
    cosine, sine = jnp.cos(angle), jnp.sin(angle)
    rows = lengths.shape[0]
    none = jnp.zeros((rows, half), F32)
    rest = jnp.zeros((rows, HS - rotary_dims), F32)
    same = jnp.concatenate([cosine, cosine, rest + 1.0], axis=1)
    right = jnp.concatenate([-sine, none, rest], axis=1)
    left = jnp.concatenate([none, sine, rest], axis=1)
    return jnp.stack([jnp.tile(f, (1, heads)) for f in (same, right, left)])


def attend(parts, places_ref, near_ref, far_ref, factors_ref, table_ref, lengths_ref,
           keys_ref, values_ref, weight_ref, kept_out, sent_out, keys_out, values_out,
           key_ref, value_ref, sems):
    half = places_ref[...][2, 0]
    slots, width = key_ref.shape
    heads = width // HS
    pages, page = keys_ref.shape[0], keys_ref.shape[1]
    tokens = pages * page
    scale = HS ** (-0.5)

    taken = take_rows(places_ref, near_ref, far_ref)
    query, key, value = (taken[:, i * width:(i + 1) * width] for i in range(3))

    def rotate(x):
        right = pltpu.roll(x, width - HS // 8, 1)
        left = pltpu.roll(x, HS // 8, 1)
        return x * factors_ref[0] + right * factors_ref[1] + left * factors_ref[2]

    query = rotate(query).astype(BF16).astype(F32)
    key = rotate(key).astype(BF16)
    key_ref[...] = key
    value_ref[...] = value.astype(BF16)
    copies = [
        pltpu.make_async_copy(key_ref, keys_out, sems.at[0]),
        pltpu.make_async_copy(value_ref, values_out, sems.at[1]),
    ]
    for copy in copies:
        copy.start()

    rows = heads * slots
    row_head = lax.broadcasted_iota(jnp.int32, (rows, width), 0) // slots
    lane_head = lax.broadcasted_iota(jnp.int32, (rows, width), 1) // HS
    mine = row_head == lane_head
    spread_query = jnp.where(mine, jnp.concatenate([query] * heads, axis=0), 0.0)
    own_score = jnp.sum(
        spread_query * jnp.concatenate([key.astype(F32)] * heads, axis=0), axis=1, keepdims=True
    ) * scale

    lane = lax.broadcasted_iota(jnp.int32, (slots, 128), 1)
    visible = jnp.zeros((slots, 128), jnp.int32)
    for i in range(table_ref.shape[1]):
        left_over = jnp.clip(lengths_ref[...] - i * page, 0, page)
        visible = jnp.where((lane == table_ref[:, i:i + 1]) & (left_over > 0), left_over, visible)
    visible = jnp.concatenate([visible] * heads, axis=0)

    scores = lax.dot_general(
        spread_query.astype(BF16), keys_ref[...].reshape(tokens, width),
        (((1,), (1,)), ((), ())), preferred_element_type=F32,
    ) * scale
    place = lax.broadcasted_iota(jnp.int32, (rows, page), 1)
    masked = jnp.concatenate(
        [
            jnp.where(place < visible[:, p:p + 1], scores[:, p * page:(p + 1) * page], -jnp.inf)
            for p in range(pages)
        ],
        axis=1,
    )
    top = jnp.maximum(jnp.max(masked, axis=1, keepdims=True), own_score)
    exps = jnp.exp(masked - top)
    own_exp = jnp.exp(own_score - top)
    total = jnp.sum(exps, axis=1, keepdims=True) + own_exp
    share = 1.0 / total
    weights = (exps * share).astype(BF16)
    own_weight = (own_exp * share).astype(BF16).astype(F32)
    attended = jnp.dot(weights, values_ref[...].reshape(tokens, width), preferred_element_type=F32)
    attended = attended + own_weight * jnp.concatenate([value] * heads, axis=0)
    attended = jnp.where(mine, attended, 0.0)
    attended = sum(attended[h * slots:(h + 1) * slots] for h in range(heads)).astype(BF16)

    for i in range(parts):
        columns = pl.ds(pl.multiple_of((half ^ i) * width, width), width)
        out = kept_out if i < parts // 2 else sent_out
        out[i % (parts // 2)] = jnp.dot(attended, weight_ref[:, columns], preferred_element_type=F32)
    for copy in copies:
        copy.wait()


def finish(places_ref, near_ref, far_ref, residual_ref, bias_ref, out_ref):
    taken = take_rows(places_ref, near_ref, far_ref)
    out_ref[...] = (residual_ref[...].astype(F32) + bias_ref[...].astype(F32) + taken).astype(BF16)


def on_device(devices, parts, query_new, key_new, value_new, residual, dense_weight, dense_bias,
              key_pool, value_pool, page_table, lengths, request_slot, arrival_index):
    rows, width = query_new.shape
    heads = width // HS
    fresh = jnp.concatenate([query_new, key_new, value_new], axis=1)
    near, far = gather_by_doubling(fresh, devices, [0, 1 << 31, 1 << 31])
    half_terms = jax.ShapeDtypeStruct((parts // 2, rows, width), F32)
    narrow = jax.ShapeDtypeStruct((rows, width), BF16)
    kept, sent, appended_keys, appended_values = pl.pallas_call(
        functools.partial(attend, parts),
        out_shape=(half_terms, half_terms, narrow, narrow),
        in_specs=[VMEM] * 9,
        out_specs=(VMEM, VMEM, ANY, ANY),
        scratch_shapes=[
            pltpu.VMEM((rows, width), BF16),
            pltpu.VMEM((rows, width), BF16),
            pltpu.SemaphoreType.DMA((2,)),
        ],
        compiler_params=pltpu.CompilerParams(vmem_limit_bytes=8 << 20),
    )(places(arrival_index, rows, devices), near, far, rotary_factors(lengths, heads), page_table,
      lengths[:, None], key_pool, value_pool, dense_weight)
    near, far = gather_by_doubling(sum_by_halving(kept, sent, parts).astype(BF16), devices, [])
    hidden = pl.pallas_call(
        finish,
        out_shape=narrow,
        in_specs=[VMEM] * 5,
        out_specs=VMEM,
        compiler_params=pltpu.CompilerParams(vmem_limit_bytes=2 << 20),
    )(places(request_slot, rows, devices), near, far, residual, dense_bias[None, :])
    return hidden, appended_keys, appended_values


def solution(mesh):
    rows = P("req", "tp")
    pool = P("req", None, "tp")
    in_specs = (rows,) * 4 + (P("tp", None), P("tp"), pool, pool, P("req", None)) + (P("req"),) * 3
    step = functools.partial(on_device, mesh.shape["req"], mesh.shape["tp"])
    return jax.shard_map(step, mesh=mesh, in_specs=in_specs, out_specs=(rows,) * 3, check_vma=False)
```

time: 52.8 us -> 42.3 us (0.80)
  local copies, waits for them, and re-layouts: 11.6 us -> 3.27 us
  waiting for transfers between devices: 16.9 us -> 13.8 us
  starting transfers between devices: 14.2 us -> 17 us
  Pallas kernels: 6.11 us -> 4.82 us
    unnamed x22 -> x14, local copies, waits for them, and re-layouts: 9.88 us -> 2.21 us
    ppermute x8, waiting for transfers between devices: 14.7 us -> 12 us  [gather_by_doubling(): other = lax.ppermute(held, 'req', [(i, i ^ bit) for i in range(devices)])]
    ppermute x8, starting transfers between devices: 12.7 us -> 14.9 us  [gather_by_doubling(): other = lax.ppermute(held, 'req', [(i, i ^ bit) for i in range(devices)])]
    pallas_call x2 -> x8, Pallas kernels: 6.11 us -> 4.82 us  [the longest x1 4.04 us: on_device(): pl.pallas_call(functools.partial(attend, parts), out_shape=(half_terms, h...]
    unnamed x2 -> x1, other arithmetic: 0.75 us -> 0.01 us
    another operation x1 -> x2, other arithmetic: 0.08 us -> 0.76 us  [places(): jnp.stack([place, rows % per, jnp.full_like(rows, lax.axis_index('tp'))])]
    broadcast_in_dim x1, local copies, waits for them, and re-layouts: 0.59 us -> 0.01 us  [on_device(): dense_bias[None, :]]
  transfers between devices with their start and end apart: 9 -> 9, of which waited for: 8 -> 9; matrix products, arithmetic and copies ran while one was open for 7% -> 6% of each run, Pallas kernels for 0% -> 0%
where the time goes in v2:
time: 42.3 us; the launch traced here: 42 us
  starting transfers between devices  17 us (40%)
  waiting for transfers between devices  13.8 us (33%)
  Pallas kernels  4.82 us (11%)
  local copies, waits for them, and re-layouts  3.27 us (8%)
  other arithmetic  2.39 us (6%)
  between operations  0.77 us (2%)
    ppermute x8, starting transfers between devices, gather_by_doubling(): other = lax.ppermute(held, 'req', [(i, i ^ bit) for i in range(devices)])  14.9 us
    ppermute x8, waiting for transfers between devices, gather_by_doubling(): other = lax.ppermute(held, 'req', [(i, i ^ bit) for i in range(devices)])  12 us
    pallas_call x1, Pallas kernels, on_device(): pl.pallas_call(functools.partial(attend, parts), out_shape=(half_terms, h...  4.04 us
    unnamed x14, local copies, waits for them, and re-layouts  2.21 us
    ppermute x1, starting transfers between devices, sum_by_halving(): kept = kept + lax.ppermute(sent, 'tp', [(i, i ^ bit) for i in range(parts)])  2.04 us
    ppermute x1, waiting for transfers between devices, sum_by_halving(): kept = kept + lax.ppermute(sent, 'tp', [(i, i ^ bit) for i in range(parts)])  1.76 us
  transfers between devices with their start and end apart: 9, of which 9 were waited for; matrix products, arithmetic and copies ran while one was open for 6% of the time, Pallas kernels for 0%

profile of v2, /device:TPU:0, one launch (start us, length us, event | category | flops | bytes accessed | tf_op | source)
XLA Modules:
  0.0 42.0 jit_solution(14736498924244411610)
XLA Ops:
  0.6 0.7 %maximum_bitcast_fusion.own_ref = bf16[1,4,3072]{2,1,0:T(4,128)(2,1)S(1)} fusion(bf16[4,1024]{1,0:T(4,128)(2,1)} %param.14, bf16[4,1024]{1,0:T(4,128)(2,1)} %param.13, bf16[4,1024]{1,0:T(4,128)(2,1)} %param.12), kind=kLoop, calls=%fused_computation.1 | loop fusion | flops 73728 | bytes 49152 | tf_op jit(solution)/shard_map/broadcast_in_dim | solution.py:35
  1.4 4.1 %collective-permute-start = (bf16[1,4,3072]{2,1,0:T(4,128)(2,1)S(1)}, bf16[1,4,3072]{2,1,0:T(4,128)(2,1)S(1)}, u32[]{:S(2)}, u32[]{:S(2)}) collective-permute-start(bf16[1,4,3072]{2,1,0:T(4,128)(2,1)S(1)} %maximum_bitcast_fusion.own_ref), channel_id=1, source_target_pairs={{0,16},{2,18},{4,20},{6,22},{8,24},{10,26},{12,28},{14,30},{16,0},... | collective-permute-start | bytes 73736 | tf_op jit(solution)/shard_map/ppermute | solution.py:38
  5.5 0.7 %convert_element_type.7 = f32[4]{0:T(128)S(1)} convert(s32[4]{0:T(128)} %param.21) | non-fusion elementwise | flops 4 | bytes 32 | tf_op jit(solution)/shard_map/convert_element_type | solution.py:84
  6.2 0.1 pad.8.clone
  6.2 0.1 pad.11.clone
  6.3 0.1 multiply_cosine_fusion
  6.4 0.1 maximum_maximum_fusion.1
  6.5 0.8 %collective-permute-done.other_ref = bf16[1,4,3072]{2,1,0:T(4,128)(2,1)S(1)} collective-permute-done((bf16[1,4,3072]{2,1,0:T(4,128)(2,1)S(1)}, bf16[1,4,3072]{2,1,0:T(4,128)(2,1)S(1)}, u32[]{:S(2)}, u32[]{:S(2)}) %collective-permute-start) | collective-permute-done | bytes 24608 | tf_op jit(solution)/shard_map/ppermute | solution.py:38
  7.3 1.9 %collective-permute-start.1 = (bf16[2,4,3072]{2,1,0:T(4,128)(2,1)S(1)}, bf16[2,4,3072]{2,1,0:T(4,128)(2,1)S(1)}, u32[]{:S(2)}, u32[]{:S(2)}) collective-permute-start(bf16[2,4,3072]{2,1,0:T(4,128)(2,1)S(1)} %shard_map.139.own_ref), channel_id=1, source_target_pairs={{0,8},{2,10},{4,12},{6,14},{8,0},{10,2},{12,4},{14,6},{16,24},{18,... | collective-permute-start | bytes 147464 | tf_op jit(solution)/shard_map/ppermute | solution.py:38
  9.2 0.7 %fusion.8 = (s32[1,4]{1,0:T(1,128)S(1)}, s32[1,4]{1,0:T(1,128)S(1)}, s32[1,4]{1,0:T(1,128)S(1)}, s32[1,4]{1,0:T(1,128)S(1)}) fusion(s32[4]{0:T(128)} %param.23, s32[]{:T(128)S(6)} %axis_index.15, s32[4]{0:T(128)} %param.22), kind=kLoop, calls=%fused_computation.37 | loop fusion | flops 280 | bytes 100 | tf_op jit(solution)/shard_map/stack | solution.py:53
  10.0 0.7 %copy.15.lengths_ref = s32[4,1]{1,0:T(4,128)S(1)} copy(s32[4,1]{0,1:T(1,128)} %bitcast.14) | data formatting | bytes 32 | tf_op jit(solution)/shard_map/broadcast_in_dim | solution.py:197
  10.7 0.1 pad.20.clone
  10.8 0.0 slice-start
  10.8 0.0 copy-start
  10.8 0.0 copy-start.3
  10.8 0.6 %collective-permute-done.1.other_ref = bf16[2,4,3072]{2,1,0:T(4,128)(2,1)S(1)} collective-permute-done((bf16[2,4,3072]{2,1,0:T(4,128)(2,1)S(1)}, bf16[2,4,3072]{2,1,0:T(4,128)(2,1)S(1)}, u32[]{:S(2)}, u32[]{:S(2)}) %collective-permute-start.1) | collective-permute-done | bytes 49184 | tf_op jit(solution)/shard_map/ppermute | solution.py:38
  11.4 0.0 slice-start.1
  11.4 2.0 %collective-permute-start.2 = (bf16[4,4,3072]{2,1,0:T(4,128)(2,1)S(1)}, bf16[4,4,3072]{2,1,0:T(4,128)(2,1)S(1)}, u32[]{:S(2)}, u32[]{:S(2)}) collective-permute-start(bf16[4,4,3072]{2,1,0:T(4,128)(2,1)S(1)} %shard_map.140.own_ref), channel_id=1, source_target_pairs={{0,4},{2,6},{4,0},{6,2},{8,12},{10,14},{12,8},{14,10},{16,20},{18,... | collective-permute-start | bytes 294920 | tf_op jit(solution)/shard_map/ppermute | solution.py:38
  13.4 2.6 %collective-permute-done.2.other_ref = bf16[4,4,3072]{2,1,0:T(4,128)(2,1)S(1)} collective-permute-done((bf16[4,4,3072]{2,1,0:T(4,128)(2,1)S(1)}, bf16[4,4,3072]{2,1,0:T(4,128)(2,1)S(1)}, u32[]{:S(2)}, u32[]{:S(2)}) %collective-permute-start.2) | collective-permute-done | bytes 98336 | tf_op jit(solution)/shard_map/ppermute | solution.py:38
  16.1 0.1 collective-permute-start.3
  16.2 0.1 add_add_fusion.1
  16.3 1.4 %collective-permute-done.3.far_ref = bf16[8,4,3072]{2,1,0:T(4,128)(2,1)S(1)} collective-permute-done((bf16[8,4,3072]{2,1,0:T(4,128)(2,1)S(1)}, bf16[8,4,3072]{2,1,0:T(4,128)(2,1)S(1)}, u32[]{:S(2)}, u32[]{:S(2)}) %collective-permute-start.3) | collective-permute-done | bytes 196640 | tf_op jit(solution)/shard_map/ppermute | solution.py:38
  17.6 0.0 slice-done
  17.6 0.0 copy-done
  17.6 0.0 copy-done.3
  17.6 0.0 slice-done.1
  17.6 0.0 copy-start.1
  17.7 2.2 %copy-done.1 = bf16[1024,2048]{1,0:T(8,128)(2,1)S(1)} copy-done((bf16[1024,2048]{1,0:T(8,128)(2,1)S(1)}, bf16[1024,2048]{1,0:T(8,128)(2,1)}, u32[]{:S(2)}) %copy-start.1) | copy-done | bytes 4194328
  19.8 0.0 copy-start.4
  19.8 0.0 copy-start.2
  19.8 4.0 %shard_map.142 = (f32[1,4,1024]{2,1,0:T(4,128)S(1)}, f32[1,4,1024]{2,1,0:T(4,128)S(1)}, bf16[4,1024]{1,0:T(4,128)(2,1)}, bf16[4,1024]{1,0:T(4,128)(2,1)}) custom-call(s32[3,4]{1,0:T(4,128)S(1)} %get-tuple-element.16.places_ref, bf16[8,4,3072]{2,1,0:T(4,128)(2,1)S(1)} %shard_map.141.near_ref, bf16[8,4,3072]{2,1,0:T(4,128)(2,1)S(1)} %collective-permute-done.3.far_ref, ...), custom_call_target="tpu_custom_call" | custom-call | tf_op jit(solution)/shard_map/pallas_call | solution.py:185
  23.9 2.0 %collective-permute-start.4 = (f32[1,4,1024]{2,1,0:T(4,128)S(1)}, f32[1,4,1024]{2,1,0:T(4,128)S(1)}, u32[]{:S(2)}, u32[]{:S(2)}) collective-permute-start(f32[1,4,1024]{2,1,0:T(4,128)S(1)} %get-tuple-element.8), channel_id=1, source_target_pairs={{0,1},{1,0},{2,3},{3,2},{4,5},{5,4},{6,7},{7,6},{8,9},{9,8},{10,11... | collective-permute-start | bytes 49160 | tf_op jit(solution)/shard_map/ppermute | solution.py:73
  25.9 1.8 %collective-permute-done.4 = f32[1,4,1024]{2,1,0:T(4,128)S(1)} collective-permute-done((f32[1,4,1024]{2,1,0:T(4,128)S(1)}, f32[1,4,1024]{2,1,0:T(4,128)S(1)}, u32[]{:S(2)}, u32[]{:S(2)}) %collective-permute-start.4) | collective-permute-done | bytes 16416 | tf_op jit(solution)/shard_map/ppermute | solution.py:73
  27.7 3.0 %collective-permute-start.5 = (bf16[1,4,1024]{2,1,0:T(4,128)(2,1)S(1)}, bf16[1,4,1024]{2,1,0:T(4,128)(2,1)S(1)}, u32[]{:S(2)}, u32[]{:S(2)}) collective-permute-start(bf16[1,4,1024]{2,1,0:T(4,128)(2,1)S(1)} %add_convert_fusion.own_ref), channel_id=1, source_target_pairs={{0,16},{2,18},{4,20},{6,22},{8,24},{10,26},{12,28},{14,30},{16,0},... | collective-permute-start | bytes 24584 | tf_op jit(solution)/shard_map/ppermute | solution.py:38
  30.7 1.6 %collective-permute-done.5.other_ref = bf16[1,4,1024]{2,1,0:T(4,128)(2,1)S(1)} collective-permute-done((bf16[1,4,1024]{2,1,0:T(4,128)(2,1)S(1)}, bf16[1,4,1024]{2,1,0:T(4,128)(2,1)S(1)}, u32[]{:S(2)}, u32[]{:S(2)}) %collective-permute-start.5) | collective-permute-done | bytes 8224 | tf_op jit(solution)/shard_map/ppermute | solution.py:38
  32.3 1.9 %collective-permute-start.6 = (bf16[2,4,1024]{2,1,0:T(4,128)(2,1)S(1)}, bf16[2,4,1024]{2,1,0:T(4,128)(2,1)S(1)}, u32[]{:S(2)}, u32[]{:S(2)}) collective-permute-start(bf16[2,4,1024]{2,1,0:T(4,128)(2,1)S(1)} %shard_map.143.own_ref), channel_id=1, source_target_pairs={{0,8},{2,10},{4,12},{6,14},{8,0},{10,2},{12,4},{14,6},{16,24},{18,... | collective-permute-start | bytes 49160 | tf_op jit(solution)/shard_map/ppermute | solution.py:38
  34.2 1.8 %collective-permute-done.6.other_ref = bf16[2,4,1024]{2,1,0:T(4,128)(2,1)S(1)} collective-permute-done((bf16[2,4,1024]{2,1,0:T(4,128)(2,1)S(1)}, bf16[2,4,1024]{2,1,0:T(4,128)(2,1)S(1)}, u32[]{:S(2)}, u32[]{:S(2)}) %collective-permute-start.6) | collective-permute-done | bytes 16416 | tf_op jit(solution)/shard_map/ppermute | solution.py:38
  36.1 1.9 %collective-permute-start.7 = (bf16[4,4,1024]{2,1,0:T(4,128)(2,1)S(1)}, bf16[4,4,1024]{2,1,0:T(4,128)(2,1)S(1)}, u32[]{:S(2)}, u32[]{:S(2)}) collective-permute-start(bf16[4,4,1024]{2,1,0:T(4,128)(2,1)S(1)} %shard_map.144.own_ref), channel_id=1, source_target_pairs={{0,4},{2,6},{4,0},{6,2},{8,12},{10,14},{12,8},{14,10},{16,20},{18,... | collective-permute-start | bytes 98312 | tf_op jit(solution)/shard_map/ppermute | solution.py:38
  38.0 2.0 %collective-permute-done.7.other_ref = bf16[4,4,1024]{2,1,0:T(4,128)(2,1)S(1)} collective-permute-done((bf16[4,4,1024]{2,1,0:T(4,128)(2,1)S(1)}, bf16[4,4,1024]{2,1,0:T(4,128)(2,1)S(1)}, u32[]{:S(2)}, u32[]{:S(2)}) %collective-permute-start.7) | collective-permute-done | bytes 32800 | tf_op jit(solution)/shard_map/ppermute | solution.py:38
  40.0 0.0 collective-permute-start.8
  40.0 0.0 copy-done.4
  40.0 1.2 %collective-permute-done.8.far_ref = bf16[8,4,1024]{2,1,0:T(4,128)(2,1)S(1)} collective-permute-done((bf16[8,4,1024]{2,1,0:T(4,128)(2,1)S(1)}, bf16[8,4,1024]{2,1,0:T(4,128)(2,1)S(1)}, u32[]{:S(2)}, u32[]{:S(2)}) %collective-permute-start.8) | collective-permute-done | bytes 65568 | tf_op jit(solution)/shard_map/ppermute | solution.py:38
  41.2 0.0 copy-done.2
  41.2 0.7 %shard_map.146 = bf16[4,1024]{1,0:T(4,128)(2,1)} custom-call(s32[3,4]{1,0:T(4,128)S(1)} %get-tuple-element.17.places_ref, bf16[8,4,1024]{2,1,0:T(4,128)(2,1)S(1)} %shard_map.145.near_ref, bf16[8,4,1024]{2,1,0:T(4,128)(2,1)S(1)} %collective-permute-done.8.far_ref, bf16[4,1024]{1,0:T(4,128)(2,1)S(1)} %copy-done.2, bf16[1,1024]{1,0:T(2,128)(2,1)S(1)} %broadcast_in_dim.40.bias_ref), custom_call_target="tpu_custom_call" | custom-call | tf_op jit(solution)/shard_map/pallas_call | solution.py:199
  (20 shorter events, 0.2 us)
Async XLA Ops:
  1.4 5.9 %collective-permute-start = (bf16[1,4,3072]{2,1,0:T(4,128)(2,1)S(1)}, bf16[1,4,3072]{2,1,0:T(4,128)(2,1)S(1)}, u32[]{:S(2)}, u32[]{:S(2)}) collective-permute-start(bf16[1,4,3072]{2,1,0:T(4,128)(2,1)S(1)} %maximum_bitcast_fusion.own_ref), channel_id=1, source_target_pairs={{0,16},{2,18},{4,20},{6,22},{8,24},{10,26},{12,28},{14,30},{16,0},... | collective-permute-start | bytes 73736 | tf_op jit(solution)/shard_map/ppermute | solution.py:38
  7.3 4.1 %collective-permute-start.1 = (bf16[2,4,3072]{2,1,0:T(4,128)(2,1)S(1)}, bf16[2,4,3072]{2,1,0:T(4,128)(2,1)S(1)}, u32[]{:S(2)}, u32[]{:S(2)}) collective-permute-start(bf16[2,4,3072]{2,1,0:T(4,128)(2,1)S(1)} %shard_map.139.own_ref), channel_id=1, source_target_pairs={{0,8},{2,10},{4,12},{6,14},{8,0},{10,2},{12,4},{14,6},{16,24},{18,... | collective-permute-start | bytes 147464 | tf_op jit(solution)/shard_map/ppermute | solution.py:38
  10.8 6.8 %slice-start = ((s8[6291456]{0:T(1024)(128)(4,1)}), s8[4194304]{0:T(1024)(128)(4,1)S(1)}, s32[]{:S(2)}) async-start(s8[6291456]{0:T(1024)(128)(4,1)} %bitcast.12), calls=%async_computation | async-start | bytes 8388608
  10.8 6.8 %copy-start = (bf16[24,128,1024]{2,1,0:T(8,128)(2,1)S(1)}, bf16[24,128,1024]{2,1,0:T(8,128)(2,1)}, u32[]{:S(2)}) copy-start(bf16[24,128,1024]{2,1,0:T(8,128)(2,1)} %values_ref.1) | copy-start | bytes 18874372
  10.8 6.8 %copy-start.3 = (s32[4,8]{1,0:T(4,128)S(1)}, s32[4,8]{1,0:T(4,128)}, u32[]{:S(2)}) copy-start(s32[4,8]{1,0:T(4,128)} %table_ref.1) | copy-start | bytes 388
  11.4 6.2 %slice-start.1 = ((s8[6291456]{0:T(1024)(128)(4,1)}), s8[2097152]{0:T(1024)(128)(4,1)S(1)}, s32[]{:S(2)}) async-start(s8[6291456]{0:T(1024)(128)(4,1)} %bitcast.12), calls=%async_computation.1 | async-start | bytes 4194304
  11.4 4.7 %collective-permute-start.2 = (bf16[4,4,3072]{2,1,0:T(4,128)(2,1)S(1)}, bf16[4,4,3072]{2,1,0:T(4,128)(2,1)S(1)}, u32[]{:S(2)}, u32[]{:S(2)}) collective-permute-start(bf16[4,4,3072]{2,1,0:T(4,128)(2,1)S(1)} %shard_map.140.own_ref), channel_id=1, source_target_pairs={{0,4},{2,6},{4,0},{6,2},{8,12},{10,14},{12,8},{14,10},{16,20},{18,... | collective-permute-start | bytes 294920 | tf_op jit(solution)/shard_map/ppermute | solution.py:38
  16.1 1.5 %collective-permute-start.3 = (bf16[8,4,3072]{2,1,0:T(4,128)(2,1)S(1)}, bf16[8,4,3072]{2,1,0:T(4,128)(2,1)S(1)}, u32[]{:S(2)}, u32[]{:S(2)}) collective-permute-start(bf16[8,4,3072]{2,1,0:T(4,128)(2,1)S(1)} %shard_map.141.near_ref), channel_id=1, source_target_pairs={{0,2},{2,0},{4,6},{6,4},{8,10},{10,8},{12,14},{14,12},{16,18},{18,... | collective-permute-start | bytes 589832 | tf_op jit(solution)/shard_map/ppermute | solution.py:38
  17.6 2.2 %copy-start.1 = (bf16[1024,2048]{1,0:T(8,128)(2,1)S(1)}, bf16[1024,2048]{1,0:T(8,128)(2,1)}, u32[]{:S(2)}) copy-start(bf16[1024,2048]{1,0:T(8,128)(2,1)} %weight_ref.1) | copy-start | bytes 12582916
  19.8 20.2 %copy-start.4 = (bf16[1024]{0:T(1024)(128)(2,1)S(1)}, bf16[1024]{0:T(1024)(128)(2,1)}, u32[]{:S(2)}) copy-start(bf16[1024]{0:T(1024)(128)(2,1)} %param.17) | copy-start | bytes 6148
  19.8 21.4 %copy-start.2 = (bf16[4,1024]{1,0:T(4,128)(2,1)S(1)}, bf16[4,1024]{1,0:T(4,128)(2,1)}, u32[]{:S(2)}) copy-start(bf16[4,1024]{1,0:T(4,128)(2,1)} %residual_ref.1) | copy-start | bytes 24580
  23.9 3.8 %collective-permute-start.4 = (f32[1,4,1024]{2,1,0:T(4,128)S(1)}, f32[1,4,1024]{2,1,0:T(4,128)S(1)}, u32[]{:S(2)}, u32[]{:S(2)}) collective-permute-start(f32[1,4,1024]{2,1,0:T(4,128)S(1)} %get-tuple-element.8), channel_id=1, source_target_pairs={{0,1},{1,0},{2,3},{3,2},{4,5},{5,4},{6,7},{7,6},{8,9},{9,8},{10,11... | collective-permute-start | bytes 49160 | tf_op jit(solution)/shard_map/ppermute | solution.py:73
  27.7 4.6 %collective-permute-start.5 = (bf16[1,4,1024]{2,1,0:T(4,128)(2,1)S(1)}, bf16[1,4,1024]{2,1,0:T(4,128)(2,1)S(1)}, u32[]{:S(2)}, u32[]{:S(2)}) collective-permute-start(bf16[1,4,1024]{2,1,0:T(4,128)(2,1)S(1)} %add_convert_fusion.own_ref), channel_id=1, source_target_pairs={{0,16},{2,18},{4,20},{6,22},{8,24},{10,26},{12,28},{14,30},{16,0},... | collective-permute-start | bytes 24584 | tf_op jit(solution)/shard_map/ppermute | solution.py:38
  32.3 3.7 %collective-permute-start.6 = (bf16[2,4,1024]{2,1,0:T(4,128)(2,1)S(1)}, bf16[2,4,1024]{2,1,0:T(4,128)(2,1)S(1)}, u32[]{:S(2)}, u32[]{:S(2)}) collective-permute-start(bf16[2,4,1024]{2,1,0:T(4,128)(2,1)S(1)} %shard_map.143.own_ref), channel_id=1, source_target_pairs={{0,8},{2,10},{4,12},{6,14},{8,0},{10,2},{12,4},{14,6},{16,24},{18,... | collective-permute-start | bytes 49160 | tf_op jit(solution)/shard_map/ppermute | solution.py:38
  36.1 3.9 %collective-permute-start.7 = (bf16[4,4,1024]{2,1,0:T(4,128)(2,1)S(1)}, bf16[4,4,1024]{2,1,0:T(4,128)(2,1)S(1)}, u32[]{:S(2)}, u32[]{:S(2)}) collective-permute-start(bf16[4,4,1024]{2,1,0:T(4,128)(2,1)S(1)} %shard_map.144.own_ref), channel_id=1, source_target_pairs={{0,4},{2,6},{4,0},{6,2},{8,12},{10,14},{12,8},{14,10},{16,20},{18,... | collective-permute-start | bytes 98312 | tf_op jit(solution)/shard_map/ppermute | solution.py:38
  40.0 1.3 %collective-permute-start.8 = (bf16[8,4,1024]{2,1,0:T(4,128)(2,1)S(1)}, bf16[8,4,1024]{2,1,0:T(4,128)(2,1)S(1)}, u32[]{:S(2)}, u32[]{:S(2)}) collective-permute-start(bf16[8,4,1024]{2,1,0:T(4,128)(2,1)S(1)} %shard_map.145.near_ref), channel_id=1, source_target_pairs={{0,2},{2,0},{4,6},{6,4},{8,10},{10,8},{12,14},{14,12},{16,18},{18,... | collective-permute-start | bytes 196616 | tf_op jit(solution)/shard_map/ppermute | solution.py:38

commit v3 on v2

--- a/solution.py
+++ b/solution.py
@@ -179,7 +179,7 @@
     rows, width = query_new.shape
     heads = width // HS
     fresh = jnp.concatenate([query_new, key_new, value_new], axis=1)
-    near, far = gather_by_doubling(fresh, devices, [0, 1 << 31, 1 << 31])
+    near, far = gather_by_doubling(fresh, devices, [0, 3 << 30, 1 << 31])
     half_terms = jax.ShapeDtypeStruct((parts // 2, rows, width), F32)
     narrow = jax.ShapeDtypeStruct((rows, width), BF16)
     kept, sent, appended_keys, appended_values = pl.pallas_call(

time: 42.3 us -> 40.2 us (0.950)
  local copies, waits for them, and re-layouts: 3.27 us -> 1.1 us
    unnamed x14 -> x16, local copies, waits for them, and re-layouts: 2.21 us -> 0.04 us
  transfers between devices with their start and end apart: 9 -> 9, of which waited for: 9 -> 9; matrix products, arithmetic and copies ran while one was open for 6% -> 7% of each run, Pallas kernels for 0% -> 0%
where the time goes in v3:
time: 40.2 us; the launch traced here: 39.9 us
  starting transfers between devices  17 us (42%)
  waiting for transfers between devices  13.8 us (34%)
  Pallas kernels  4.83 us (12%)
  other arithmetic  2.39 us (6%)
  local copies, waits for them, and re-layouts  1.1 us (3%)
  between operations  0.81 us (2%)
    ppermute x8, starting transfers between devices, gather_by_doubling(): other = lax.ppermute(held, 'req', [(i, i ^ bit) for i in range(devices)])  14.9 us
    ppermute x8, waiting for transfers between devices, gather_by_doubling(): other = lax.ppermute(held, 'req', [(i, i ^ bit) for i in range(devices)])  12 us
    pallas_call x1, Pallas kernels, on_device(): pl.pallas_call(functools.partial(attend, parts), out_shape=(half_terms, h...  4.04 us
    ppermute x1, starting transfers between devices, sum_by_halving(): kept = kept + lax.ppermute(sent, 'tp', [(i, i ^ bit) for i in range(parts)])  2.04 us
    ppermute x1, waiting for transfers between devices, sum_by_halving(): kept = kept + lax.ppermute(sent, 'tp', [(i, i ^ bit) for i in range(parts)])  1.76 us
  transfers between devices with their start and end apart: 9, of which 9 were waited for; matrix products, arithmetic and copies ran while one was open for 7% of the time, Pallas kernels for 0%

profile of v3, /device:TPU:0, one launch (start us, length us, event | category | flops | bytes accessed | tf_op | source)
XLA Modules:
  0.0 39.9 jit_solution(3739030512281821863)
XLA Ops:
  0.6 0.7 %maximum_bitcast_fusion.own_ref = bf16[1,4,3072]{2,1,0:T(4,128)(2,1)S(1)} fusion(bf16[4,1024]{1,0:T(4,128)(2,1)} %param.14, bf16[4,1024]{1,0:T(4,128)(2,1)} %param.13, bf16[4,1024]{1,0:T(4,128)(2,1)} %param.12), kind=kLoop, calls=%fused_computation.1 | loop fusion | flops 73728 | bytes 49152 | tf_op jit(solution)/shard_map/broadcast_in_dim | solution.py:35
  1.4 4.1 %collective-permute-start = (bf16[1,4,3072]{2,1,0:T(4,128)(2,1)S(1)}, bf16[1,4,3072]{2,1,0:T(4,128)(2,1)S(1)}, u32[]{:S(2)}, u32[]{:S(2)}) collective-permute-start(bf16[1,4,3072]{2,1,0:T(4,128)(2,1)S(1)} %maximum_bitcast_fusion.own_ref), channel_id=1, source_target_pairs={{0,16},{2,18},{4,20},{6,22},{8,24},{10,26},{12,28},{14,30},{16,0},... | collective-permute-start | bytes 73736 | tf_op jit(solution)/shard_map/ppermute | solution.py:38
  5.5 0.7 %convert_element_type.7 = f32[4]{0:T(128)S(1)} convert(s32[4]{0:T(128)} %param.21) | non-fusion elementwise | flops 4 | bytes 32 | tf_op jit(solution)/shard_map/convert_element_type | solution.py:84
  6.2 0.1 pad.8.clone
  6.2 0.1 pad.11.clone
  6.3 0.1 multiply_cosine_fusion
  6.4 0.1 maximum_maximum_fusion.1
  6.5 0.8 %collective-permute-done.other_ref = bf16[1,4,3072]{2,1,0:T(4,128)(2,1)S(1)} collective-permute-done((bf16[1,4,3072]{2,1,0:T(4,128)(2,1)S(1)}, bf16[1,4,3072]{2,1,0:T(4,128)(2,1)S(1)}, u32[]{:S(2)}, u32[]{:S(2)}) %collective-permute-start) | collective-permute-done | bytes 24608 | tf_op jit(solution)/shard_map/ppermute | solution.py:38
  7.3 1.9 %collective-permute-start.1 = (bf16[2,4,3072]{2,1,0:T(4,128)(2,1)S(1)}, bf16[2,4,3072]{2,1,0:T(4,128)(2,1)S(1)}, u32[]{:S(2)}, u32[]{:S(2)}) collective-permute-start(bf16[2,4,3072]{2,1,0:T(4,128)(2,1)S(1)} %shard_map.139.own_ref), channel_id=1, source_target_pairs={{0,8},{2,10},{4,12},{6,14},{8,0},{10,2},{12,4},{14,6},{16,24},{18,... | collective-permute-start | bytes 147464 | tf_op jit(solution)/shard_map/ppermute | solution.py:38
  9.2 0.7 %fusion.8 = (s32[1,4]{1,0:T(1,128)S(1)}, s32[1,4]{1,0:T(1,128)S(1)}, s32[1,4]{1,0:T(1,128)S(1)}, s32[1,4]{1,0:T(1,128)S(1)}) fusion(s32[4]{0:T(128)} %param.23, s32[]{:T(128)S(6)} %axis_index.15, s32[4]{0:T(128)} %param.22), kind=kLoop, calls=%fused_computation.37 | loop fusion | flops 280 | bytes 100 | tf_op jit(solution)/shard_map/stack | solution.py:53
  10.0 0.7 %copy.15.lengths_ref = s32[4,1]{1,0:T(4,128)S(1)} copy(s32[4,1]{0,1:T(1,128)} %bitcast.16) | data formatting | bytes 32 | tf_op jit(solution)/shard_map/broadcast_in_dim | solution.py:197
  10.7 0.0 slice-start
  10.7 0.0 slice-start.2
  10.7 0.1 pad.20.clone
  10.8 0.0 slice-start.1
  10.8 0.0 slice-start.3
  10.8 0.6 %collective-permute-done.1.other_ref = bf16[2,4,3072]{2,1,0:T(4,128)(2,1)S(1)} collective-permute-done((bf16[2,4,3072]{2,1,0:T(4,128)(2,1)S(1)}, bf16[2,4,3072]{2,1,0:T(4,128)(2,1)S(1)}, u32[]{:S(2)}, u32[]{:S(2)}) %collective-permute-start.1) | collective-permute-done | bytes 49184 | tf_op jit(solution)/shard_map/ppermute | solution.py:38
  11.4 0.0 copy-start
  11.4 0.0 copy-start.2
  11.4 2.0 %collective-permute-start.2 = (bf16[4,4,3072]{2,1,0:T(4,128)(2,1)S(1)}, bf16[4,4,3072]{2,1,0:T(4,128)(2,1)S(1)}, u32[]{:S(2)}, u32[]{:S(2)}) collective-permute-start(bf16[4,4,3072]{2,1,0:T(4,128)(2,1)S(1)} %shard_map.140.own_ref), channel_id=1, source_target_pairs={{0,4},{2,6},{4,0},{6,2},{8,12},{10,14},{12,8},{14,10},{16,20},{18,... | collective-permute-start | bytes 294920 | tf_op jit(solution)/shard_map/ppermute | solution.py:38
  13.5 2.6 %collective-permute-done.2.other_ref = bf16[4,4,3072]{2,1,0:T(4,128)(2,1)S(1)} collective-permute-done((bf16[4,4,3072]{2,1,0:T(4,128)(2,1)S(1)}, bf16[4,4,3072]{2,1,0:T(4,128)(2,1)S(1)}, u32[]{:S(2)}, u32[]{:S(2)}) %collective-permute-start.2) | collective-permute-done | bytes 98336 | tf_op jit(solution)/shard_map/ppermute | solution.py:38
  16.1 0.1 collective-permute-start.3
  16.2 0.1 add_add_fusion.1
  16.3 1.4 %collective-permute-done.3.far_ref = bf16[8,4,3072]{2,1,0:T(4,128)(2,1)S(1)} collective-permute-done((bf16[8,4,3072]{2,1,0:T(4,128)(2,1)S(1)}, bf16[8,4,3072]{2,1,0:T(4,128)(2,1)S(1)}, u32[]{:S(2)}, u32[]{:S(2)}) %collective-permute-start.3) | collective-permute-done | bytes 196640 | tf_op jit(solution)/shard_map/ppermute | solution.py:38
  17.6 0.0 slice-done
  17.6 0.0 slice-done.2
  17.6 0.0 slice-done.1
  17.6 0.0 slice-done.3
  17.7 0.0 copy-done
  17.7 0.0 copy-done.2
  17.7 0.0 copy-start.3
  17.7 0.0 copy-start.1
  17.7 4.0 %shard_map.142 = (f32[1,4,1024]{2,1,0:T(4,128)S(1)}, f32[1,4,1024]{2,1,0:T(4,128)S(1)}, bf16[4,1024]{1,0:T(4,128)(2,1)}, bf16[4,1024]{1,0:T(4,128)(2,1)}) custom-call(s32[3,4]{1,0:T(4,128)S(1)} %get-tuple-element.16.places_ref, bf16[8,4,3072]{2,1,0:T(4,128)(2,1)S(1)} %shard_map.141.near_ref, bf16[8,4,3072]{2,1,0:T(4,128)(2,1)S(1)} %collective-permute-done.3.far_ref, ...), custom_call_target="tpu_custom_call" | custom-call | tf_op jit(solution)/shard_map/pallas_call | solution.py:185
  21.8 2.0 %collective-permute-start.4 = (f32[1,4,1024]{2,1,0:T(4,128)S(1)}, f32[1,4,1024]{2,1,0:T(4,128)S(1)}, u32[]{:S(2)}, u32[]{:S(2)}) collective-permute-start(f32[1,4,1024]{2,1,0:T(4,128)S(1)} %get-tuple-element.8), channel_id=1, source_target_pairs={{0,1},{1,0},{2,3},{3,2},{4,5},{5,4},{6,7},{7,6},{8,9},{9,8},{10,11... | collective-permute-start | bytes 49160 | tf_op jit(solution)/shard_map/ppermute | solution.py:73
  23.8 1.8 %collective-permute-done.4 = f32[1,4,1024]{2,1,0:T(4,128)S(1)} collective-permute-done((f32[1,4,1024]{2,1,0:T(4,128)S(1)}, f32[1,4,1024]{2,1,0:T(4,128)S(1)}, u32[]{:S(2)}, u32[]{:S(2)}) %collective-permute-start.4) | collective-permute-done | bytes 16416 | tf_op jit(solution)/shard_map/ppermute | solution.py:73
  25.6 3.0 %collective-permute-start.5 = (bf16[1,4,1024]{2,1,0:T(4,128)(2,1)S(1)}, bf16[1,4,1024]{2,1,0:T(4,128)(2,1)S(1)}, u32[]{:S(2)}, u32[]{:S(2)}) collective-permute-start(bf16[1,4,1024]{2,1,0:T(4,128)(2,1)S(1)} %add_convert_fusion.own_ref), channel_id=1, source_target_pairs={{0,16},{2,18},{4,20},{6,22},{8,24},{10,26},{12,28},{14,30},{16,0},... | collective-permute-start | bytes 24584 | tf_op jit(solution)/shard_map/ppermute | solution.py:38
  28.6 1.6 %collective-permute-done.5.other_ref = bf16[1,4,1024]{2,1,0:T(4,128)(2,1)S(1)} collective-permute-done((bf16[1,4,1024]{2,1,0:T(4,128)(2,1)S(1)}, bf16[1,4,1024]{2,1,0:T(4,128)(2,1)S(1)}, u32[]{:S(2)}, u32[]{:S(2)}) %collective-permute-start.5) | collective-permute-done | bytes 8224 | tf_op jit(solution)/shard_map/ppermute | solution.py:38
  30.2 1.9 %collective-permute-start.6 = (bf16[2,4,1024]{2,1,0:T(4,128)(2,1)S(1)}, bf16[2,4,1024]{2,1,0:T(4,128)(2,1)S(1)}, u32[]{:S(2)}, u32[]{:S(2)}) collective-permute-start(bf16[2,4,1024]{2,1,0:T(4,128)(2,1)S(1)} %shard_map.143.own_ref), channel_id=1, source_target_pairs={{0,8},{2,10},{4,12},{6,14},{8,0},{10,2},{12,4},{14,6},{16,24},{18,... | collective-permute-start | bytes 49160 | tf_op jit(solution)/shard_map/ppermute | solution.py:38
  32.1 1.8 %collective-permute-done.6.other_ref = bf16[2,4,1024]{2,1,0:T(4,128)(2,1)S(1)} collective-permute-done((bf16[2,4,1024]{2,1,0:T(4,128)(2,1)S(1)}, bf16[2,4,1024]{2,1,0:T(4,128)(2,1)S(1)}, u32[]{:S(2)}, u32[]{:S(2)}) %collective-permute-start.6) | collective-permute-done | bytes 16416 | tf_op jit(solution)/shard_map/ppermute | solution.py:38
  33.9 1.9 %collective-permute-start.7 = (bf16[4,4,1024]{2,1,0:T(4,128)(2,1)S(1)}, bf16[4,4,1024]{2,1,0:T(4,128)(2,1)S(1)}, u32[]{:S(2)}, u32[]{:S(2)}) collective-permute-start(bf16[4,4,1024]{2,1,0:T(4,128)(2,1)S(1)} %shard_map.144.own_ref), channel_id=1, source_target_pairs={{0,4},{2,6},{4,0},{6,2},{8,12},{10,14},{12,8},{14,10},{16,20},{18,... | collective-permute-start | bytes 98312 | tf_op jit(solution)/shard_map/ppermute | solution.py:38
  35.9 2.0 %collective-permute-done.7.other_ref = bf16[4,4,1024]{2,1,0:T(4,128)(2,1)S(1)} collective-permute-done((bf16[4,4,1024]{2,1,0:T(4,128)(2,1)S(1)}, bf16[4,4,1024]{2,1,0:T(4,128)(2,1)S(1)}, u32[]{:S(2)}, u32[]{:S(2)}) %collective-permute-start.7) | collective-permute-done | bytes 32800 | tf_op jit(solution)/shard_map/ppermute | solution.py:38
  37.9 0.0 collective-permute-start.8
  37.9 0.0 copy-done.3
  37.9 1.2 %collective-permute-done.8.far_ref = bf16[8,4,1024]{2,1,0:T(4,128)(2,1)S(1)} collective-permute-done((bf16[8,4,1024]{2,1,0:T(4,128)(2,1)S(1)}, bf16[8,4,1024]{2,1,0:T(4,128)(2,1)S(1)}, u32[]{:S(2)}, u32[]{:S(2)}) %collective-permute-start.8) | collective-permute-done | bytes 65568 | tf_op jit(solution)/shard_map/ppermute | solution.py:38
  39.1 0.0 copy-done.1
  39.1 0.7 %shard_map.146 = bf16[4,1024]{1,0:T(4,128)(2,1)} custom-call(s32[3,4]{1,0:T(4,128)S(1)} %get-tuple-element.17.places_ref, bf16[8,4,1024]{2,1,0:T(4,128)(2,1)S(1)} %shard_map.145.near_ref, bf16[8,4,1024]{2,1,0:T(4,128)(2,1)S(1)} %collective-permute-done.8.far_ref, bf16[4,1024]{1,0:T(4,128)(2,1)S(1)} %copy-done.1, bf16[1,1024]{1,0:T(2,128)(2,1)S(1)} %broadcast_in_dim.40.bias_ref), custom_call_target="tpu_custom_call" | custom-call | tf_op jit(solution)/shard_map/pallas_call | solution.py:199
  (21 shorter events, 0.2 us)
Async XLA Ops:
  1.4 5.9 %collective-permute-start = (bf16[1,4,3072]{2,1,0:T(4,128)(2,1)S(1)}, bf16[1,4,3072]{2,1,0:T(4,128)(2,1)S(1)}, u32[]{:S(2)}, u32[]{:S(2)}) collective-permute-start(bf16[1,4,3072]{2,1,0:T(4,128)(2,1)S(1)} %maximum_bitcast_fusion.own_ref), channel_id=1, source_target_pairs={{0,16},{2,18},{4,20},{6,22},{8,24},{10,26},{12,28},{14,30},{16,0},... | collective-permute-start | bytes 73736 | tf_op jit(solution)/shard_map/ppermute | solution.py:38
  7.3 4.1 %collective-permute-start.1 = (bf16[2,4,3072]{2,1,0:T(4,128)(2,1)S(1)}, bf16[2,4,3072]{2,1,0:T(4,128)(2,1)S(1)}, u32[]{:S(2)}, u32[]{:S(2)}) collective-permute-start(bf16[2,4,3072]{2,1,0:T(4,128)(2,1)S(1)} %shard_map.139.own_ref), channel_id=1, source_target_pairs={{0,8},{2,10},{4,12},{6,14},{8,0},{10,2},{12,4},{14,6},{16,24},{18,... | collective-permute-start | bytes 147464 | tf_op jit(solution)/shard_map/ppermute | solution.py:38
  10.7 6.9 %slice-start = ((s8[6291456]{0:T(1024)(128)(4,1)}), s8[4194304]{0:T(1024)(128)(4,1)S(1)}, s32[]{:S(2)}) async-start(s8[6291456]{0:T(1024)(128)(4,1)} %bitcast.12), calls=%async_computation | async-start | bytes 8388608
  10.7 6.9 %slice-start.2 = ((s8[6291456]{0:T(1024)(128)(4,1)}), s8[4194304]{0:T(1024)(128)(4,1)S(1)}, s32[]{:S(2)}) async-start(s8[6291456]{0:T(1024)(128)(4,1)} %bitcast.14), calls=%async_computation.2 | async-start | bytes 8388608
  10.8 6.8 %slice-start.1 = ((s8[6291456]{0:T(1024)(128)(4,1)}), s8[2097152]{0:T(1024)(128)(4,1)S(1)}, s32[]{:S(2)}) async-start(s8[6291456]{0:T(1024)(128)(4,1)} %bitcast.12), calls=%async_computation.1 | async-start | bytes 4194304
  10.8 6.8 %slice-start.3 = ((s8[6291456]{0:T(1024)(128)(4,1)}), s8[2097152]{0:T(1024)(128)(4,1)S(1)}, s32[]{:S(2)}) async-start(s8[6291456]{0:T(1024)(128)(4,1)} %bitcast.14), calls=%async_computation.3 | async-start | bytes 4194304
  11.4 6.3 %copy-start = (bf16[1024,2048]{1,0:T(8,128)(2,1)S(1)}, bf16[1024,2048]{1,0:T(8,128)(2,1)}, u32[]{:S(2)}) copy-start(bf16[1024,2048]{1,0:T(8,128)(2,1)} %weight_ref.1) | copy-start | bytes 12582916
  11.4 6.3 %copy-start.2 = (s32[4,8]{1,0:T(4,128)S(1)}, s32[4,8]{1,0:T(4,128)}, u32[]{:S(2)}) copy-start(s32[4,8]{1,0:T(4,128)} %table_ref.1) | copy-start | bytes 388
  11.4 4.7 %collective-permute-start.2 = (bf16[4,4,3072]{2,1,0:T(4,128)(2,1)S(1)}, bf16[4,4,3072]{2,1,0:T(4,128)(2,1)S(1)}, u32[]{:S(2)}, u32[]{:S(2)}) collective-permute-start(bf16[4,4,3072]{2,1,0:T(4,128)(2,1)S(1)} %shard_map.140.own_ref), channel_id=1, source_target_pairs={{0,4},{2,6},{4,0},{6,2},{8,12},{10,14},{12,8},{14,10},{16,20},{18,... | collective-permute-start | bytes 294920 | tf_op jit(solution)/shard_map/ppermute | solution.py:38
  16.1 1.5 %collective-permute-start.3 = (bf16[8,4,3072]{2,1,0:T(4,128)(2,1)S(1)}, bf16[8,4,3072]{2,1,0:T(4,128)(2,1)S(1)}, u32[]{:S(2)}, u32[]{:S(2)}) collective-permute-start(bf16[8,4,3072]{2,1,0:T(4,128)(2,1)S(1)} %shard_map.141.near_ref), channel_id=1, source_target_pairs={{0,2},{2,0},{4,6},{6,4},{8,10},{10,8},{12,14},{14,12},{16,18},{18,... | collective-permute-start | bytes 589832 | tf_op jit(solution)/shard_map/ppermute | solution.py:38
  17.7 20.2 %copy-start.3 = (bf16[1024]{0:T(1024)(128)(2,1)S(1)}, bf16[1024]{0:T(1024)(128)(2,1)}, u32[]{:S(2)}) copy-start(bf16[1024]{0:T(1024)(128)(2,1)} %param.17) | copy-start | bytes 6148
  17.7 21.4 %copy-start.1 = (bf16[4,1024]{1,0:T(4,128)(2,1)S(1)}, bf16[4,1024]{1,0:T(4,128)(2,1)}, u32[]{:S(2)}) copy-start(bf16[4,1024]{1,0:T(4,128)(2,1)} %residual_ref.1) | copy-start | bytes 24580
  21.8 3.8 %collective-permute-start.4 = (f32[1,4,1024]{2,1,0:T(4,128)S(1)}, f32[1,4,1024]{2,1,0:T(4,128)S(1)}, u32[]{:S(2)}, u32[]{:S(2)}) collective-permute-start(f32[1,4,1024]{2,1,0:T(4,128)S(1)} %get-tuple-element.8), channel_id=1, source_target_pairs={{0,1},{1,0},{2,3},{3,2},{4,5},{5,4},{6,7},{7,6},{8,9},{9,8},{10,11... | collective-permute-start | bytes 49160 | tf_op jit(solution)/shard_map/ppermute | solution.py:73
  25.6 4.6 %collective-permute-start.5 = (bf16[1,4,1024]{2,1,0:T(4,128)(2,1)S(1)}, bf16[1,4,1024]{2,1,0:T(4,128)(2,1)S(1)}, u32[]{:S(2)}, u32[]{:S(2)}) collective-permute-start(bf16[1,4,1024]{2,1,0:T(4,128)(2,1)S(1)} %add_convert_fusion.own_ref), channel_id=1, source_target_pairs={{0,16},{2,18},{4,20},{6,22},{8,24},{10,26},{12,28},{14,30},{16,0},... | collective-permute-start | bytes 24584 | tf_op jit(solution)/shard_map/ppermute | solution.py:38
  30.2 3.7 %collective-permute-start.6 = (bf16[2,4,1024]{2,1,0:T(4,128)(2,1)S(1)}, bf16[2,4,1024]{2,1,0:T(4,128)(2,1)S(1)}, u32[]{:S(2)}, u32[]{:S(2)}) collective-permute-start(bf16[2,4,1024]{2,1,0:T(4,128)(2,1)S(1)} %shard_map.143.own_ref), channel_id=1, source_target_pairs={{0,8},{2,10},{4,12},{6,14},{8,0},{10,2},{12,4},{14,6},{16,24},{18,... | collective-permute-start | bytes 49160 | tf_op jit(solution)/shard_map/ppermute | solution.py:38
  33.9 3.9 %collective-permute-start.7 = (bf16[4,4,1024]{2,1,0:T(4,128)(2,1)S(1)}, bf16[4,4,1024]{2,1,0:T(4,128)(2,1)S(1)}, u32[]{:S(2)}, u32[]{:S(2)}) collective-permute-start(bf16[4,4,1024]{2,1,0:T(4,128)(2,1)S(1)} %shard_map.144.own_ref), channel_id=1, source_target_pairs={{0,4},{2,6},{4,0},{6,2},{8,12},{10,14},{12,8},{14,10},{16,20},{18,... | collective-permute-start | bytes 98312 | tf_op jit(solution)/shard_map/ppermute | solution.py:38
  37.9 1.3 %collective-permute-start.8 = (bf16[8,4,1024]{2,1,0:T(4,128)(2,1)S(1)}, bf16[8,4,1024]{2,1,0:T(4,128)(2,1)S(1)}, u32[]{:S(2)}, u32[]{:S(2)}) collective-permute-start(bf16[8,4,1024]{2,1,0:T(4,128)(2,1)S(1)} %shard_map.145.near_ref), channel_id=1, source_target_pairs={{0,2},{2,0},{4,6},{6,4},{8,10},{10,8},{12,14},{14,12},{16,18},{18,... | collective-permute-start | bytes 196616 | tf_op jit(solution)/shard_map/ppermute | solution.py:38

commit v4 on v3

--- a/solution.py
+++ b/solution.py
@@ -8,37 +8,42 @@
 from jax.sharding import PartitionSpec as P
 
 HS = 256
+TURN = 4<<30
 BF16 = jnp.bfloat16
 F32 = jnp.float32
 ANY = pl.BlockSpec(memory_space=pl.ANY)
 VMEM = pl.BlockSpec(memory_space=pltpu.VMEM)
 
 
-def joined(own_ref, other_ref, out_ref):
+def joined(own_ref, other_ref, *rest):
+    out_ref = rest[-1]
     count = own_ref.shape[0]
     out_ref[:count] = own_ref[...]
     out_ref[count:] = other_ref[...]
 
 
-def join(own, other, work):
+def join(own, other, work, *first):
     return pl.pallas_call(
         joined,
         out_shape=jax.ShapeDtypeStruct((2 * own.shape[0],) + own.shape[1:], own.dtype),
-        in_specs=[VMEM, VMEM],
+        in_specs=[VMEM, VMEM] + [ANY] * len(first),
         out_specs=VMEM,
         cost_estimate=pl.CostEstimate(flops=work, bytes_accessed=work >> 14, transcendentals=0),
         compiler_params=pltpu.CompilerParams(vmem_limit_bytes=1 << 20),
-    )(own, other)
-
-
-def gather_by_doubling(block, devices, works):
+    )(own, other, *first)
+
+
+def gather_by_doubling(block, devices, works, beside=None):
     held = block[None]
     bit = devices // 2
+    extra = ()
     while True:
         other = lax.ppermute(held, "req", [(i, i ^ bit) for i in range(devices)])
         if bit == 1:
-            return held, other
-        held = join(held, other, works.pop(0) if works else 0)
+            return (held, other) + extra
+        if bit == 2 and beside is not None:
+            extra = (beside(held),)
+        held = join(held, other, works.pop(0) if works else 0, *extra)
         bit //= 2
 
 
@@ -92,13 +97,31 @@
     return jnp.stack([jnp.tile(f, (1, heads)) for f in (same, right, left)])
 
 
+def turn(pages_ref, after_ref, out_ref):
+    pages, page, _ = pages_ref.shape
+    for p in range(pages):
+        out_ref[:, p * page:(p + 1) * page] = pages_ref[p].T
+
+
+def turned(pool, after):
+    pages, page, width = pool.shape
+    return pl.pallas_call(
+        turn,
+        out_shape=jax.ShapeDtypeStruct((width, pages * page), pool.dtype),
+        in_specs=[VMEM, ANY],
+        out_specs=VMEM,
+        cost_estimate=pl.CostEstimate(flops=TURN, bytes_accessed=1 << 20, transcendentals=0),
+        compiler_params=pltpu.CompilerParams(vmem_limit_bytes=8 << 20),
+    )(pool, after)
+
+
 def attend(parts, places_ref, near_ref, far_ref, factors_ref, table_ref, lengths_ref,
            keys_ref, values_ref, weight_ref, kept_out, sent_out, keys_out, values_out,
            key_ref, value_ref, sems):
     half = places_ref[...][2, 0]
     slots, width = key_ref.shape
     heads = width // HS
-    pages, page = keys_ref.shape[0], keys_ref.shape[1]
+    pages, page = values_ref.shape[0], values_ref.shape[1]
     tokens = pages * page
     scale = HS ** (-0.5)
 
@@ -137,27 +160,35 @@
         visible = jnp.where((lane == table_ref[:, i:i + 1]) & (left_over > 0), left_over, visible)
     visible = jnp.concatenate([visible] * heads, axis=0)
 
-    scores = lax.dot_general(
-        spread_query.astype(BF16), keys_ref[...].reshape(tokens, width),
-        (((1,), (1,)), ((), ())), preferred_element_type=F32,
-    ) * scale
+    queries = spread_query.astype(BF16)
     place = lax.broadcasted_iota(jnp.int32, (rows, page), 1)
-    masked = jnp.concatenate(
-        [
-            jnp.where(place < visible[:, p:p + 1], scores[:, p * page:(p + 1) * page], -jnp.inf)
-            for p in range(pages)
-        ],
-        axis=1,
-    )
-    top = jnp.maximum(jnp.max(masked, axis=1, keepdims=True), own_score)
-    exps = jnp.exp(masked - top)
+    step = next(n for n in (24, 4, 2, 1) if pages % n == 0)
+    tops, sums, parts_seen = [], [], []
+    for first in range(0, pages, step):
+        scores = jnp.dot(queries, keys_ref[:, first * page:(first + step) * page], preferred_element_type=F32) * scale
+        masked = jnp.concatenate(
+            [
+                jnp.where(place < visible[:, first + p:first + p + 1], scores[:, p * page:(p + 1) * page], -jnp.inf)
+                for p in range(step)
+            ],
+            axis=1,
+        )
+        top = jnp.maximum(jnp.max(masked, axis=1, keepdims=True), own_score)
+        exps = jnp.exp(masked - top)
+        tops.append(top)
+        sums.append(jnp.sum(exps, axis=1, keepdims=True))
+        parts_seen.append(
+            jnp.dot(exps.astype(BF16), values_ref[first:first + step].reshape(step * page, width), preferred_element_type=F32)
+        )
+    top = functools.reduce(jnp.maximum, tops)
     own_exp = jnp.exp(own_score - top)
-    total = jnp.sum(exps, axis=1, keepdims=True) + own_exp
-    share = 1.0 / total
-    weights = (exps * share).astype(BF16)
-    own_weight = (own_exp * share).astype(BF16).astype(F32)
-    attended = jnp.dot(weights, values_ref[...].reshape(tokens, width), preferred_element_type=F32)
-    attended = attended + own_weight * jnp.concatenate([value] * heads, axis=0)
+    total = own_exp
+    attended = own_exp * jnp.concatenate([value] * heads, axis=0)
+    for group_top, group_sum, seen in zip(tops, sums, parts_seen):
+        factor = jnp.exp(group_top - top)
+        total = total + factor * group_sum
+        attended = attended + factor * seen
+    attended = attended * (1.0 / total)
     attended = jnp.where(mine, attended, 0.0)
     attended = sum(attended[h * slots:(h + 1) * slots] for h in range(heads)).astype(BF16)
 
@@ -179,7 +210,7 @@
     rows, width = query_new.shape
     heads = width // HS
     fresh = jnp.concatenate([query_new, key_new, value_new], axis=1)
-    near, far = gather_by_doubling(fresh, devices, [0, 3 << 30, 1 << 31])
+    near, far, keys = gather_by_doubling(fresh, devices, [0,6<<30,2<<30], functools.partial(turned, key_pool))
     half_terms = jax.ShapeDtypeStruct((parts // 2, rows, width), F32)
     narrow = jax.ShapeDtypeStruct((rows, width), BF16)
     kept, sent, appended_keys, appended_values = pl.pallas_call(
@@ -194,7 +225,7 @@
         ],
         compiler_params=pltpu.CompilerParams(vmem_limit_bytes=8 << 20),
     )(places(arrival_index, rows, devices), near, far, rotary_factors(lengths, heads), page_table,
-      lengths[:, None], key_pool, value_pool, dense_weight)
+      lengths[:, None], keys, value_pool, dense_weight)
     near, far = gather_by_doubling(sum_by_halving(kept, sent, parts).astype(BF16), devices, [])
     hidden = pl.pallas_call(
         finish,

time: 40.2 us -> 39.4 us (0.980)
  waiting for transfers between devices: 13.8 us -> 12.4 us
  Pallas kernels: 4.83 us -> 5.91 us
  starting transfers between devices: 17 us -> 16.5 us
    pallas_call x0 -> x1, Pallas kernels: none -> 1.95 us  [turned(): pl.pallas_call(turn, out_shape=jax.ShapeDtypeStruct((width, pages * page)...]
    ppermute x8, waiting for transfers between devices: 12 us -> 10.5 us  [gather_by_doubling(): other = lax.ppermute(held, 'req', [(i, i ^ bit) for i in range(devices)])]
    pallas_call x1, Pallas kernels: 4.04 us -> 3.18 us  [on_device(): pl.pallas_call(functools.partial(attend, parts), out_shape=(half_terms, h...]
    ppermute x8, starting transfers between devices: 14.9 us -> 14.5 us  [gather_by_doubling(): other = lax.ppermute(held, 'req', [(i, i ^ bit) for i in range(devices)])]
  transfers between devices with their start and end apart: 9 -> 9, of which waited for: 9 -> 8; matrix products, arithmetic and copies ran while one was open for 7% -> 7% of each run, Pallas kernels for 0% -> 5%
where the time goes in v4:
time: 39.4 us; the launch traced here: 39.1 us
  starting transfers between devices  16.5 us (42%)
  waiting for transfers between devices  12.4 us (31%)
  Pallas kernels  5.91 us (15%)
  other arithmetic  2.39 us (6%)
  local copies, waits for them, and re-layouts  1.1 us (3%)
  between operations  0.82 us (2%)
    ppermute x8, starting transfers between devices, gather_by_doubling(): other = lax.ppermute(held, 'req', [(i, i ^ bit) for i in range(devices)])  14.5 us
    ppermute x8, waiting for transfers between devices, gather_by_doubling(): other = lax.ppermute(held, 'req', [(i, i ^ bit) for i in range(devices)])  10.5 us
    pallas_call x1, Pallas kernels, on_device(): pl.pallas_call(functools.partial(attend, parts), out_shape=(half_terms, h...  3.18 us
    ppermute x1, starting transfers between devices, sum_by_halving(): kept = kept + lax.ppermute(sent, 'tp', [(i, i ^ bit) for i in range(parts)])  1.95 us
    pallas_call x1, Pallas kernels, turned(): pl.pallas_call(turn, out_shape=jax.ShapeDtypeStruct((width, pages * page)...  1.95 us
    ppermute x1, waiting for transfers between devices, sum_by_halving(): kept = kept + lax.ppermute(sent, 'tp', [(i, i ^ bit) for i in range(parts)])  1.85 us
  transfers between devices with their start and end apart: 9, of which 8 were waited for; matrix products, arithmetic and copies ran while one was open for 7% of the time, Pallas kernels for 5%

profile of v4, /device:TPU:0, one launch (start us, length us, event | category | flops | bytes accessed | tf_op | source)
XLA Modules:
  0.0 39.1 jit_solution(13152624864943019188)
XLA Ops:
  0.6 0.7 %maximum_bitcast_fusion.own_ref = bf16[1,4,3072]{2,1,0:T(4,128)(2,1)S(1)} fusion(bf16[4,1024]{1,0:T(4,128)(2,1)} %param.14, bf16[4,1024]{1,0:T(4,128)(2,1)} %param.13, bf16[4,1024]{1,0:T(4,128)(2,1)} %param.12), kind=kLoop, calls=%fused_computation.1 | loop fusion | flops 73728 | bytes 49152 | tf_op jit(solution)/shard_map/broadcast_in_dim | solution.py:37
  1.4 4.1 %collective-permute-start = (bf16[1,4,3072]{2,1,0:T(4,128)(2,1)S(1)}, bf16[1,4,3072]{2,1,0:T(4,128)(2,1)S(1)}, u32[]{:S(2)}, u32[]{:S(2)}) collective-permute-start(bf16[1,4,3072]{2,1,0:T(4,128)(2,1)S(1)} %maximum_bitcast_fusion.own_ref), channel_id=1, source_target_pairs={{0,16},{2,18},{4,20},{6,22},{8,24},{10,26},{12,28},{14,30},{16,0},... | collective-permute-start | bytes 73736 | tf_op jit(solution)/shard_map/ppermute | solution.py:41
  5.5 0.7 %convert_element_type.7 = f32[4]{0:T(128)S(1)} convert(s32[4]{0:T(128)} %param.21) | non-fusion elementwise | flops 4 | bytes 32 | tf_op jit(solution)/shard_map/convert_element_type | solution.py:89
  6.2 0.1 pad.8.clone
  6.2 0.1 pad.11.clone
  6.3 0.1 multiply_cosine_fusion
  6.4 0.1 maximum_maximum_fusion.1
  6.5 0.7 %fusion.8 = (s32[1,4]{1,0:T(1,128)S(1)}, s32[1,4]{1,0:T(1,128)S(1)}, s32[1,4]{1,0:T(1,128)S(1)}, s32[1,4]{1,0:T(1,128)S(1)}) fusion(s32[4]{0:T(128)} %param.23, s32[]{:T(128)S(6)} %axis_index.15, s32[4]{0:T(128)} %param.22), kind=kLoop, calls=%fused_computation.37 | loop fusion | flops 280 | bytes 100 | tf_op jit(solution)/shard_map/stack | solution.py:58
  7.3 0.0 collective-permute-done.other_ref
  7.3 1.9 %collective-permute-start.1 = (bf16[2,4,3072]{2,1,0:T(4,128)(2,1)S(1)}, bf16[2,4,3072]{2,1,0:T(4,128)(2,1)S(1)}, u32[]{:S(2)}, u32[]{:S(2)}) collective-permute-start(bf16[2,4,3072]{2,1,0:T(4,128)(2,1)S(1)} %shard_map.139.own_ref), channel_id=1, source_target_pairs={{0,8},{2,10},{4,12},{6,14},{8,0},{10,2},{12,4},{14,6},{16,24},{18,... | collective-permute-start | bytes 147464 | tf_op jit(solution)/shard_map/ppermute | solution.py:41
  9.2 0.7 %copy.15.lengths_ref = s32[4,1]{1,0:T(4,128)S(1)} copy(s32[4,1]{0,1:T(1,128)} %bitcast.16) | data formatting | bytes 32 | tf_op jit(solution)/shard_map/broadcast_in_dim | solution.py:228
  10.0 0.0 slice-start.2
  10.0 0.1 pad.20.clone
  10.0 0.0 slice-start.3
  10.0 1.5 %collective-permute-done.1.other_ref = bf16[2,4,3072]{2,1,0:T(4,128)(2,1)S(1)} collective-permute-done((bf16[2,4,3072]{2,1,0:T(4,128)(2,1)S(1)}, bf16[2,4,3072]{2,1,0:T(4,128)(2,1)S(1)}, u32[]{:S(2)}, u32[]{:S(2)}) %collective-permute-start.1) | collective-permute-done | bytes 49184 | tf_op jit(solution)/shard_map/ppermute | solution.py:41
  11.5 0.0 slice-start
  11.5 0.0 slice-start.1
  11.5 1.9 %collective-permute-start.2 = (bf16[4,4,3072]{2,1,0:T(4,128)(2,1)S(1)}, bf16[4,4,3072]{2,1,0:T(4,128)(2,1)S(1)}, u32[]{:S(2)}, u32[]{:S(2)}) collective-permute-start(bf16[4,4,3072]{2,1,0:T(4,128)(2,1)S(1)} %shard_map.140.after_ref.own_ref), channel_id=1, source_target_pairs={{0,4},{2,6},{4,0},{6,2},{8,12},{10,14},{12,8},{14,10},{16,20},{18,... | collective-permute-start | bytes 294920 | tf_op jit(solution)/shard_map/ppermute | solution.py:41
  13.4 0.0 slice-done.2
  13.4 0.0 slice-done.3
  13.4 1.9 %shard_map.141.rest_0_.keys_ref = bf16[1024,3072]{1,0:T(8,128)(2,1)S(1)} custom-call(bf16[24,128,1024]{2,1,0:T(8,128)(2,1)S(1)} %bitcast.15, bf16[4,4,3072]{2,1,0:T(4,128)(2,1)S(1)} %shard_map.140.after_ref.own_ref), custom_call_target="tpu_custom_call" | custom-call | flops 4294967296 | bytes 1048576 | tf_op jit(solution)/shard_map/pallas_call | solution.py:108
  15.4 0.0 copy-start
  15.4 0.0 copy-start.2
  15.4 0.8 %collective-permute-done.2.other_ref = bf16[4,4,3072]{2,1,0:T(4,128)(2,1)S(1)} collective-permute-done((bf16[4,4,3072]{2,1,0:T(4,128)(2,1)S(1)}, bf16[4,4,3072]{2,1,0:T(4,128)(2,1)S(1)}, u32[]{:S(2)}, u32[]{:S(2)}) %collective-permute-start.2) | collective-permute-done | bytes 98336 | tf_op jit(solution)/shard_map/ppermute | solution.py:41
  16.2 0.1 collective-permute-start.3
  16.3 0.1 add_add_fusion.1
  16.4 1.4 %collective-permute-done.3.far_ref = bf16[8,4,3072]{2,1,0:T(4,128)(2,1)S(1)} collective-permute-done((bf16[8,4,3072]{2,1,0:T(4,128)(2,1)S(1)}, bf16[8,4,3072]{2,1,0:T(4,128)(2,1)S(1)}, u32[]{:S(2)}, u32[]{:S(2)}) %collective-permute-start.3) | collective-permute-done | bytes 196640 | tf_op jit(solution)/shard_map/ppermute | solution.py:41
  17.7 0.0 slice-done
  17.7 0.0 slice-done.1
  17.7 0.0 copy-done
  17.7 0.0 copy-done.2
  17.8 0.0 copy-start.3
  17.8 0.0 copy-start.1
  17.8 3.2 %shard_map.143 = (f32[1,4,1024]{2,1,0:T(4,128)S(1)}, f32[1,4,1024]{2,1,0:T(4,128)S(1)}, bf16[4,1024]{1,0:T(4,128)(2,1)}, bf16[4,1024]{1,0:T(4,128)(2,1)}) custom-call(s32[3,4]{1,0:T(4,128)S(1)} %get-tuple-element.16.places_ref, bf16[8,4,3072]{2,1,0:T(4,128)(2,1)S(1)} %shard_map.142.near_ref, bf16[8,4,3072]{2,1,0:T(4,128)(2,1)S(1)} %collective-permute-done.3.far_ref, ...), custom_call_target="tpu_custom_call" | custom-call | tf_op jit(solution)/shard_map/pallas_call | solution.py:216
  21.0 1.9 %collective-permute-start.4 = (f32[1,4,1024]{2,1,0:T(4,128)S(1)}, f32[1,4,1024]{2,1,0:T(4,128)S(1)}, u32[]{:S(2)}, u32[]{:S(2)}) collective-permute-start(f32[1,4,1024]{2,1,0:T(4,128)S(1)} %get-tuple-element.8), channel_id=1, source_target_pairs={{0,1},{1,0},{2,3},{3,2},{4,5},{5,4},{6,7},{7,6},{8,9},{9,8},{10,11... | collective-permute-start | bytes 49160 | tf_op jit(solution)/shard_map/ppermute | solution.py:78
  22.9 1.9 %collective-permute-done.4 = f32[1,4,1024]{2,1,0:T(4,128)S(1)} collective-permute-done((f32[1,4,1024]{2,1,0:T(4,128)S(1)}, f32[1,4,1024]{2,1,0:T(4,128)S(1)}, u32[]{:S(2)}, u32[]{:S(2)}) %collective-permute-start.4) | collective-permute-done | bytes 16416 | tf_op jit(solution)/shard_map/ppermute | solution.py:78
  24.8 2.9 %collective-permute-start.5 = (bf16[1,4,1024]{2,1,0:T(4,128)(2,1)S(1)}, bf16[1,4,1024]{2,1,0:T(4,128)(2,1)S(1)}, u32[]{:S(2)}, u32[]{:S(2)}) collective-permute-start(bf16[1,4,1024]{2,1,0:T(4,128)(2,1)S(1)} %add_convert_fusion.own_ref), channel_id=1, source_target_pairs={{0,16},{2,18},{4,20},{6,22},{8,24},{10,26},{12,28},{14,30},{16,0},... | collective-permute-start | bytes 24584 | tf_op jit(solution)/shard_map/ppermute | solution.py:41
  27.7 1.7 %collective-permute-done.5.other_ref = bf16[1,4,1024]{2,1,0:T(4,128)(2,1)S(1)} collective-permute-done((bf16[1,4,1024]{2,1,0:T(4,128)(2,1)S(1)}, bf16[1,4,1024]{2,1,0:T(4,128)(2,1)S(1)}, u32[]{:S(2)}, u32[]{:S(2)}) %collective-permute-start.5) | collective-permute-done | bytes 8224 | tf_op jit(solution)/shard_map/ppermute | solution.py:41
  29.4 1.8 %collective-permute-start.6 = (bf16[2,4,1024]{2,1,0:T(4,128)(2,1)S(1)}, bf16[2,4,1024]{2,1,0:T(4,128)(2,1)S(1)}, u32[]{:S(2)}, u32[]{:S(2)}) collective-permute-start(bf16[2,4,1024]{2,1,0:T(4,128)(2,1)S(1)} %shard_map.144.own_ref), channel_id=1, source_target_pairs={{0,8},{2,10},{4,12},{6,14},{8,0},{10,2},{12,4},{14,6},{16,24},{18,... | collective-permute-start | bytes 49160 | tf_op jit(solution)/shard_map/ppermute | solution.py:41
  31.2 1.9 %collective-permute-done.6.other_ref = bf16[2,4,1024]{2,1,0:T(4,128)(2,1)S(1)} collective-permute-done((bf16[2,4,1024]{2,1,0:T(4,128)(2,1)S(1)}, bf16[2,4,1024]{2,1,0:T(4,128)(2,1)S(1)}, u32[]{:S(2)}, u32[]{:S(2)}) %collective-permute-start.6) | collective-permute-done | bytes 16416 | tf_op jit(solution)/shard_map/ppermute | solution.py:41
  33.1 1.9 %collective-permute-start.7 = (bf16[4,4,1024]{2,1,0:T(4,128)(2,1)S(1)}, bf16[4,4,1024]{2,1,0:T(4,128)(2,1)S(1)}, u32[]{:S(2)}, u32[]{:S(2)}) collective-permute-start(bf16[4,4,1024]{2,1,0:T(4,128)(2,1)S(1)} %shard_map.145.own_ref), channel_id=1, source_target_pairs={{0,4},{2,6},{4,0},{6,2},{8,12},{10,14},{12,8},{14,10},{16,20},{18,... | collective-permute-start | bytes 98312 | tf_op jit(solution)/shard_map/ppermute | solution.py:41
  35.0 2.1 %collective-permute-done.7.other_ref = bf16[4,4,1024]{2,1,0:T(4,128)(2,1)S(1)} collective-permute-done((bf16[4,4,1024]{2,1,0:T(4,128)(2,1)S(1)}, bf16[4,4,1024]{2,1,0:T(4,128)(2,1)S(1)}, u32[]{:S(2)}, u32[]{:S(2)}) %collective-permute-start.7) | collective-permute-done | bytes 32800 | tf_op jit(solution)/shard_map/ppermute | solution.py:41
  37.0 0.0 collective-permute-start.8
  37.1 0.0 copy-done.3
  37.1 1.2 %collective-permute-done.8.far_ref = bf16[8,4,1024]{2,1,0:T(4,128)(2,1)S(1)} collective-permute-done((bf16[8,4,1024]{2,1,0:T(4,128)(2,1)S(1)}, bf16[8,4,1024]{2,1,0:T(4,128)(2,1)S(1)}, u32[]{:S(2)}, u32[]{:S(2)}) %collective-permute-start.8) | collective-permute-done | bytes 65568 | tf_op jit(solution)/shard_map/ppermute | solution.py:41
  38.3 0.0 copy-done.1
  38.3 0.7 %shard_map.147 = bf16[4,1024]{1,0:T(4,128)(2,1)} custom-call(s32[3,4]{1,0:T(4,128)S(1)} %get-tuple-element.17.places_ref, bf16[8,4,1024]{2,1,0:T(4,128)(2,1)S(1)} %shard_map.146.near_ref, bf16[8,4,1024]{2,1,0:T(4,128)(2,1)S(1)} %collective-permute-done.8.far_ref, bf16[4,1024]{1,0:T(4,128)(2,1)S(1)} %copy-done.1, bf16[1,1024]{1,0:T(2,128)(2,1)S(1)} %broadcast_in_dim.40.bias_ref), custom_call_target="tpu_custom_call" | custom-call | tf_op jit(solution)/shard_map/pallas_call | solution.py:230
  (21 shorter events, 0.2 us)
Async XLA Ops:
  1.4 5.9 %collective-permute-start = (bf16[1,4,3072]{2,1,0:T(4,128)(2,1)S(1)}, bf16[1,4,3072]{2,1,0:T(4,128)(2,1)S(1)}, u32[]{:S(2)}, u32[]{:S(2)}) collective-permute-start(bf16[1,4,3072]{2,1,0:T(4,128)(2,1)S(1)} %maximum_bitcast_fusion.own_ref), channel_id=1, source_target_pairs={{0,16},{2,18},{4,20},{6,22},{8,24},{10,26},{12,28},{14,30},{16,0},... | collective-permute-start | bytes 73736 | tf_op jit(solution)/shard_map/ppermute | solution.py:41
  7.3 4.2 %collective-permute-start.1 = (bf16[2,4,3072]{2,1,0:T(4,128)(2,1)S(1)}, bf16[2,4,3072]{2,1,0:T(4,128)(2,1)S(1)}, u32[]{:S(2)}, u32[]{:S(2)}) collective-permute-start(bf16[2,4,3072]{2,1,0:T(4,128)(2,1)S(1)} %shard_map.139.own_ref), channel_id=1, source_target_pairs={{0,8},{2,10},{4,12},{6,14},{8,0},{10,2},{12,4},{14,6},{16,24},{18,... | collective-permute-start | bytes 147464 | tf_op jit(solution)/shard_map/ppermute | solution.py:41
  10.0 3.5 %slice-start.2 = ((s8[6291456]{0:T(1024)(128)(4,1)}), s8[2097152]{0:T(1024)(128)(4,1)S(1)}, s32[]{:S(2)}) async-start(s8[6291456]{0:T(1024)(128)(4,1)} %bitcast.14), calls=%async_computation.2 | async-start | bytes 4194304
  10.0 3.4 %slice-start.3 = ((s8[6291456]{0:T(1024)(128)(4,1)}), s8[4194304]{0:T(1024)(128)(4,1)S(1)}, s32[]{:S(2)}) async-start(s8[6291456]{0:T(1024)(128)(4,1)} %bitcast.14), calls=%async_computation.3 | async-start | bytes 8388608
  11.5 6.2 %slice-start = ((s8[6291456]{0:T(1024)(128)(4,1)}), s8[4194304]{0:T(1024)(128)(4,1)S(1)}, s32[]{:S(2)}) async-start(s8[6291456]{0:T(1024)(128)(4,1)} %bitcast.12), calls=%async_computation | async-start | bytes 8388608
  11.5 6.2 %slice-start.1 = ((s8[6291456]{0:T(1024)(128)(4,1)}), s8[2097152]{0:T(1024)(128)(4,1)S(1)}, s32[]{:S(2)}) async-start(s8[6291456]{0:T(1024)(128)(4,1)} %bitcast.12), calls=%async_computation.1 | async-start | bytes 4194304
  11.5 4.7 %collective-permute-start.2 = (bf16[4,4,3072]{2,1,0:T(4,128)(2,1)S(1)}, bf16[4,4,3072]{2,1,0:T(4,128)(2,1)S(1)}, u32[]{:S(2)}, u32[]{:S(2)}) collective-permute-start(bf16[4,4,3072]{2,1,0:T(4,128)(2,1)S(1)} %shard_map.140.after_ref.own_ref), channel_id=1, source_target_pairs={{0,4},{2,6},{4,0},{6,2},{8,12},{10,14},{12,8},{14,10},{16,20},{18,... | collective-permute-start | bytes 294920 | tf_op jit(solution)/shard_map/ppermute | solution.py:41
  15.4 2.3 %copy-start = (bf16[1024,2048]{1,0:T(8,128)(2,1)S(1)}, bf16[1024,2048]{1,0:T(8,128)(2,1)}, u32[]{:S(2)}) copy-start(bf16[1024,2048]{1,0:T(8,128)(2,1)} %weight_ref.1) | copy-start | bytes 12582916
  15.4 2.3 %copy-start.2 = (s32[4,8]{1,0:T(4,128)S(1)}, s32[4,8]{1,0:T(4,128)}, u32[]{:S(2)}) copy-start(s32[4,8]{1,0:T(4,128)} %table_ref.1) | copy-start | bytes 388
  16.2 1.5 %collective-permute-start.3 = (bf16[8,4,3072]{2,1,0:T(4,128)(2,1)S(1)}, bf16[8,4,3072]{2,1,0:T(4,128)(2,1)S(1)}, u32[]{:S(2)}, u32[]{:S(2)}) collective-permute-start(bf16[8,4,3072]{2,1,0:T(4,128)(2,1)S(1)} %shard_map.142.near_ref), channel_id=1, source_target_pairs={{0,2},{2,0},{4,6},{6,4},{8,10},{10,8},{12,14},{14,12},{16,18},{18,... | collective-permute-start | bytes 589832 | tf_op jit(solution)/shard_map/ppermute | solution.py:41
  17.8 19.3 %copy-start.3 = (bf16[1024]{0:T(1024)(128)(2,1)S(1)}, bf16[1024]{0:T(1024)(128)(2,1)}, u32[]{:S(2)}) copy-start(bf16[1024]{0:T(1024)(128)(2,1)} %param.17) | copy-start | bytes 6148
  17.8 20.5 %copy-start.1 = (bf16[4,1024]{1,0:T(4,128)(2,1)S(1)}, bf16[4,1024]{1,0:T(4,128)(2,1)}, u32[]{:S(2)}) copy-start(bf16[4,1024]{1,0:T(4,128)(2,1)} %residual_ref.1) | copy-start | bytes 24580
  21.0 3.8 %collective-permute-start.4 = (f32[1,4,1024]{2,1,0:T(4,128)S(1)}, f32[1,4,1024]{2,1,0:T(4,128)S(1)}, u32[]{:S(2)}, u32[]{:S(2)}) collective-permute-start(f32[1,4,1024]{2,1,0:T(4,128)S(1)} %get-tuple-element.8), channel_id=1, source_target_pairs={{0,1},{1,0},{2,3},{3,2},{4,5},{5,4},{6,7},{7,6},{8,9},{9,8},{10,11... | collective-permute-start | bytes 49160 | tf_op jit(solution)/shard_map/ppermute | solution.py:78
  24.8 4.6 %collective-permute-start.5 = (bf16[1,4,1024]{2,1,0:T(4,128)(2,1)S(1)}, bf16[1,4,1024]{2,1,0:T(4,128)(2,1)S(1)}, u32[]{:S(2)}, u32[]{:S(2)}) collective-permute-start(bf16[1,4,1024]{2,1,0:T(4,128)(2,1)S(1)} %add_convert_fusion.own_ref), channel_id=1, source_target_pairs={{0,16},{2,18},{4,20},{6,22},{8,24},{10,26},{12,28},{14,30},{16,0},... | collective-permute-start | bytes 24584 | tf_op jit(solution)/shard_map/ppermute | solution.py:41
  29.4 3.7 %collective-permute-start.6 = (bf16[2,4,1024]{2,1,0:T(4,128)(2,1)S(1)}, bf16[2,4,1024]{2,1,0:T(4,128)(2,1)S(1)}, u32[]{:S(2)}, u32[]{:S(2)}) collective-permute-start(bf16[2,4,1024]{2,1,0:T(4,128)(2,1)S(1)} %shard_map.144.own_ref), channel_id=1, source_target_pairs={{0,8},{2,10},{4,12},{6,14},{8,0},{10,2},{12,4},{14,6},{16,24},{18,... | collective-permute-start | bytes 49160 | tf_op jit(solution)/shard_map/ppermute | solution.py:41
  33.1 3.9 %collective-permute-start.7 = (bf16[4,4,1024]{2,1,0:T(4,128)(2,1)S(1)}, bf16[4,4,1024]{2,1,0:T(4,128)(2,1)S(1)}, u32[]{:S(2)}, u32[]{:S(2)}) collective-permute-start(bf16[4,4,1024]{2,1,0:T(4,128)(2,1)S(1)} %shard_map.145.own_ref), channel_id=1, source_target_pairs={{0,4},{2,6},{4,0},{6,2},{8,12},{10,14},{12,8},{14,10},{16,20},{18,... | collective-permute-start | bytes 98312 | tf_op jit(solution)/shard_map/ppermute | solution.py:41
  37.0 1.3 %collective-permute-start.8 = (bf16[8,4,1024]{2,1,0:T(4,128)(2,1)S(1)}, bf16[8,4,1024]{2,1,0:T(4,128)(2,1)S(1)}, u32[]{:S(2)}, u32[]{:S(2)}) collective-permute-start(bf16[8,4,1024]{2,1,0:T(4,128)(2,1)S(1)} %shard_map.146.near_ref), channel_id=1, source_target_pairs={{0,2},{2,0},{4,6},{6,4},{8,10},{10,8},{12,14},{14,12},{16,18},{18,... | collective-permute-start | bytes 196616 | tf_op jit(solution)/shard_map/ppermute | solution.py:41

commit v5 on v4

--- a/solution.py
+++ b/solution.py
@@ -75,11 +75,11 @@
 def sum_by_halving(kept, sent, parts):
     bit = parts // 2
     while True:
-        kept = kept + lax.ppermute(sent, "tp", [(i, i ^ bit) for i in range(parts)])
+        kept = kept + lax.ppermute(sent, "tp", [(i, i ^ bit) for i in range(parts)]).astype(F32)
         if bit == 1:
             return kept[0]
         bit //= 2
-        kept, sent = kept[:bit], kept[bit:]
+        kept, sent = kept[:bit], kept[bit:].astype(BF16)
 
 
 def rotary_factors(lengths, heads):
@@ -115,8 +115,14 @@
     )(pool, after)
 
 
+def project(attended, weight_ref, part):
+    width = attended.shape[1]
+    columns = pl.ds(pl.multiple_of(part * width, width), width)
+    return jnp.dot(attended, weight_ref[:, columns], preferred_element_type=F32)
+
+
 def attend(parts, places_ref, near_ref, far_ref, factors_ref, table_ref, lengths_ref,
-           keys_ref, values_ref, weight_ref, kept_out, sent_out, keys_out, values_out,
+           keys_ref, values_ref, weight_ref, attended_out, sent_out, keys_out, values_out,
            key_ref, value_ref, sems):
     half = places_ref[...][2, 0]
     slots, width = key_ref.shape
@@ -144,60 +150,52 @@
     for copy in copies:
         copy.start()
 
-    rows = heads * slots
-    row_head = lax.broadcasted_iota(jnp.int32, (rows, width), 0) // slots
-    lane_head = lax.broadcasted_iota(jnp.int32, (rows, width), 1) // HS
-    mine = row_head == lane_head
-    spread_query = jnp.where(mine, jnp.concatenate([query] * heads, axis=0), 0.0)
-    own_score = jnp.sum(
-        spread_query * jnp.concatenate([key.astype(F32)] * heads, axis=0), axis=1, keepdims=True
-    ) * scale
-
     lane = lax.broadcasted_iota(jnp.int32, (slots, 128), 1)
     visible = jnp.zeros((slots, 128), jnp.int32)
     for i in range(table_ref.shape[1]):
         left_over = jnp.clip(lengths_ref[...] - i * page, 0, page)
         visible = jnp.where((lane == table_ref[:, i:i + 1]) & (left_over > 0), left_over, visible)
-    visible = jnp.concatenate([visible] * heads, axis=0)
-
-    queries = spread_query.astype(BF16)
+
+    together = min(1, heads)
+    rows, lanes = together * slots, together * HS
+    row_head = lax.broadcasted_iota(jnp.int32, (rows, lanes), 0) // slots
+    lane_head = lax.broadcasted_iota(jnp.int32, (rows, lanes), 1) // HS
+    mine = row_head == lane_head
     place = lax.broadcasted_iota(jnp.int32, (rows, page), 1)
-    step = next(n for n in (24, 4, 2, 1) if pages % n == 0)
-    tops, sums, parts_seen = [], [], []
-    for first in range(0, pages, step):
-        scores = jnp.dot(queries, keys_ref[:, first * page:(first + step) * page], preferred_element_type=F32) * scale
+    shown = jnp.concatenate([visible] * together, axis=0)
+    shown = [place < shown[:, p:p + 1] for p in range(pages)]
+    attended = []
+    for first in range(0, width, lanes):
+        spread = [jnp.concatenate([x[:, first:first + lanes]] * together, axis=0) for x in (query, key.astype(F32), value)]
+        queries = jnp.where(mine, spread[0], 0.0)
+        own_score = jnp.sum(queries * spread[1], axis=1, keepdims=True) * scale
+        scores = jnp.dot(queries.astype(BF16), keys_ref[first:first + lanes], preferred_element_type=F32) * scale
         masked = jnp.concatenate(
-            [
-                jnp.where(place < visible[:, first + p:first + p + 1], scores[:, p * page:(p + 1) * page], -jnp.inf)
-                for p in range(step)
-            ],
-            axis=1,
+            [jnp.where(shown[p], scores[:, p * page:(p + 1) * page], -jnp.inf) for p in range(pages)], axis=1
         )
         top = jnp.maximum(jnp.max(masked, axis=1, keepdims=True), own_score)
         exps = jnp.exp(masked - top)
-        tops.append(top)
-        sums.append(jnp.sum(exps, axis=1, keepdims=True))
-        parts_seen.append(
-            jnp.dot(exps.astype(BF16), values_ref[first:first + step].reshape(step * page, width), preferred_element_type=F32)
+        own_exp = jnp.exp(own_score - top)
+        total = jnp.sum(exps, axis=1, keepdims=True) + own_exp
+        seen = jnp.dot(
+            exps.astype(BF16),
+            values_ref[:, :, first:first + lanes].reshape(tokens, lanes),
+            preferred_element_type=F32,
         )
-    top = functools.reduce(jnp.maximum, tops)
-    own_exp = jnp.exp(own_score - top)
-    total = own_exp
-    attended = own_exp * jnp.concatenate([value] * heads, axis=0)
-    for group_top, group_sum, seen in zip(tops, sums, parts_seen):
-        factor = jnp.exp(group_top - top)
-        total = total + factor * group_sum
-        attended = attended + factor * seen
-    attended = attended * (1.0 / total)
-    attended = jnp.where(mine, attended, 0.0)
-    attended = sum(attended[h * slots:(h + 1) * slots] for h in range(heads)).astype(BF16)
-
-    for i in range(parts):
-        columns = pl.ds(pl.multiple_of((half ^ i) * width, width), width)
-        out = kept_out if i < parts // 2 else sent_out
-        out[i % (parts // 2)] = jnp.dot(attended, weight_ref[:, columns], preferred_element_type=F32)
+        seen = jnp.where(mine, (seen + own_exp * spread[2]) * (1.0 / total), 0.0)
+        attended.append(sum(seen[h * slots:(h + 1) * slots] for h in range(together)))
+    attended = jnp.concatenate(attended, axis=1).astype(BF16)
+
+    attended_out[...] = attended
+    for i in range(parts // 2):
+        sent_out[i] = project(attended, weight_ref, half ^ (parts // 2 + i)).astype(BF16)
     for copy in copies:
         copy.wait()
+
+
+def keep(parts, places_ref, attended_ref, weight_ref, kept_out):
+    for i in range(parts // 2):
+        kept_out[i] = project(attended_ref[...], weight_ref, places_ref[...][2, 0] ^ i)
 
 
 def finish(places_ref, near_ref, far_ref, residual_ref, bias_ref, out_ref):
@@ -211,11 +209,11 @@
     heads = width // HS
     fresh = jnp.concatenate([query_new, key_new, value_new], axis=1)
     near, far, keys = gather_by_doubling(fresh, devices, [0,6<<30,2<<30], functools.partial(turned, key_pool))
-    half_terms = jax.ShapeDtypeStruct((parts // 2, rows, width), F32)
     narrow = jax.ShapeDtypeStruct((rows, width), BF16)
-    kept, sent, appended_keys, appended_values = pl.pallas_call(
+    where = places(arrival_index, rows, devices)
+    attended, sent, appended_keys, appended_values = pl.pallas_call(
         functools.partial(attend, parts),
-        out_shape=(half_terms, half_terms, narrow, narrow),
+        out_shape=(narrow, jax.ShapeDtypeStruct((parts // 2, rows, width), BF16), narrow, narrow),
         in_specs=[VMEM] * 9,
         out_specs=(VMEM, VMEM, ANY, ANY),
         scratch_shapes=[
@@ -224,8 +222,15 @@
             pltpu.SemaphoreType.DMA((2,)),
         ],
         compiler_params=pltpu.CompilerParams(vmem_limit_bytes=8 << 20),
-    )(places(arrival_index, rows, devices), near, far, rotary_factors(lengths, heads), page_table,
-      lengths[:, None], keys, value_pool, dense_weight)
+    )(where, near, far, rotary_factors(lengths, heads), page_table, lengths[:, None], keys, value_pool, dense_weight)
+    kept = pl.pallas_call(
+        functools.partial(keep, parts),
+        out_shape=jax.ShapeDtypeStruct((parts // 2, rows, width), F32),
+        in_specs=[VMEM] * 3,
+        out_specs=VMEM,
+        cost_estimate=pl.CostEstimate(flops=1 << 30, bytes_accessed=1 << 20, transcendentals=0),
+        compiler_params=pltpu.CompilerParams(vmem_limit_bytes=8 << 20),
+    )(where, attended, dense_weight)
     near, far = gather_by_doubling(sum_by_halving(kept, sent, parts).astype(BF16), devices, [])
     hidden = pl.pallas_call(
         finish,

time: 39.4 us -> 38.9 us (0.987)
  waiting for transfers between devices: 12.4 us -> 11.9 us
    ppermute x1, waiting for transfers between devices: 1.85 us -> 1.36 us  [sum_by_halving(): lax.ppermute(sent, 'tp', [(i, i ^ bit) for i in range(parts)]).astype(F32)]
    pallas_call x1 -> x2, Pallas kernels: 3.18 us -> 3.21 us  [the longest x1 2.8 us: on_device(): pl.pallas_call(functools.partial(attend, parts), out_shape=(narrow, jax.S...]
  transfers between devices with their start and end apart: 9 -> 9, of which waited for: 8 -> 8; matrix products, arithmetic and copies ran while one was open for 7% -> 7% of each run, Pallas kernels for 5% -> 6%
where the time goes in v5:
time: 38.9 us; the launch traced here: 38.6 us
  starting transfers between devices  16.5 us (42%)
  waiting for transfers between devices  11.9 us (31%)
  Pallas kernels  5.94 us (15%)
  other arithmetic  2.39 us (6%)
  local copies, waits for them, and re-layouts  1.1 us (3%)
  between operations  0.82 us (2%)
    ppermute x8, starting transfers between devices, gather_by_doubling(): other = lax.ppermute(held, 'req', [(i, i ^ bit) for i in range(devices)])  14.5 us
    ppermute x8, waiting for transfers between devices, gather_by_doubling(): other = lax.ppermute(held, 'req', [(i, i ^ bit) for i in range(devices)])  10.5 us
    pallas_call x1, Pallas kernels, on_device(): pl.pallas_call(functools.partial(attend, parts), out_shape=(narrow, jax.S...  2.8 us
    ppermute x1, starting transfers between devices, sum_by_halving(): lax.ppermute(sent, 'tp', [(i, i ^ bit) for i in range(parts)]).astype(F32)  1.95 us
    pallas_call x1, Pallas kernels, turned(): pl.pallas_call(turn, out_shape=jax.ShapeDtypeStruct((width, pages * page)...  1.95 us
    ppermute x1, waiting for transfers between devices, sum_by_halving(): lax.ppermute(sent, 'tp', [(i, i ^ bit) for i in range(parts)]).astype(F32)  1.36 us
  transfers between devices with their start and end apart: 9, of which 8 were waited for; matrix products, arithmetic and copies ran while one was open for 7% of the time, Pallas kernels for 6%

profile of v5, /device:TPU:0, one launch (start us, length us, event | category | flops | bytes accessed | tf_op | source)
XLA Modules:
  0.0 38.6 jit_solution(15896241990009903753)
XLA Ops:
  0.6 0.7 %maximum_bitcast_fusion.own_ref = bf16[1,4,3072]{2,1,0:T(4,128)(2,1)S(1)} fusion(bf16[4,1024]{1,0:T(4,128)(2,1)} %param.14, bf16[4,1024]{1,0:T(4,128)(2,1)} %param.13, bf16[4,1024]{1,0:T(4,128)(2,1)} %param.12), kind=kLoop, calls=%fused_computation.1 | loop fusion | flops 73728 | bytes 49152 | tf_op jit(solution)/shard_map/broadcast_in_dim | solution.py:37
  1.4 4.1 %collective-permute-start = (bf16[1,4,3072]{2,1,0:T(4,128)(2,1)S(1)}, bf16[1,4,3072]{2,1,0:T(4,128)(2,1)S(1)}, u32[]{:S(2)}, u32[]{:S(2)}) collective-permute-start(bf16[1,4,3072]{2,1,0:T(4,128)(2,1)S(1)} %maximum_bitcast_fusion.own_ref), channel_id=1, source_target_pairs={{0,16},{2,18},{4,20},{6,22},{8,24},{10,26},{12,28},{14,30},{16,0},... | collective-permute-start | bytes 73736 | tf_op jit(solution)/shard_map/ppermute | solution.py:41
  5.5 0.7 %convert_element_type.10 = f32[4]{0:T(128)S(1)} convert(s32[4]{0:T(128)} %param.21) | non-fusion elementwise | flops 4 | bytes 32 | tf_op jit(solution)/shard_map/convert_element_type | solution.py:89
  6.2 0.1 pad.11.clone
  6.2 0.1 pad.8.clone
  6.3 0.1 multiply_cosine_fusion
  6.4 0.1 maximum_maximum_fusion.1
  6.5 0.7 %fusion.8 = (s32[1,4]{1,0:T(1,128)S(1)}, s32[1,4]{1,0:T(1,128)S(1)}, s32[1,4]{1,0:T(1,128)S(1)}, s32[1,4]{1,0:T(1,128)S(1)}) fusion(s32[4]{0:T(128)} %param.23, s32[]{:T(128)S(6)} %axis_index.15, s32[4]{0:T(128)} %param.22), kind=kLoop, calls=%fused_computation.37 | loop fusion | flops 280 | bytes 100 | tf_op jit(solution)/shard_map/stack | solution.py:58
  7.3 0.0 collective-permute-done.other_ref
  7.3 1.9 %collective-permute-start.1 = (bf16[2,4,3072]{2,1,0:T(4,128)(2,1)S(1)}, bf16[2,4,3072]{2,1,0:T(4,128)(2,1)S(1)}, u32[]{:S(2)}, u32[]{:S(2)}) collective-permute-start(bf16[2,4,3072]{2,1,0:T(4,128)(2,1)S(1)} %shard_map.139.own_ref), channel_id=1, source_target_pairs={{0,8},{2,10},{4,12},{6,14},{8,0},{10,2},{12,4},{14,6},{16,24},{18,... | collective-permute-start | bytes 147464 | tf_op jit(solution)/shard_map/ppermute | solution.py:41
  9.2 0.7 %copy.15.lengths_ref = s32[4,1]{1,0:T(4,128)S(1)} copy(s32[4,1]{0,1:T(1,128)} %bitcast.16) | data formatting | bytes 32 | tf_op jit(solution)/shard_map/broadcast_in_dim | solution.py:225
  10.0 0.0 slice-start.2
  10.0 0.1 pad.20.clone
  10.0 0.0 slice-start.3
  10.0 1.5 %collective-permute-done.1.other_ref = bf16[2,4,3072]{2,1,0:T(4,128)(2,1)S(1)} collective-permute-done((bf16[2,4,3072]{2,1,0:T(4,128)(2,1)S(1)}, bf16[2,4,3072]{2,1,0:T(4,128)(2,1)S(1)}, u32[]{:S(2)}, u32[]{:S(2)}) %collective-permute-start.1) | collective-permute-done | bytes 49184 | tf_op jit(solution)/shard_map/ppermute | solution.py:41
  11.5 0.0 slice-start
  11.5 0.0 slice-start.1
  11.5 1.9 %collective-permute-start.2 = (bf16[4,4,3072]{2,1,0:T(4,128)(2,1)S(1)}, bf16[4,4,3072]{2,1,0:T(4,128)(2,1)S(1)}, u32[]{:S(2)}, u32[]{:S(2)}) collective-permute-start(bf16[4,4,3072]{2,1,0:T(4,128)(2,1)S(1)} %shard_map.140.after_ref.own_ref), channel_id=1, source_target_pairs={{0,4},{2,6},{4,0},{6,2},{8,12},{10,14},{12,8},{14,10},{16,20},{18,... | collective-permute-start | bytes 294920 | tf_op jit(solution)/shard_map/ppermute | solution.py:41
  13.4 0.0 slice-done.2
  13.4 0.0 slice-done.3
  13.4 1.9 %shard_map.141.rest_0_.keys_ref = bf16[1024,3072]{1,0:T(8,128)(2,1)S(1)} custom-call(bf16[24,128,1024]{2,1,0:T(8,128)(2,1)S(1)} %bitcast.15, bf16[4,4,3072]{2,1,0:T(4,128)(2,1)S(1)} %shard_map.140.after_ref.own_ref), custom_call_target="tpu_custom_call" | custom-call | flops 4294967296 | bytes 1048576 | tf_op jit(solution)/shard_map/pallas_call | solution.py:108
  15.4 0.0 copy-start
  15.4 0.0 copy-start.2
  15.4 0.8 %collective-permute-done.2.other_ref = bf16[4,4,3072]{2,1,0:T(4,128)(2,1)S(1)} collective-permute-done((bf16[4,4,3072]{2,1,0:T(4,128)(2,1)S(1)}, bf16[4,4,3072]{2,1,0:T(4,128)(2,1)S(1)}, u32[]{:S(2)}, u32[]{:S(2)}) %collective-permute-start.2) | collective-permute-done | bytes 98336 | tf_op jit(solution)/shard_map/ppermute | solution.py:41
  16.2 0.1 collective-permute-start.3
  16.3 0.1 add_add_fusion.1
  16.4 1.4 %collective-permute-done.3.far_ref = bf16[8,4,3072]{2,1,0:T(4,128)(2,1)S(1)} collective-permute-done((bf16[8,4,3072]{2,1,0:T(4,128)(2,1)S(1)}, bf16[8,4,3072]{2,1,0:T(4,128)(2,1)S(1)}, u32[]{:S(2)}, u32[]{:S(2)}) %collective-permute-start.3) | collective-permute-done | bytes 196640 | tf_op jit(solution)/shard_map/ppermute | solution.py:41
  17.7 0.0 slice-done
  17.7 0.0 slice-done.1
  17.7 0.0 copy-done
  17.7 0.0 copy-done.2
  17.8 0.0 copy-start.3
  17.8 0.0 copy-start.1
  17.8 2.8 %shard_map.143 = (bf16[4,1024]{1,0:T(4,128)(2,1)S(1)}, bf16[1,4,1024]{2,1,0:T(4,128)(2,1)S(1)}, bf16[4,1024]{1,0:T(4,128)(2,1)}, bf16[4,1024]{1,0:T(4,128)(2,1)}) custom-call(s32[3,4]{1,0:T(4,128)S(1)} %get-tuple-element.16.places_ref, bf16[8,4,3072]{2,1,0:T(4,128)(2,1)S(1)} %shard_map.142.near_ref, bf16[8,4,3072]{2,1,0:T(4,128)(2,1)S(1)} %collective-permute-done.3.far_ref, ...), custom_call_target="tpu_custom_call" | custom-call | tf_op jit(solution)/shard_map/pallas_call | solution.py:214
  20.6 1.9 %collective-permute-start.4 = (bf16[1,4,1024]{2,1,0:T(4,128)(2,1)S(1)}, bf16[1,4,1024]{2,1,0:T(4,128)(2,1)S(1)}, u32[]{:S(2)}, u32[]{:S(2)}) collective-permute-start(bf16[1,4,1024]{2,1,0:T(4,128)(2,1)S(1)} %get-tuple-element.8), channel_id=1, source_target_pairs={{0,1},{1,0},{2,3},{3,2},{4,5},{5,4},{6,7},{7,6},{8,9},{9,8},{10,11... | collective-permute-start | bytes 24584 | tf_op jit(solution)/shard_map/ppermute | solution.py:78
  22.5 0.4 %shard_map.144 = f32[1,4,1024]{2,1,0:T(4,128)S(1)} custom-call(s32[3,4]{1,0:T(4,128)S(1)} %get-tuple-element.16.places_ref, bf16[4,1024]{1,0:T(4,128)(2,1)S(1)} %get-tuple-element.7.attended_ref, bf16[1024,2048]{1,0:T(8,128)(2,1)S(1)} %copy-done), custom_call_target="tpu_custom_call" | custom-call | flops 1073741824 | bytes 1048576 | tf_op jit(solution)/shard_map/pallas_call | solution.py:226
  22.9 1.4 %collective-permute-done.4 = bf16[1,4,1024]{2,1,0:T(4,128)(2,1)S(1)} collective-permute-done((bf16[1,4,1024]{2,1,0:T(4,128)(2,1)S(1)}, bf16[1,4,1024]{2,1,0:T(4,128)(2,1)S(1)}, u32[]{:S(2)}, u32[]{:S(2)}) %collective-permute-start.4) | collective-permute-done | bytes 8224 | tf_op jit(solution)/shard_map/ppermute | solution.py:78
  24.3 2.9 %collective-permute-start.5 = (bf16[1,4,1024]{2,1,0:T(4,128)(2,1)S(1)}, bf16[1,4,1024]{2,1,0:T(4,128)(2,1)S(1)}, u32[]{:S(2)}, u32[]{:S(2)}) collective-permute-start(bf16[1,4,1024]{2,1,0:T(4,128)(2,1)S(1)} %add_convert_fusion.own_ref), channel_id=1, source_target_pairs={{0,16},{2,18},{4,20},{6,22},{8,24},{10,26},{12,28},{14,30},{16,0},... | collective-permute-start | bytes 24584 | tf_op jit(solution)/shard_map/ppermute | solution.py:41
  27.2 1.7 %collective-permute-done.5.other_ref = bf16[1,4,1024]{2,1,0:T(4,128)(2,1)S(1)} collective-permute-done((bf16[1,4,1024]{2,1,0:T(4,128)(2,1)S(1)}, bf16[1,4,1024]{2,1,0:T(4,128)(2,1)S(1)}, u32[]{:S(2)}, u32[]{:S(2)}) %collective-permute-start.5) | collective-permute-done | bytes 8224 | tf_op jit(solution)/shard_map/ppermute | solution.py:41
  28.9 1.8 %collective-permute-start.6 = (bf16[2,4,1024]{2,1,0:T(4,128)(2,1)S(1)}, bf16[2,4,1024]{2,1,0:T(4,128)(2,1)S(1)}, u32[]{:S(2)}, u32[]{:S(2)}) collective-permute-start(bf16[2,4,1024]{2,1,0:T(4,128)(2,1)S(1)} %shard_map.145.own_ref), channel_id=1, source_target_pairs={{0,8},{2,10},{4,12},{6,14},{8,0},{10,2},{12,4},{14,6},{16,24},{18,... | collective-permute-start | bytes 49160 | tf_op jit(solution)/shard_map/ppermute | solution.py:41
  30.7 1.9 %collective-permute-done.6.other_ref = bf16[2,4,1024]{2,1,0:T(4,128)(2,1)S(1)} collective-permute-done((bf16[2,4,1024]{2,1,0:T(4,128)(2,1)S(1)}, bf16[2,4,1024]{2,1,0:T(4,128)(2,1)S(1)}, u32[]{:S(2)}, u32[]{:S(2)}) %collective-permute-start.6) | collective-permute-done | bytes 16416 | tf_op jit(solution)/shard_map/ppermute | solution.py:41
  32.7 1.9 %collective-permute-start.7 = (bf16[4,4,1024]{2,1,0:T(4,128)(2,1)S(1)}, bf16[4,4,1024]{2,1,0:T(4,128)(2,1)S(1)}, u32[]{:S(2)}, u32[]{:S(2)}) collective-permute-start(bf16[4,4,1024]{2,1,0:T(4,128)(2,1)S(1)} %shard_map.146.own_ref), channel_id=1, source_target_pairs={{0,4},{2,6},{4,0},{6,2},{8,12},{10,14},{12,8},{14,10},{16,20},{18,... | collective-permute-start | bytes 98312 | tf_op jit(solution)/shard_map/ppermute | solution.py:41
  34.5 2.1 %collective-permute-done.7.other_ref = bf16[4,4,1024]{2,1,0:T(4,128)(2,1)S(1)} collective-permute-done((bf16[4,4,1024]{2,1,0:T(4,128)(2,1)S(1)}, bf16[4,4,1024]{2,1,0:T(4,128)(2,1)S(1)}, u32[]{:S(2)}, u32[]{:S(2)}) %collective-permute-start.7) | collective-permute-done | bytes 32800 | tf_op jit(solution)/shard_map/ppermute | solution.py:41
  36.6 0.0 collective-permute-start.8
  36.6 0.0 copy-done.3
  36.6 1.2 %collective-permute-done.8.far_ref = bf16[8,4,1024]{2,1,0:T(4,128)(2,1)S(1)} collective-permute-done((bf16[8,4,1024]{2,1,0:T(4,128)(2,1)S(1)}, bf16[8,4,1024]{2,1,0:T(4,128)(2,1)S(1)}, u32[]{:S(2)}, u32[]{:S(2)}) %collective-permute-start.8) | collective-permute-done | bytes 65568 | tf_op jit(solution)/shard_map/ppermute | solution.py:41
  37.8 0.0 copy-done.1
  37.8 0.7 %shard_map.148 = bf16[4,1024]{1,0:T(4,128)(2,1)} custom-call(s32[3,4]{1,0:T(4,128)S(1)} %get-tuple-element.17.places_ref, bf16[8,4,1024]{2,1,0:T(4,128)(2,1)S(1)} %shard_map.147.near_ref, bf16[8,4,1024]{2,1,0:T(4,128)(2,1)S(1)} %collective-permute-done.8.far_ref, bf16[4,1024]{1,0:T(4,128)(2,1)S(1)} %copy-done.1, bf16[1,1024]{1,0:T(2,128)(2,1)S(1)} %broadcast_in_dim.40.bias_ref), custom_call_target="tpu_custom_call" | custom-call | tf_op jit(solution)/shard_map/pallas_call | solution.py:235
  (21 shorter events, 0.2 us)
Async XLA Ops:
  1.4 5.9 %collective-permute-start = (bf16[1,4,3072]{2,1,0:T(4,128)(2,1)S(1)}, bf16[1,4,3072]{2,1,0:T(4,128)(2,1)S(1)}, u32[]{:S(2)}, u32[]{:S(2)}) collective-permute-start(bf16[1,4,3072]{2,1,0:T(4,128)(2,1)S(1)} %maximum_bitcast_fusion.own_ref), channel_id=1, source_target_pairs={{0,16},{2,18},{4,20},{6,22},{8,24},{10,26},{12,28},{14,30},{16,0},... | collective-permute-start | bytes 73736 | tf_op jit(solution)/shard_map/ppermute | solution.py:41
  7.3 4.2 %collective-permute-start.1 = (bf16[2,4,3072]{2,1,0:T(4,128)(2,1)S(1)}, bf16[2,4,3072]{2,1,0:T(4,128)(2,1)S(1)}, u32[]{:S(2)}, u32[]{:S(2)}) collective-permute-start(bf16[2,4,3072]{2,1,0:T(4,128)(2,1)S(1)} %shard_map.139.own_ref), channel_id=1, source_target_pairs={{0,8},{2,10},{4,12},{6,14},{8,0},{10,2},{12,4},{14,6},{16,24},{18,... | collective-permute-start | bytes 147464 | tf_op jit(solution)/shard_map/ppermute | solution.py:41
  10.0 3.5 %slice-start.2 = ((s8[6291456]{0:T(1024)(128)(4,1)}), s8[2097152]{0:T(1024)(128)(4,1)S(1)}, s32[]{:S(2)}) async-start(s8[6291456]{0:T(1024)(128)(4,1)} %bitcast.14), calls=%async_computation.2 | async-start | bytes 4194304
  10.0 3.4 %slice-start.3 = ((s8[6291456]{0:T(1024)(128)(4,1)}), s8[4194304]{0:T(1024)(128)(4,1)S(1)}, s32[]{:S(2)}) async-start(s8[6291456]{0:T(1024)(128)(4,1)} %bitcast.14), calls=%async_computation.3 | async-start | bytes 8388608
  11.5 6.2 %slice-start = ((s8[6291456]{0:T(1024)(128)(4,1)}), s8[4194304]{0:T(1024)(128)(4,1)S(1)}, s32[]{:S(2)}) async-start(s8[6291456]{0:T(1024)(128)(4,1)} %bitcast.12), calls=%async_computation | async-start | bytes 8388608
  11.5 6.2 %slice-start.1 = ((s8[6291456]{0:T(1024)(128)(4,1)}), s8[2097152]{0:T(1024)(128)(4,1)S(1)}, s32[]{:S(2)}) async-start(s8[6291456]{0:T(1024)(128)(4,1)} %bitcast.12), calls=%async_computation.1 | async-start | bytes 4194304
  11.5 4.7 %collective-permute-start.2 = (bf16[4,4,3072]{2,1,0:T(4,128)(2,1)S(1)}, bf16[4,4,3072]{2,1,0:T(4,128)(2,1)S(1)}, u32[]{:S(2)}, u32[]{:S(2)}) collective-permute-start(bf16[4,4,3072]{2,1,0:T(4,128)(2,1)S(1)} %shard_map.140.after_ref.own_ref), channel_id=1, source_target_pairs={{0,4},{2,6},{4,0},{6,2},{8,12},{10,14},{12,8},{14,10},{16,20},{18,... | collective-permute-start | bytes 294920 | tf_op jit(solution)/shard_map/ppermute | solution.py:41
  15.4 2.3 %copy-start = (bf16[1024,2048]{1,0:T(8,128)(2,1)S(1)}, bf16[1024,2048]{1,0:T(8,128)(2,1)}, u32[]{:S(2)}) copy-start(bf16[1024,2048]{1,0:T(8,128)(2,1)} %weight_ref.3) | copy-start | bytes 12582916
  15.4 2.3 %copy-start.2 = (s32[4,8]{1,0:T(4,128)S(1)}, s32[4,8]{1,0:T(4,128)}, u32[]{:S(2)}) copy-start(s32[4,8]{1,0:T(4,128)} %table_ref.1) | copy-start | bytes 388
  16.2 1.5 %collective-permute-start.3 = (bf16[8,4,3072]{2,1,0:T(4,128)(2,1)S(1)}, bf16[8,4,3072]{2,1,0:T(4,128)(2,1)S(1)}, u32[]{:S(2)}, u32[]{:S(2)}) collective-permute-start(bf16[8,4,3072]{2,1,0:T(4,128)(2,1)S(1)} %shard_map.142.near_ref), channel_id=1, source_target_pairs={{0,2},{2,0},{4,6},{6,4},{8,10},{10,8},{12,14},{14,12},{16,18},{18,... | collective-permute-start | bytes 589832 | tf_op jit(solution)/shard_map/ppermute | solution.py:41
  17.8 18.9 %copy-start.3 = (bf16[1024]{0:T(1024)(128)(2,1)S(1)}, bf16[1024]{0:T(1024)(128)(2,1)}, u32[]{:S(2)}) copy-start(bf16[1024]{0:T(1024)(128)(2,1)} %param.17) | copy-start | bytes 6148
  17.8 20.1 %copy-start.1 = (bf16[4,1024]{1,0:T(4,128)(2,1)S(1)}, bf16[4,1024]{1,0:T(4,128)(2,1)}, u32[]{:S(2)}) copy-start(bf16[4,1024]{1,0:T(4,128)(2,1)} %residual_ref.1) | copy-start | bytes 24580
  20.6 3.7 %collective-permute-start.4 = (bf16[1,4,1024]{2,1,0:T(4,128)(2,1)S(1)}, bf16[1,4,1024]{2,1,0:T(4,128)(2,1)S(1)}, u32[]{:S(2)}, u32[]{:S(2)}) collective-permute-start(bf16[1,4,1024]{2,1,0:T(4,128)(2,1)S(1)} %get-tuple-element.8), channel_id=1, source_target_pairs={{0,1},{1,0},{2,3},{3,2},{4,5},{5,4},{6,7},{7,6},{8,9},{9,8},{10,11... | collective-permute-start | bytes 24584 | tf_op jit(solution)/shard_map/ppermute | solution.py:78
  24.3 4.6 %collective-permute-start.5 = (bf16[1,4,1024]{2,1,0:T(4,128)(2,1)S(1)}, bf16[1,4,1024]{2,1,0:T(4,128)(2,1)S(1)}, u32[]{:S(2)}, u32[]{:S(2)}) collective-permute-start(bf16[1,4,1024]{2,1,0:T(4,128)(2,1)S(1)} %add_convert_fusion.own_ref), channel_id=1, source_target_pairs={{0,16},{2,18},{4,20},{6,22},{8,24},{10,26},{12,28},{14,30},{16,0},... | collective-permute-start | bytes 24584 | tf_op jit(solution)/shard_map/ppermute | solution.py:41
  28.9 3.7 %collective-permute-start.6 = (bf16[2,4,1024]{2,1,0:T(4,128)(2,1)S(1)}, bf16[2,4,1024]{2,1,0:T(4,128)(2,1)S(1)}, u32[]{:S(2)}, u32[]{:S(2)}) collective-permute-start(bf16[2,4,1024]{2,1,0:T(4,128)(2,1)S(1)} %shard_map.145.own_ref), channel_id=1, source_target_pairs={{0,8},{2,10},{4,12},{6,14},{8,0},{10,2},{12,4},{14,6},{16,24},{18,... | collective-permute-start | bytes 49160 | tf_op jit(solution)/shard_map/ppermute | solution.py:41
  32.7 3.9 %collective-permute-start.7 = (bf16[4,4,1024]{2,1,0:T(4,128)(2,1)S(1)}, bf16[4,4,1024]{2,1,0:T(4,128)(2,1)S(1)}, u32[]{:S(2)}, u32[]{:S(2)}) collective-permute-start(bf16[4,4,1024]{2,1,0:T(4,128)(2,1)S(1)} %shard_map.146.own_ref), channel_id=1, source_target_pairs={{0,4},{2,6},{4,0},{6,2},{8,12},{10,14},{12,8},{14,10},{16,20},{18,... | collective-permute-start | bytes 98312 | tf_op jit(solution)/shard_map/ppermute | solution.py:41
  36.6 1.3 %collective-permute-start.8 = (bf16[8,4,1024]{2,1,0:T(4,128)(2,1)S(1)}, bf16[8,4,1024]{2,1,0:T(4,128)(2,1)S(1)}, u32[]{:S(2)}, u32[]{:S(2)}) collective-permute-start(bf16[8,4,1024]{2,1,0:T(4,128)(2,1)S(1)} %shard_map.147.near_ref), channel_id=1, source_target_pairs={{0,2},{2,0},{4,6},{6,4},{8,10},{10,8},{12,14},{14,12},{16,18},{18,... | collective-permute-start | bytes 196616 | tf_op jit(solution)/shard_map/ppermute | solution.py:41

commit v6 on v5

--- a/solution.py
+++ b/solution.py
@@ -156,7 +156,7 @@
         left_over = jnp.clip(lengths_ref[...] - i * page, 0, page)
         visible = jnp.where((lane == table_ref[:, i:i + 1]) & (left_over > 0), left_over, visible)
 
-    together = min(1, heads)
+    together = min(2, heads)
     rows, lanes = together * slots, together * HS
     row_head = lax.broadcasted_iota(jnp.int32, (rows, lanes), 0) // slots
     lane_head = lax.broadcasted_iota(jnp.int32, (rows, lanes), 1) // HS
@@ -164,26 +164,32 @@
     place = lax.broadcasted_iota(jnp.int32, (rows, page), 1)
     shown = jnp.concatenate([visible] * together, axis=0)
     shown = [place < shown[:, p:p + 1] for p in range(pages)]
-    attended = []
-    for first in range(0, width, lanes):
+    starts = range(0, width, lanes)
+
+    def score(first):
         spread = [jnp.concatenate([x[:, first:first + lanes]] * together, axis=0) for x in (query, key.astype(F32), value)]
         queries = jnp.where(mine, spread[0], 0.0)
         own_score = jnp.sum(queries * spread[1], axis=1, keepdims=True) * scale
-        scores = jnp.dot(queries.astype(BF16), keys_ref[first:first + lanes], preferred_element_type=F32) * scale
+        return jnp.dot(queries.astype(BF16), keys_ref[first:first + lanes], preferred_element_type=F32), own_score, spread[2]
+
+    def soften(scores, own_score, own_value):
         masked = jnp.concatenate(
-            [jnp.where(shown[p], scores[:, p * page:(p + 1) * page], -jnp.inf) for p in range(pages)], axis=1
+            [jnp.where(shown[p], scores[:, p * page:(p + 1) * page] * scale, -jnp.inf) for p in range(pages)], axis=1
         )
         top = jnp.maximum(jnp.max(masked, axis=1, keepdims=True), own_score)
         exps = jnp.exp(masked - top)
         own_exp = jnp.exp(own_score - top)
         total = jnp.sum(exps, axis=1, keepdims=True) + own_exp
-        seen = jnp.dot(
-            exps.astype(BF16),
-            values_ref[:, :, first:first + lanes].reshape(tokens, lanes),
-            preferred_element_type=F32,
-        )
-        seen = jnp.where(mine, (seen + own_exp * spread[2]) * (1.0 / total), 0.0)
-        attended.append(sum(seen[h * slots:(h + 1) * slots] for h in range(together)))
+        return exps.astype(BF16), own_exp * own_value, 1.0 / total
+
+    def gather_values(first, exps, own, share):
+        seen = jnp.dot(exps, values_ref[:, :, first:first + lanes].reshape(tokens, lanes), preferred_element_type=F32)
+        seen = jnp.where(mine, (seen + own) * share, 0.0)
+        return sum(seen[h * slots:(h + 1) * slots] for h in range(together))
+
+    scored = [score(first) for first in starts]
+    softened = [soften(*x) for x in scored]
+    attended = [gather_values(first, *x) for first, x in zip(starts, softened)]
     attended = jnp.concatenate(attended, axis=1).astype(BF16)
 
     attended_out[...] = attended

time: 38.9 us -> 38.4 us (0.987)
  Pallas kernels: 5.94 us -> 5.4 us
    pallas_call x1, Pallas kernels: 2.8 us -> 2.26 us  [on_device(): pl.pallas_call(functools.partial(attend, parts), out_shape=(narrow, jax.S...]
where the time goes in v6:
time: 38.4 us; the launch traced here: 38.1 us
  starting transfers between devices  16.5 us (43%)
  waiting for transfers between devices  11.9 us (31%)
  Pallas kernels  5.4 us (14%)
  other arithmetic  2.39 us (6%)
  local copies, waits for them, and re-layouts  1.1 us (3%)
  between operations  0.82 us (2%)
    ppermute x8, starting transfers between devices, gather_by_doubling(): other = lax.ppermute(held, 'req', [(i, i ^ bit) for i in range(devices)])  14.5 us
    ppermute x8, waiting for transfers between devices, gather_by_doubling(): other = lax.ppermute(held, 'req', [(i, i ^ bit) for i in range(devices)])  10.5 us
    pallas_call x1, Pallas kernels, on_device(): pl.pallas_call(functools.partial(attend, parts), out_shape=(narrow, jax.S...  2.26 us
    ppermute x1, starting transfers between devices, sum_by_halving(): lax.ppermute(sent, 'tp', [(i, i ^ bit) for i in range(parts)]).astype(F32)  1.95 us
    pallas_call x1, Pallas kernels, turned(): pl.pallas_call(turn, out_shape=jax.ShapeDtypeStruct((width, pages * page)...  1.95 us
    ppermute x1, waiting for transfers between devices, sum_by_halving(): lax.ppermute(sent, 'tp', [(i, i ^ bit) for i in range(parts)]).astype(F32)  1.36 us
  transfers between devices with their start and end apart: 9, of which 8 were waited for; matrix products, arithmetic and copies ran while one was open for 7% of the time, Pallas kernels for 6%

profile of v6, /device:TPU:0, one launch (start us, length us, event | category | flops | bytes accessed | tf_op | source)
XLA Modules:
  0.0 38.1 jit_solution(17430075176652507625)
XLA Ops:
  0.6 0.7 %maximum_bitcast_fusion.own_ref = bf16[1,4,3072]{2,1,0:T(4,128)(2,1)S(1)} fusion(bf16[4,1024]{1,0:T(4,128)(2,1)} %param.14, bf16[4,1024]{1,0:T(4,128)(2,1)} %param.13, bf16[4,1024]{1,0:T(4,128)(2,1)} %param.12), kind=kLoop, calls=%fused_computation.1 | loop fusion | flops 73728 | bytes 49152 | tf_op jit(solution)/shard_map/broadcast_in_dim | solution.py:37
  1.4 4.1 %collective-permute-start = (bf16[1,4,3072]{2,1,0:T(4,128)(2,1)S(1)}, bf16[1,4,3072]{2,1,0:T(4,128)(2,1)S(1)}, u32[]{:S(2)}, u32[]{:S(2)}) collective-permute-start(bf16[1,4,3072]{2,1,0:T(4,128)(2,1)S(1)} %maximum_bitcast_fusion.own_ref), channel_id=1, source_target_pairs={{0,16},{2,18},{4,20},{6,22},{8,24},{10,26},{12,28},{14,30},{16,0},... | collective-permute-start | bytes 73736 | tf_op jit(solution)/shard_map/ppermute | solution.py:41
  5.5 0.7 %convert_element_type.10 = f32[4]{0:T(128)S(1)} convert(s32[4]{0:T(128)} %param.21) | non-fusion elementwise | flops 4 | bytes 32 | tf_op jit(solution)/shard_map/convert_element_type | solution.py:89
  6.2 0.1 pad.11.clone
  6.2 0.1 pad.8.clone
  6.3 0.1 multiply_cosine_fusion
  6.4 0.1 maximum_maximum_fusion.1
  6.5 0.7 %fusion.8 = (s32[1,4]{1,0:T(1,128)S(1)}, s32[1,4]{1,0:T(1,128)S(1)}, s32[1,4]{1,0:T(1,128)S(1)}, s32[1,4]{1,0:T(1,128)S(1)}) fusion(s32[4]{0:T(128)} %param.23, s32[]{:T(128)S(6)} %axis_index.15, s32[4]{0:T(128)} %param.22), kind=kLoop, calls=%fused_computation.37 | loop fusion | flops 280 | bytes 100 | tf_op jit(solution)/shard_map/stack | solution.py:58
  7.3 0.0 collective-permute-done.other_ref
  7.3 1.9 %collective-permute-start.1 = (bf16[2,4,3072]{2,1,0:T(4,128)(2,1)S(1)}, bf16[2,4,3072]{2,1,0:T(4,128)(2,1)S(1)}, u32[]{:S(2)}, u32[]{:S(2)}) collective-permute-start(bf16[2,4,3072]{2,1,0:T(4,128)(2,1)S(1)} %shard_map.139.own_ref), channel_id=1, source_target_pairs={{0,8},{2,10},{4,12},{6,14},{8,0},{10,2},{12,4},{14,6},{16,24},{18,... | collective-permute-start | bytes 147464 | tf_op jit(solution)/shard_map/ppermute | solution.py:41
  9.2 0.7 %copy.15.lengths_ref = s32[4,1]{1,0:T(4,128)S(1)} copy(s32[4,1]{0,1:T(1,128)} %bitcast.16) | data formatting | bytes 32 | tf_op jit(solution)/shard_map/broadcast_in_dim | solution.py:231
  10.0 0.0 slice-start.2
  10.0 0.1 pad.20.clone
  10.0 0.0 slice-start.3
  10.0 1.5 %collective-permute-done.1.other_ref = bf16[2,4,3072]{2,1,0:T(4,128)(2,1)S(1)} collective-permute-done((bf16[2,4,3072]{2,1,0:T(4,128)(2,1)S(1)}, bf16[2,4,3072]{2,1,0:T(4,128)(2,1)S(1)}, u32[]{:S(2)}, u32[]{:S(2)}) %collective-permute-start.1) | collective-permute-done | bytes 49184 | tf_op jit(solution)/shard_map/ppermute | solution.py:41
  11.5 0.0 slice-start
  11.5 0.0 slice-start.1
  11.5 1.9 %collective-permute-start.2 = (bf16[4,4,3072]{2,1,0:T(4,128)(2,1)S(1)}, bf16[4,4,3072]{2,1,0:T(4,128)(2,1)S(1)}, u32[]{:S(2)}, u32[]{:S(2)}) collective-permute-start(bf16[4,4,3072]{2,1,0:T(4,128)(2,1)S(1)} %shard_map.140.after_ref.own_ref), channel_id=1, source_target_pairs={{0,4},{2,6},{4,0},{6,2},{8,12},{10,14},{12,8},{14,10},{16,20},{18,... | collective-permute-start | bytes 294920 | tf_op jit(solution)/shard_map/ppermute | solution.py:41
  13.4 0.0 slice-done.2
  13.4 0.0 slice-done.3
  13.4 1.9 %shard_map.141.rest_0_.keys_ref = bf16[1024,3072]{1,0:T(8,128)(2,1)S(1)} custom-call(bf16[24,128,1024]{2,1,0:T(8,128)(2,1)S(1)} %bitcast.15, bf16[4,4,3072]{2,1,0:T(4,128)(2,1)S(1)} %shard_map.140.after_ref.own_ref), custom_call_target="tpu_custom_call" | custom-call | flops 4294967296 | bytes 1048576 | tf_op jit(solution)/shard_map/pallas_call | solution.py:108
  15.4 0.0 copy-start
  15.4 0.0 copy-start.2
  15.4 0.8 %collective-permute-done.2.other_ref = bf16[4,4,3072]{2,1,0:T(4,128)(2,1)S(1)} collective-permute-done((bf16[4,4,3072]{2,1,0:T(4,128)(2,1)S(1)}, bf16[4,4,3072]{2,1,0:T(4,128)(2,1)S(1)}, u32[]{:S(2)}, u32[]{:S(2)}) %collective-permute-start.2) | collective-permute-done | bytes 98336 | tf_op jit(solution)/shard_map/ppermute | solution.py:41
  16.2 0.1 collective-permute-start.3
  16.3 0.1 add_add_fusion.1
  16.4 1.4 %collective-permute-done.3.far_ref = bf16[8,4,3072]{2,1,0:T(4,128)(2,1)S(1)} collective-permute-done((bf16[8,4,3072]{2,1,0:T(4,128)(2,1)S(1)}, bf16[8,4,3072]{2,1,0:T(4,128)(2,1)S(1)}, u32[]{:S(2)}, u32[]{:S(2)}) %collective-permute-start.3) | collective-permute-done | bytes 196640 | tf_op jit(solution)/shard_map/ppermute | solution.py:41
  17.7 0.0 slice-done
  17.7 0.0 slice-done.1
  17.7 0.0 copy-done
  17.7 0.0 copy-done.2
  17.8 0.0 copy-start.3
  17.8 0.0 copy-start.1
  17.8 2.3 %shard_map.143 = (bf16[4,1024]{1,0:T(4,128)(2,1)S(1)}, bf16[1,4,1024]{2,1,0:T(4,128)(2,1)S(1)}, bf16[4,1024]{1,0:T(4,128)(2,1)}, bf16[4,1024]{1,0:T(4,128)(2,1)}) custom-call(s32[3,4]{1,0:T(4,128)S(1)} %get-tuple-element.16.places_ref, bf16[8,4,3072]{2,1,0:T(4,128)(2,1)S(1)} %shard_map.142.near_ref, bf16[8,4,3072]{2,1,0:T(4,128)(2,1)S(1)} %collective-permute-done.3.far_ref, ...), custom_call_target="tpu_custom_call" | custom-call | tf_op jit(solution)/shard_map/pallas_call | solution.py:220
  20.0 1.9 %collective-permute-start.4 = (bf16[1,4,1024]{2,1,0:T(4,128)(2,1)S(1)}, bf16[1,4,1024]{2,1,0:T(4,128)(2,1)S(1)}, u32[]{:S(2)}, u32[]{:S(2)}) collective-permute-start(bf16[1,4,1024]{2,1,0:T(4,128)(2,1)S(1)} %get-tuple-element.8), channel_id=1, source_target_pairs={{0,1},{1,0},{2,3},{3,2},{4,5},{5,4},{6,7},{7,6},{8,9},{9,8},{10,11... | collective-permute-start | bytes 24584 | tf_op jit(solution)/shard_map/ppermute | solution.py:78
  22.0 0.4 %shard_map.144 = f32[1,4,1024]{2,1,0:T(4,128)S(1)} custom-call(s32[3,4]{1,0:T(4,128)S(1)} %get-tuple-element.16.places_ref, bf16[4,1024]{1,0:T(4,128)(2,1)S(1)} %get-tuple-element.7.attended_ref, bf16[1024,2048]{1,0:T(8,128)(2,1)S(1)} %copy-done), custom_call_target="tpu_custom_call" | custom-call | flops 1073741824 | bytes 1048576 | tf_op jit(solution)/shard_map/pallas_call | solution.py:232
  22.4 1.4 %collective-permute-done.4 = bf16[1,4,1024]{2,1,0:T(4,128)(2,1)S(1)} collective-permute-done((bf16[1,4,1024]{2,1,0:T(4,128)(2,1)S(1)}, bf16[1,4,1024]{2,1,0:T(4,128)(2,1)S(1)}, u32[]{:S(2)}, u32[]{:S(2)}) %collective-permute-start.4) | collective-permute-done | bytes 8224 | tf_op jit(solution)/shard_map/ppermute | solution.py:78
  23.8 2.9 %collective-permute-start.5 = (bf16[1,4,1024]{2,1,0:T(4,128)(2,1)S(1)}, bf16[1,4,1024]{2,1,0:T(4,128)(2,1)S(1)}, u32[]{:S(2)}, u32[]{:S(2)}) collective-permute-start(bf16[1,4,1024]{2,1,0:T(4,128)(2,1)S(1)} %add_convert_fusion.own_ref), channel_id=1, source_target_pairs={{0,16},{2,18},{4,20},{6,22},{8,24},{10,26},{12,28},{14,30},{16,0},... | collective-permute-start | bytes 24584 | tf_op jit(solution)/shard_map/ppermute | solution.py:41
  26.7 1.7 %collective-permute-done.5.other_ref = bf16[1,4,1024]{2,1,0:T(4,128)(2,1)S(1)} collective-permute-done((bf16[1,4,1024]{2,1,0:T(4,128)(2,1)S(1)}, bf16[1,4,1024]{2,1,0:T(4,128)(2,1)S(1)}, u32[]{:S(2)}, u32[]{:S(2)}) %collective-permute-start.5) | collective-permute-done | bytes 8224 | tf_op jit(solution)/shard_map/ppermute | solution.py:41
  28.4 1.8 %collective-permute-start.6 = (bf16[2,4,1024]{2,1,0:T(4,128)(2,1)S(1)}, bf16[2,4,1024]{2,1,0:T(4,128)(2,1)S(1)}, u32[]{:S(2)}, u32[]{:S(2)}) collective-permute-start(bf16[2,4,1024]{2,1,0:T(4,128)(2,1)S(1)} %shard_map.145.own_ref), channel_id=1, source_target_pairs={{0,8},{2,10},{4,12},{6,14},{8,0},{10,2},{12,4},{14,6},{16,24},{18,... | collective-permute-start | bytes 49160 | tf_op jit(solution)/shard_map/ppermute | solution.py:41
  30.2 1.9 %collective-permute-done.6.other_ref = bf16[2,4,1024]{2,1,0:T(4,128)(2,1)S(1)} collective-permute-done((bf16[2,4,1024]{2,1,0:T(4,128)(2,1)S(1)}, bf16[2,4,1024]{2,1,0:T(4,128)(2,1)S(1)}, u32[]{:S(2)}, u32[]{:S(2)}) %collective-permute-start.6) | collective-permute-done | bytes 16416 | tf_op jit(solution)/shard_map/ppermute | solution.py:41
  32.1 1.9 %collective-permute-start.7 = (bf16[4,4,1024]{2,1,0:T(4,128)(2,1)S(1)}, bf16[4,4,1024]{2,1,0:T(4,128)(2,1)S(1)}, u32[]{:S(2)}, u32[]{:S(2)}) collective-permute-start(bf16[4,4,1024]{2,1,0:T(4,128)(2,1)S(1)} %shard_map.146.own_ref), channel_id=1, source_target_pairs={{0,4},{2,6},{4,0},{6,2},{8,12},{10,14},{12,8},{14,10},{16,20},{18,... | collective-permute-start | bytes 98312 | tf_op jit(solution)/shard_map/ppermute | solution.py:41
  34.0 2.1 %collective-permute-done.7.other_ref = bf16[4,4,1024]{2,1,0:T(4,128)(2,1)S(1)} collective-permute-done((bf16[4,4,1024]{2,1,0:T(4,128)(2,1)S(1)}, bf16[4,4,1024]{2,1,0:T(4,128)(2,1)S(1)}, u32[]{:S(2)}, u32[]{:S(2)}) %collective-permute-start.7) | collective-permute-done | bytes 32800 | tf_op jit(solution)/shard_map/ppermute | solution.py:41
  36.1 0.0 collective-permute-start.8
  36.1 0.0 copy-done.3
  36.1 1.2 %collective-permute-done.8.far_ref = bf16[8,4,1024]{2,1,0:T(4,128)(2,1)S(1)} collective-permute-done((bf16[8,4,1024]{2,1,0:T(4,128)(2,1)S(1)}, bf16[8,4,1024]{2,1,0:T(4,128)(2,1)S(1)}, u32[]{:S(2)}, u32[]{:S(2)}) %collective-permute-start.8) | collective-permute-done | bytes 65568 | tf_op jit(solution)/shard_map/ppermute | solution.py:41
  37.3 0.0 copy-done.1
  37.3 0.7 %shard_map.148 = bf16[4,1024]{1,0:T(4,128)(2,1)} custom-call(s32[3,4]{1,0:T(4,128)S(1)} %get-tuple-element.17.places_ref, bf16[8,4,1024]{2,1,0:T(4,128)(2,1)S(1)} %shard_map.147.near_ref, bf16[8,4,1024]{2,1,0:T(4,128)(2,1)S(1)} %collective-permute-done.8.far_ref, bf16[4,1024]{1,0:T(4,128)(2,1)S(1)} %copy-done.1, bf16[1,1024]{1,0:T(2,128)(2,1)S(1)} %broadcast_in_dim.40.bias_ref), custom_call_target="tpu_custom_call" | custom-call | tf_op jit(solution)/shard_map/pallas_call | solution.py:241
  (21 shorter events, 0.2 us)
Async XLA Ops:
  1.4 5.9 %collective-permute-start = (bf16[1,4,3072]{2,1,0:T(4,128)(2,1)S(1)}, bf16[1,4,3072]{2,1,0:T(4,128)(2,1)S(1)}, u32[]{:S(2)}, u32[]{:S(2)}) collective-permute-start(bf16[1,4,3072]{2,1,0:T(4,128)(2,1)S(1)} %maximum_bitcast_fusion.own_ref), channel_id=1, source_target_pairs={{0,16},{2,18},{4,20},{6,22},{8,24},{10,26},{12,28},{14,30},{16,0},... | collective-permute-start | bytes 73736 | tf_op jit(solution)/shard_map/ppermute | solution.py:41
  7.3 4.2 %collective-permute-start.1 = (bf16[2,4,3072]{2,1,0:T(4,128)(2,1)S(1)}, bf16[2,4,3072]{2,1,0:T(4,128)(2,1)S(1)}, u32[]{:S(2)}, u32[]{:S(2)}) collective-permute-start(bf16[2,4,3072]{2,1,0:T(4,128)(2,1)S(1)} %shard_map.139.own_ref), channel_id=1, source_target_pairs={{0,8},{2,10},{4,12},{6,14},{8,0},{10,2},{12,4},{14,6},{16,24},{18,... | collective-permute-start | bytes 147464 | tf_op jit(solution)/shard_map/ppermute | solution.py:41
  10.0 3.5 %slice-start.2 = ((s8[6291456]{0:T(1024)(128)(4,1)}), s8[2097152]{0:T(1024)(128)(4,1)S(1)}, s32[]{:S(2)}) async-start(s8[6291456]{0:T(1024)(128)(4,1)} %bitcast.14), calls=%async_computation.2 | async-start | bytes 4194304
  10.0 3.4 %slice-start.3 = ((s8[6291456]{0:T(1024)(128)(4,1)}), s8[4194304]{0:T(1024)(128)(4,1)S(1)}, s32[]{:S(2)}) async-start(s8[6291456]{0:T(1024)(128)(4,1)} %bitcast.14), calls=%async_computation.3 | async-start | bytes 8388608
  11.5 6.2 %slice-start = ((s8[6291456]{0:T(1024)(128)(4,1)}), s8[4194304]{0:T(1024)(128)(4,1)S(1)}, s32[]{:S(2)}) async-start(s8[6291456]{0:T(1024)(128)(4,1)} %bitcast.12), calls=%async_computation | async-start | bytes 8388608
  11.5 6.2 %slice-start.1 = ((s8[6291456]{0:T(1024)(128)(4,1)}), s8[2097152]{0:T(1024)(128)(4,1)S(1)}, s32[]{:S(2)}) async-start(s8[6291456]{0:T(1024)(128)(4,1)} %bitcast.12), calls=%async_computation.1 | async-start | bytes 4194304
  11.5 4.7 %collective-permute-start.2 = (bf16[4,4,3072]{2,1,0:T(4,128)(2,1)S(1)}, bf16[4,4,3072]{2,1,0:T(4,128)(2,1)S(1)}, u32[]{:S(2)}, u32[]{:S(2)}) collective-permute-start(bf16[4,4,3072]{2,1,0:T(4,128)(2,1)S(1)} %shard_map.140.after_ref.own_ref), channel_id=1, source_target_pairs={{0,4},{2,6},{4,0},{6,2},{8,12},{10,14},{12,8},{14,10},{16,20},{18,... | collective-permute-start | bytes 294920 | tf_op jit(solution)/shard_map/ppermute | solution.py:41
  15.4 2.3 %copy-start = (bf16[1024,2048]{1,0:T(8,128)(2,1)S(1)}, bf16[1024,2048]{1,0:T(8,128)(2,1)}, u32[]{:S(2)}) copy-start(bf16[1024,2048]{1,0:T(8,128)(2,1)} %weight_ref.3) | copy-start | bytes 12582916
  15.4 2.3 %copy-start.2 = (s32[4,8]{1,0:T(4,128)S(1)}, s32[4,8]{1,0:T(4,128)}, u32[]{:S(2)}) copy-start(s32[4,8]{1,0:T(4,128)} %table_ref.1) | copy-start | bytes 388
  16.2 1.5 %collective-permute-start.3 = (bf16[8,4,3072]{2,1,0:T(4,128)(2,1)S(1)}, bf16[8,4,3072]{2,1,0:T(4,128)(2,1)S(1)}, u32[]{:S(2)}, u32[]{:S(2)}) collective-permute-start(bf16[8,4,3072]{2,1,0:T(4,128)(2,1)S(1)} %shard_map.142.near_ref), channel_id=1, source_target_pairs={{0,2},{2,0},{4,6},{6,4},{8,10},{10,8},{12,14},{14,12},{16,18},{18,... | collective-permute-start | bytes 589832 | tf_op jit(solution)/shard_map/ppermute | solution.py:41
  17.8 18.3 %copy-start.3 = (bf16[1024]{0:T(1024)(128)(2,1)S(1)}, bf16[1024]{0:T(1024)(128)(2,1)}, u32[]{:S(2)}) copy-start(bf16[1024]{0:T(1024)(128)(2,1)} %param.17) | copy-start | bytes 6148
  17.8 19.5 %copy-start.1 = (bf16[4,1024]{1,0:T(4,128)(2,1)S(1)}, bf16[4,1024]{1,0:T(4,128)(2,1)}, u32[]{:S(2)}) copy-start(bf16[4,1024]{1,0:T(4,128)(2,1)} %residual_ref.1) | copy-start | bytes 24580
  20.0 3.7 %collective-permute-start.4 = (bf16[1,4,1024]{2,1,0:T(4,128)(2,1)S(1)}, bf16[1,4,1024]{2,1,0:T(4,128)(2,1)S(1)}, u32[]{:S(2)}, u32[]{:S(2)}) collective-permute-start(bf16[1,4,1024]{2,1,0:T(4,128)(2,1)S(1)} %get-tuple-element.8), channel_id=1, source_target_pairs={{0,1},{1,0},{2,3},{3,2},{4,5},{5,4},{6,7},{7,6},{8,9},{9,8},{10,11... | collective-permute-start | bytes 24584 | tf_op jit(solution)/shard_map/ppermute | solution.py:78
  23.8 4.6 %collective-permute-start.5 = (bf16[1,4,1024]{2,1,0:T(4,128)(2,1)S(1)}, bf16[1,4,1024]{2,1,0:T(4,128)(2,1)S(1)}, u32[]{:S(2)}, u32[]{:S(2)}) collective-permute-start(bf16[1,4,1024]{2,1,0:T(4,128)(2,1)S(1)} %add_convert_fusion.own_ref), channel_id=1, source_target_pairs={{0,16},{2,18},{4,20},{6,22},{8,24},{10,26},{12,28},{14,30},{16,0},... | collective-permute-start | bytes 24584 | tf_op jit(solution)/shard_map/ppermute | solution.py:41
  28.4 3.7 %collective-permute-start.6 = (bf16[2,4,1024]{2,1,0:T(4,128)(2,1)S(1)}, bf16[2,4,1024]{2,1,0:T(4,128)(2,1)S(1)}, u32[]{:S(2)}, u32[]{:S(2)}) collective-permute-start(bf16[2,4,1024]{2,1,0:T(4,128)(2,1)S(1)} %shard_map.145.own_ref), channel_id=1, source_target_pairs={{0,8},{2,10},{4,12},{6,14},{8,0},{10,2},{12,4},{14,6},{16,24},{18,... | collective-permute-start | bytes 49160 | tf_op jit(solution)/shard_map/ppermute | solution.py:41
  32.1 3.9 %collective-permute-start.7 = (bf16[4,4,1024]{2,1,0:T(4,128)(2,1)S(1)}, bf16[4,4,1024]{2,1,0:T(4,128)(2,1)S(1)}, u32[]{:S(2)}, u32[]{:S(2)}) collective-permute-start(bf16[4,4,1024]{2,1,0:T(4,128)(2,1)S(1)} %shard_map.146.own_ref), channel_id=1, source_target_pairs={{0,4},{2,6},{4,0},{6,2},{8,12},{10,14},{12,8},{14,10},{16,20},{18,... | collective-permute-start | bytes 98312 | tf_op jit(solution)/shard_map/ppermute | solution.py:41
  36.1 1.3 %collective-permute-start.8 = (bf16[8,4,1024]{2,1,0:T(4,128)(2,1)S(1)}, bf16[8,4,1024]{2,1,0:T(4,128)(2,1)S(1)}, u32[]{:S(2)}, u32[]{:S(2)}) collective-permute-start(bf16[8,4,1024]{2,1,0:T(4,128)(2,1)S(1)} %shard_map.147.near_ref), channel_id=1, source_target_pairs={{0,2},{2,0},{4,6},{6,4},{8,10},{10,8},{12,14},{14,12},{16,18},{18,... | collective-permute-start | bytes 196616 | tf_op jit(solution)/shard_map/ppermute | solution.py:41

commit v7 on v6

--- a/solution.py
+++ b/solution.py
@@ -8,7 +8,8 @@
 from jax.sharding import PartitionSpec as P
 
 HS = 256
-TURN = 4<<30
+CORES = 2
+TURN = 4 << 30
 BF16 = jnp.bfloat16
 F32 = jnp.float32
 ANY = pl.BlockSpec(memory_space=pl.ANY)
@@ -33,16 +34,16 @@
     )(own, other, *first)
 
 
-def gather_by_doubling(block, devices, works, beside=None):
+def gather_by_doubling(block, devices, works, beside):
     held = block[None]
     bit = devices // 2
-    extra = ()
+    results = ()
     while True:
         other = lax.ppermute(held, "req", [(i, i ^ bit) for i in range(devices)])
         if bit == 1:
-            return (held, other) + extra
-        if bit == 2 and beside is not None:
-            extra = (beside(held),)
+            return (held, other) + results
+        extra = beside[bit](held) if bit in beside else ()
+        results += extra
         held = join(held, other, works.pop(0) if works else 0, *extra)
         bit //= 2
 
@@ -55,7 +56,7 @@
         place = place + jnp.where((apart & bit) != 0, weight, 0)
         bit //= 2
         weight *= 2
-    return jnp.stack([place, rows % per, jnp.full_like(rows, lax.axis_index("tp"))])
+    return jnp.stack([place, rows % per])
 
 
 def take_rows(places_ref, near_ref, far_ref):
@@ -70,16 +71,6 @@
         block = jnp.where(place < count, near, far)
         taken.append(jnp.sum(jnp.where(rows == row, block, 0.0), axis=0, keepdims=True))
     return jnp.concatenate(taken, axis=0)
-
-
-def sum_by_halving(kept, sent, parts):
-    bit = parts // 2
-    while True:
-        kept = kept + lax.ppermute(sent, "tp", [(i, i ^ bit) for i in range(parts)]).astype(F32)
-        if bit == 1:
-            return kept[0]
-        bit //= 2
-        kept, sent = kept[:bit], kept[bit:].astype(BF16)
 
 
 def rotary_factors(lengths, heads):
@@ -115,16 +106,9 @@
     )(pool, after)
 
 
-def project(attended, weight_ref, part):
-    width = attended.shape[1]
-    columns = pl.ds(pl.multiple_of(part * width, width), width)
-    return jnp.dot(attended, weight_ref[:, columns], preferred_element_type=F32)
-
-
-def attend(parts, places_ref, near_ref, far_ref, factors_ref, table_ref, lengths_ref,
-           keys_ref, values_ref, weight_ref, attended_out, sent_out, keys_out, values_out,
+def attend(devices, parts, places_ref, near_ref, far_ref, factors_ref, table_ref, lengths_ref,
+           keys_ref, values_ref, weight_ref, where_ref, sent_out, keys_out, values_out,
            key_ref, value_ref, sems):
-    half = places_ref[...][2, 0]
     slots, width = key_ref.shape
     heads = width // HS
     pages, page = values_ref.shape[0], values_ref.shape[1]
@@ -192,21 +176,34 @@
     attended = [gather_values(first, *x) for first, x in zip(starts, softened)]
     attended = jnp.concatenate(attended, axis=1).astype(BF16)
 
-    attended_out[...] = attended
-    for i in range(parts // 2):
-        sent_out[i] = project(attended, weight_ref, half ^ (parts // 2 + i)).astype(BF16)
+    for part in range(parts):
+        columns = weight_ref[:, part * width:(part + 1) * width]
+        terms = jnp.dot(attended, columns, preferred_element_type=F32).astype(BF16)
+        for device in range(devices):
+            first = device % CORES * (width // CORES)
+            sent_out[device * parts + part] = terms[:, first:first + width // CORES]
     for copy in copies:
         copy.wait()
 
 
-def keep(parts, places_ref, attended_ref, weight_ref, kept_out):
-    for i in range(parts // 2):
-        kept_out[i] = project(attended_ref[...], weight_ref, places_ref[...][2, 0] ^ i)
-
-
-def finish(places_ref, near_ref, far_ref, residual_ref, bias_ref, out_ref):
-    taken = take_rows(places_ref, near_ref, far_ref)
-    out_ref[...] = (residual_ref[...].astype(F32) + bias_ref[...].astype(F32) + taken).astype(BF16)
+def sort(parts, where_ref, terms_ref, mine_out, theirs_out):
+    rows, lanes = mine_out.shape
+    table = where_ref[...]
+    row = lax.broadcasted_iota(jnp.int32, (rows, lanes), 0)
+    taken = []
+    for i in range(CORES * rows):
+        first = table[0, i] * parts
+        block = sum(terms_ref[first + part].astype(F32) for part in range(parts))
+        taken.append(jnp.sum(jnp.where(row == table[1, i], block, 0.0), axis=0, keepdims=True))
+    mine_out[...] = jnp.concatenate(taken[:rows], axis=0).astype(BF16)
+    theirs_out[...] = jnp.concatenate(taken[rows:], axis=0).astype(BF16)
+
+
+def finish(where_ref, mine_ref, other_ref, residual_ref, bias_ref, out_ref):
+    first = where_ref[...][2, 0] == 0
+    mine, other = mine_ref[...].astype(F32), other_ref[...].astype(F32)
+    taken = jnp.concatenate([jnp.where(first, mine, other), jnp.where(first, other, mine)], axis=1)
+    out_ref[...] = (residual_ref[...].astype(F32) + bias_ref[...].astype(F32)[None, :] + taken).astype(BF16)
 
 
 def on_device(devices, parts, query_new, key_new, value_new, residual, dense_weight, dense_bias,
@@ -214,37 +211,52 @@
     rows, width = query_new.shape
     heads = width // HS
     fresh = jnp.concatenate([query_new, key_new, value_new], axis=1)
-    near, far, keys = gather_by_doubling(fresh, devices, [0,6<<30,2<<30], functools.partial(turned, key_pool))
+    other_core = [(i, i ^ 1) for i in range(devices)]
+
+    def integers(after):
+        slots, long, _ = lax.optimization_barrier((request_slot, lengths, after))
+        return lax.ppermute(slots, "req", other_core), long[:, None]
+
+    def keys_turned(after):
+        return (turned(key_pool, after),)
+
+    near, far, slots, column, keys = gather_by_doubling(
+        fresh, devices, [0, 3 << 30, 2 << 30], {4: integers, 2: keys_turned}
+    )
     narrow = jax.ShapeDtypeStruct((rows, width), BF16)
-    where = places(arrival_index, rows, devices)
-    attended, sent, appended_keys, appended_values = pl.pallas_call(
-        functools.partial(attend, parts),
-        out_shape=(narrow, jax.ShapeDtypeStruct((parts // 2, rows, width), BF16), narrow, narrow),
-        in_specs=[VMEM] * 9,
-        out_specs=(VMEM, VMEM, ANY, ANY),
+    half = jax.ShapeDtypeStruct((rows, width // CORES), BF16)
+    own_slots, slots, _ = lax.optimization_barrier((request_slot, slots, near))
+    slots = jnp.concatenate([own_slots, slots])
+    core = lax.axis_index("req").astype(jnp.int32) % CORES
+    where = jnp.stack([slots // rows, slots % rows, jnp.full_like(slots, core)])
+    sent, appended_keys, appended_values = pl.pallas_call(
+        functools.partial(attend, devices, parts),
+        out_shape=(jax.ShapeDtypeStruct((devices * parts,) + half.shape, BF16), narrow, narrow),
+        in_specs=[VMEM] * 9 + [ANY],
+        out_specs=(VMEM, ANY, ANY),
         scratch_shapes=[
             pltpu.VMEM((rows, width), BF16),
             pltpu.VMEM((rows, width), BF16),
             pltpu.SemaphoreType.DMA((2,)),
         ],
         compiler_params=pltpu.CompilerParams(vmem_limit_bytes=8 << 20),
-    )(where, near, far, rotary_factors(lengths, heads), page_table, lengths[:, None], keys, value_pool, dense_weight)
-    kept = pl.pallas_call(
-        functools.partial(keep, parts),
-        out_shape=jax.ShapeDtypeStruct((parts // 2, rows, width), F32),
-        in_specs=[VMEM] * 3,
-        out_specs=VMEM,
-        cost_estimate=pl.CostEstimate(flops=1 << 30, bytes_accessed=1 << 20, transcendentals=0),
-        compiler_params=pltpu.CompilerParams(vmem_limit_bytes=8 << 20),
-    )(where, attended, dense_weight)
-    near, far = gather_by_doubling(sum_by_halving(kept, sent, parts).astype(BF16), devices, [])
+    )(places(arrival_index, rows, devices), near, far, rotary_factors(lengths, heads), page_table, column,
+      keys, value_pool, dense_weight, where)
+    terms = lax.all_to_all(sent, ("req", "tp"), 0, 0, tiled=True)
+    mine, theirs = pl.pallas_call(
+        functools.partial(sort, parts),
+        out_shape=(half, half),
+        in_specs=[VMEM] * 2,
+        out_specs=(VMEM, VMEM),
+        compiler_params=pltpu.CompilerParams(vmem_limit_bytes=2 << 20),
+    )(where, terms)
     hidden = pl.pallas_call(
         finish,
         out_shape=narrow,
         in_specs=[VMEM] * 5,
         out_specs=VMEM,
         compiler_params=pltpu.CompilerParams(vmem_limit_bytes=2 << 20),
-    )(places(request_slot, rows, devices), near, far, residual, dense_bias[None, :])
+    )(where, mine, lax.ppermute(theirs, "req", other_core), residual, dense_bias)
     return hidden, appended_keys, appended_values
 
 

time: 38.4 us -> 37.8 us (0.984)
  blocking collectives: 0 us -> 14.6 us
  starting transfers between devices: 16.5 us -> 8.04 us
  waiting for transfers between devices: 11.9 us -> 4.72 us
    all_to_all x0 -> x1, blocking collectives: none -> 14.6 us  [on_device(): terms = lax.all_to_all(sent, ('req', 'tp'), 0, 0, tiled=True)]
    ppermute x8 -> x4, waiting for transfers between devices: 10.5 us -> 2.31 us  [gather_by_doubling(): other = lax.ppermute(held, 'req', [(i, i ^ bit) for i in range(devices)])]
    ppermute x8 -> x4, starting transfers between devices: 14.5 us -> 7.97 us  [gather_by_doubling(): other = lax.ppermute(held, 'req', [(i, i ^ bit) for i in range(devices)])]
    ppermute x1 -> x2, starting transfers between devices: 1.95 us -> 0.07 us  [the longest x1 0.07 us: on_device(): lax.ppermute(theirs, 'req', other_core)]
    ppermute x1 -> x2, waiting for transfers between devices: 1.36 us -> 2.41 us  [the longest x1 1.25 us: integers(): return (lax.ppermute(slots, 'req', other_core), long[:, None])]
    pallas_call x2, Pallas kernels: 2.67 us -> 3.15 us  [the longest x1 3 us: on_device(): pl.pallas_call(functools.partial(attend, devices, parts), out_shape=(jax....]
  transfers between devices with their start and end apart: 9 -> 6, of which waited for: 8 -> 5; matrix products, arithmetic and copies ran while one was open for 7% -> 7% of each run, Pallas kernels for 6% -> 5%
where the time goes in v7:
time: 37.8 us; the launch traced here: 37.5 us
  blocking collectives  14.6 us (39%)
  starting transfers between devices  8.04 us (21%)
  Pallas kernels  5.77 us (15%)
  waiting for transfers between devices  4.72 us (12%)
  other arithmetic  2.46 us (7%)
  local copies, waits for them, and re-layouts  1.09 us (3%)
  between operations  0.81 us (2%)
    all_to_all x1, blocking collectives, on_device(): terms = lax.all_to_all(sent, ('req', 'tp'), 0, 0, tiled=True)  14.6 us
    ppermute x4, starting transfers between devices, gather_by_doubling(): other = lax.ppermute(held, 'req', [(i, i ^ bit) for i in range(devices)])  7.97 us
    pallas_call x1, Pallas kernels, on_device(): pl.pallas_call(functools.partial(attend, devices, parts), out_shape=(jax....  3 us
    ppermute x4, waiting for transfers between devices, gather_by_doubling(): other = lax.ppermute(held, 'req', [(i, i ^ bit) for i in range(devices)])  2.31 us
    pallas_call x1, Pallas kernels, turned(): pl.pallas_call(turn, out_shape=jax.ShapeDtypeStruct((width, pages * page)...  1.95 us
    ppermute x1, waiting for transfers between devices, integers(): return (lax.ppermute(slots, 'req', other_core), long[:, None])  1.25 us
    ppermute x1, waiting for transfers between devices, on_device(): lax.ppermute(theirs, 'req', other_core)  1.15 us
  transfers between devices with their start and end apart: 6, of which 5 were waited for; matrix products, arithmetic and copies ran while one was open for 7% of the time, Pallas kernels for 5%

profile of v7, /device:TPU:0, one launch (start us, length us, event | category | flops | bytes accessed | tf_op | source)
XLA Modules:
  0.0 37.5 jit_solution(11320828794008783441)
XLA Ops:
  0.6 0.7 %maximum_bitcast_fusion.own_ref = bf16[1,4,3072]{2,1,0:T(4,128)(2,1)S(1)} fusion(bf16[4,1024]{1,0:T(4,128)(2,1)} %param.14, bf16[4,1024]{1,0:T(4,128)(2,1)} %param.13, bf16[4,1024]{1,0:T(4,128)(2,1)} %param.12), kind=kLoop, calls=%fused_computation.1 | loop fusion | flops 73728 | bytes 49152 | tf_op jit(solution)/shard_map/broadcast_in_dim | solution.py:38
  1.4 4.1 %collective-permute-start = (bf16[1,4,3072]{2,1,0:T(4,128)(2,1)S(1)}, bf16[1,4,3072]{2,1,0:T(4,128)(2,1)S(1)}, u32[]{:S(2)}, u32[]{:S(2)}) collective-permute-start(bf16[1,4,3072]{2,1,0:T(4,128)(2,1)S(1)} %maximum_bitcast_fusion.own_ref), channel_id=1, source_target_pairs={{0,16},{2,18},{4,20},{6,22},{8,24},{10,26},{12,28},{14,30},{16,0},... | collective-permute-start | bytes 73736 | tf_op jit(solution)/shard_map/ppermute | solution.py:42
  5.5 0.7 %convert_element_type.3 = f32[4]{0:T(128)S(1)} convert(s32[4]{0:T(128)} %param.21) | non-fusion elementwise | flops 4 | bytes 32 | tf_op jit(solution)/shard_map/convert_element_type | solution.py:80
  6.2 0.1 pad.11.clone
  6.2 0.1 pad.8.clone
  6.3 0.1 multiply_cosine_fusion
  6.4 0.1 maximum_maximum_fusion.1
  6.6 0.7 %fusion.4 = (s32[1,4]{1,0:T(1,128)S(1)}, s32[1,4]{1,0:T(1,128)S(1)}) fusion(s32[4]{0:T(128)} %param.23, s32[]{:T(128)S(6)} %axis_index.19), kind=kLoop, calls=%fused_computation.29 | loop fusion | flops 140 | bytes 52 | tf_op jit(solution)/shard_map/stack | solution.py:59
  7.3 0.0 collective-permute-done.other_ref
  7.3 1.9 %collective-permute-start.2 = (bf16[2,4,3072]{2,1,0:T(4,128)(2,1)S(1)}, bf16[2,4,3072]{2,1,0:T(4,128)(2,1)S(1)}, u32[]{:S(2)}, u32[]{:S(2)}) collective-permute-start(bf16[2,4,3072]{2,1,0:T(4,128)(2,1)S(1)} %shard_map.139.own_ref), channel_id=1, source_target_pairs={{0,8},{2,10},{4,12},{6,14},{8,0},{10,2},{12,4},{14,6},{16,24},{18,... | collective-permute-start | bytes 147464 | tf_op jit(solution)/shard_map/ppermute | solution.py:42
  9.2 0.1 pad.16.clone
  9.3 0.7 %copy.15.rest_1_.lengths_ref = s32[4,1]{1,0:T(4,128)S(1)} copy(s32[4,1]{0,1:T(1,128)} %bitcast.13) | data formatting | bytes 32 | tf_op jit(solution)/shard_map/broadcast_in_dim | solution.py:218
  10.0 0.0 copy-start.4
  10.0 0.0 collective-permute-start.1
  10.0 1.3 %collective-permute-done.1.rest_0_ = s32[4]{0:T(128)S(1)} collective-permute-done((s32[4]{0:T(128)}, s32[4]{0:T(128)S(1)}, u32[]{:S(2)}, u32[]{:S(2)}) %collective-permute-start.1) | collective-permute-done | bytes 48 | tf_op jit(solution)/shard_map/ppermute | solution.py:218
  11.3 0.2 collective-permute-done.2.other_ref
  11.5 0.0 slice-start
  11.5 0.0 slice-start.1
  11.5 1.9 %collective-permute-start.3 = (bf16[4,4,3072]{2,1,0:T(4,128)(2,1)S(1)}, bf16[4,4,3072]{2,1,0:T(4,128)(2,1)S(1)}, u32[]{:S(2)}, u32[]{:S(2)}) collective-permute-start(bf16[4,4,3072]{2,1,0:T(4,128)(2,1)S(1)} %shard_map.140.after_ref.own_ref), channel_id=1, source_target_pairs={{0,4},{2,6},{4,0},{6,2},{8,12},{10,14},{12,8},{14,10},{16,20},{18,... | collective-permute-start | bytes 294920 | tf_op jit(solution)/shard_map/ppermute | solution.py:42
  13.4 0.0 copy-done.4
  13.4 1.9 %shard_map.141.rest_0_.keys_ref = bf16[1024,3072]{1,0:T(8,128)(2,1)S(1)} custom-call(bf16[24,128,1024]{2,1,0:T(8,128)(2,1)S(1)} %copy-done.4, bf16[4,4,3072]{2,1,0:T(4,128)(2,1)S(1)} %shard_map.140.after_ref.own_ref), custom_call_target="tpu_custom_call" | custom-call | flops 4294967296 | bytes 1048576 | tf_op jit(solution)/shard_map/pallas_call | solution.py:99
  15.4 0.0 copy-start.5
  15.4 0.0 copy-start
  15.4 0.0 copy-start.2
  15.4 0.9 %collective-permute-done.3.other_ref = bf16[4,4,3072]{2,1,0:T(4,128)(2,1)S(1)} collective-permute-done((bf16[4,4,3072]{2,1,0:T(4,128)(2,1)S(1)}, bf16[4,4,3072]{2,1,0:T(4,128)(2,1)S(1)}, u32[]{:S(2)}, u32[]{:S(2)}) %collective-permute-start.3) | collective-permute-done | bytes 98336 | tf_op jit(solution)/shard_map/ppermute | solution.py:42
  16.3 0.1 collective-permute-start.4
  16.4 0.0 copy-done.5
  16.4 0.1 and_select_fusion.3
  16.5 0.1 add_add_fusion.where_ref
  16.6 0.0 copy-start.1
  16.6 0.0 copy-start.3
  16.6 1.3 %collective-permute-done.4.far_ref = bf16[8,4,3072]{2,1,0:T(4,128)(2,1)S(1)} collective-permute-done((bf16[8,4,3072]{2,1,0:T(4,128)(2,1)S(1)}, bf16[8,4,3072]{2,1,0:T(4,128)(2,1)S(1)}, u32[]{:S(2)}, u32[]{:S(2)}) %collective-permute-start.4) | collective-permute-done | bytes 196640 | tf_op jit(solution)/shard_map/ppermute | solution.py:42
  17.8 0.0 slice-done
  17.8 0.0 slice-done.1
  17.8 0.0 copy-done
  17.8 0.0 copy-done.2
  17.8 3.0 %shard_map.143 = (bf16[32,4,512]{2,1,0:T(4,128)(2,1)S(1)}, bf16[4,1024]{1,0:T(4,128)(2,1)}, bf16[4,1024]{1,0:T(4,128)(2,1)}) custom-call(s32[2,4]{1,0:T(2,128)S(1)} %pad_add_fusion.places_ref, bf16[8,4,3072]{2,1,0:T(4,128)(2,1)S(1)} %shard_map.142.near_ref, bf16[8,4,3072]{2,1,0:T(4,128)(2,1)S(1)} %collective-permute-done.4.far_ref, ...), custom_call_target="tpu_custom_call" | custom-call | tf_op jit(solution)/shard_map/pallas_call | solution.py:232
  20.8 14.6 %all_to_all.5.terms_ref = bf16[32,4,512]{2,1,0:T(4,128)(2,1)S(1)} all-to-all(bf16[32,4,512]{2,1,0:T(4,128)(2,1)S(1)} %get-tuple-element.16), channel_id=1, replica_groups=mesh['req'=16,'tp'=2] {'req','tp'}, dimensions={0} | all-to-all | bytes 262144 | tf_op jit(solution)/shard_map/all_to_all | solution.py:245
  35.4 0.2 shard_map.144
  35.6 0.1 collective-permute-start.5
  35.6 1.2 %collective-permute-done.5.other_ref = bf16[4,512]{1,0:T(4,128)(2,1)S(1)} collective-permute-done((bf16[4,512]{1,0:T(4,128)(2,1)S(1)}, bf16[4,512]{1,0:T(4,128)(2,1)S(1)}, u32[]{:S(2)}, u32[]{:S(2)}) %collective-permute-start.5) | collective-permute-done | bytes 4128 | tf_op jit(solution)/shard_map/ppermute | solution.py:259
  36.8 0.0 copy-done.1
  36.8 0.0 copy-done.3
  36.8 0.6 %shard_map.145 = bf16[4,1024]{1,0:T(4,128)(2,1)} custom-call(s32[3,8]{1,0:T(4,128)S(1)} %add_add_fusion.where_ref, bf16[4,512]{1,0:T(4,128)(2,1)S(1)} %get-tuple-element.17.mine_ref, bf16[4,512]{1,0:T(4,128)(2,1)S(1)} %collective-permute-done.5.other_ref, bf16[4,1024]{1,0:T(4,128)(2,1)S(1)} %copy-done.1, bf16[1024]{0:T(1024)(128)(2,1)S(1)} %copy-done.3), custom_call_target="tpu_custom_call" | custom-call | tf_op jit(solution)/shard_map/pallas_call | solution.py:253
  (17 shorter events, 0.1 us)
Async XLA Ops:
  1.4 5.9 %collective-permute-start = (bf16[1,4,3072]{2,1,0:T(4,128)(2,1)S(1)}, bf16[1,4,3072]{2,1,0:T(4,128)(2,1)S(1)}, u32[]{:S(2)}, u32[]{:S(2)}) collective-permute-start(bf16[1,4,3072]{2,1,0:T(4,128)(2,1)S(1)} %maximum_bitcast_fusion.own_ref), channel_id=1, source_target_pairs={{0,16},{2,18},{4,20},{6,22},{8,24},{10,26},{12,28},{14,30},{16,0},... | collective-permute-start | bytes 73736 | tf_op jit(solution)/shard_map/ppermute | solution.py:42
  7.3 4.2 %collective-permute-start.2 = (bf16[2,4,3072]{2,1,0:T(4,128)(2,1)S(1)}, bf16[2,4,3072]{2,1,0:T(4,128)(2,1)S(1)}, u32[]{:S(2)}, u32[]{:S(2)}) collective-permute-start(bf16[2,4,3072]{2,1,0:T(4,128)(2,1)S(1)} %shard_map.139.own_ref), channel_id=1, source_target_pairs={{0,8},{2,10},{4,12},{6,14},{8,0},{10,2},{12,4},{14,6},{16,24},{18,... | collective-permute-start | bytes 147464 | tf_op jit(solution)/shard_map/ppermute | solution.py:42
  10.0 3.4 %copy-start.4 = (bf16[24,128,1024]{2,1,0:T(8,128)(2,1)S(1)}, bf16[24,128,1024]{2,1,0:T(8,128)(2,1)}, u32[]{:S(2)}) copy-start(bf16[24,128,1024]{2,1,0:T(8,128)(2,1)} %pages_ref.1) | copy-start | bytes 18874372
  10.0 1.3 %collective-permute-start.1 = (s32[4]{0:T(128)}, s32[4]{0:T(128)S(1)}, u32[]{:S(2)}, u32[]{:S(2)}) collective-permute-start(s32[4]{0:T(128)} %param.22), channel_id=1, source_target_pairs={{0,2},{2,0},{4,6},{6,4},{8,10},{10,8},{12,14},{14,12},{16,18},{18,... | collective-permute-start | bytes 56 | tf_op jit(solution)/shard_map/ppermute | solution.py:218
  11.5 6.3 %slice-start = ((s8[6291456]{0:T(1024)(128)(4,1)}), s8[4194304]{0:T(1024)(128)(4,1)S(1)}, s32[]{:S(2)}) async-start(s8[6291456]{0:T(1024)(128)(4,1)} %bitcast.10), calls=%async_computation.1 | async-start | bytes 8388608
  11.5 6.3 %slice-start.1 = ((s8[6291456]{0:T(1024)(128)(4,1)}), s8[2097152]{0:T(1024)(128)(4,1)S(1)}, s32[]{:S(2)}) async-start(s8[6291456]{0:T(1024)(128)(4,1)} %bitcast.10), calls=%async_computation.2 | async-start | bytes 4194304
  11.5 4.8 %collective-permute-start.3 = (bf16[4,4,3072]{2,1,0:T(4,128)(2,1)S(1)}, bf16[4,4,3072]{2,1,0:T(4,128)(2,1)S(1)}, u32[]{:S(2)}, u32[]{:S(2)}) collective-permute-start(bf16[4,4,3072]{2,1,0:T(4,128)(2,1)S(1)} %shard_map.140.after_ref.own_ref), channel_id=1, source_target_pairs={{0,4},{2,6},{4,0},{6,2},{8,12},{10,14},{12,8},{14,10},{16,20},{18,... | collective-permute-start | bytes 294920 | tf_op jit(solution)/shard_map/ppermute | solution.py:42
  15.4 1.0 %copy-start.5 = (s32[4]{0:T(128)S(1)}, s32[4]{0:T(128)}, u32[]{:S(2)}) copy-start(s32[4]{0:T(128)} %param.22) | copy-start | bytes 52
  15.4 2.4 %copy-start = (bf16[1024,2048]{1,0:T(8,128)(2,1)S(1)}, bf16[1024,2048]{1,0:T(8,128)(2,1)}, u32[]{:S(2)}) copy-start(bf16[1024,2048]{1,0:T(8,128)(2,1)} %weight_ref.1) | copy-start | bytes 12582916
  15.4 2.4 %copy-start.2 = (s32[4,8]{1,0:T(4,128)S(1)}, s32[4,8]{1,0:T(4,128)}, u32[]{:S(2)}) copy-start(s32[4,8]{1,0:T(4,128)} %table_ref.1) | copy-start | bytes 388
  16.3 1.5 %collective-permute-start.4 = (bf16[8,4,3072]{2,1,0:T(4,128)(2,1)S(1)}, bf16[8,4,3072]{2,1,0:T(4,128)(2,1)S(1)}, u32[]{:S(2)}, u32[]{:S(2)}) collective-permute-start(bf16[8,4,3072]{2,1,0:T(4,128)(2,1)S(1)} %shard_map.142.near_ref), channel_id=1, source_target_pairs={{0,2},{2,0},{4,6},{6,4},{8,10},{10,8},{12,14},{14,12},{16,18},{18,... | collective-permute-start | bytes 589832 | tf_op jit(solution)/shard_map/ppermute | solution.py:42
  16.6 20.3 %copy-start.1 = (bf16[4,1024]{1,0:T(4,128)(2,1)S(1)}, bf16[4,1024]{1,0:T(4,128)(2,1)}, u32[]{:S(2)}) copy-start(bf16[4,1024]{1,0:T(4,128)(2,1)} %residual_ref.1) | copy-start | bytes 24580
  16.6 20.3 %copy-start.3 = (bf16[1024]{0:T(1024)(128)(2,1)S(1)}, bf16[1024]{0:T(1024)(128)(2,1)}, u32[]{:S(2)}) copy-start(bf16[1024]{0:T(1024)(128)(2,1)} %bias_ref.1) | copy-start | bytes 6148
  35.6 1.2 %collective-permute-start.5 = (bf16[4,512]{1,0:T(4,128)(2,1)S(1)}, bf16[4,512]{1,0:T(4,128)(2,1)S(1)}, u32[]{:S(2)}, u32[]{:S(2)}) collective-permute-start(bf16[4,512]{1,0:T(4,128)(2,1)S(1)} %get-tuple-element.18), channel_id=1, source_target_pairs={{0,2},{2,0},{4,6},{6,4},{8,10},{10,8},{12,14},{14,12},{16,18},{18,... | collective-permute-start | bytes 12296 | tf_op jit(solution)/shard_map/ppermute | solution.py:259

commit v8 on v7

--- a/solution.py
+++ b/solution.py
@@ -174,11 +174,12 @@
     scored = [score(first) for first in starts]
     softened = [soften(*x) for x in scored]
     attended = [gather_values(first, *x) for first, x in zip(starts, softened)]
-    attended = jnp.concatenate(attended, axis=1).astype(BF16)
 
     for part in range(parts):
-        columns = weight_ref[:, part * width:(part + 1) * width]
-        terms = jnp.dot(attended, columns, preferred_element_type=F32).astype(BF16)
+        terms = sum(
+            jnp.dot(x.astype(BF16), weight_ref[first:first + lanes, part * width:(part + 1) * width], preferred_element_type=F32)
+            for first, x in zip(starts, attended)
+        ).astype(BF16)
         for device in range(devices):
             first = device % CORES * (width // CORES)
             sent_out[device * parts + part] = terms[:, first:first + width // CORES]

time: 37.8 us -> 37.4 us (0.989)
  Pallas kernels: 5.77 us -> 5.38 us
    pallas_call x1, Pallas kernels: 3 us -> 2.61 us  [on_device(): pl.pallas_call(functools.partial(attend, devices, parts), out_shape=(jax....]
where the time goes in v8:
time: 37.4 us; the launch traced here: 37.1 us
  blocking collectives  14.6 us (39%)
  starting transfers between devices  8.04 us (21%)
  Pallas kernels  5.38 us (14%)
  waiting for transfers between devices  4.72 us (13%)
  other arithmetic  2.46 us (7%)
  local copies, waits for them, and re-layouts  1.09 us (3%)
  between operations  0.81 us (2%)
    all_to_all x1, blocking collectives, on_device(): terms = lax.all_to_all(sent, ('req', 'tp'), 0, 0, tiled=True)  14.6 us
    ppermute x4, starting transfers between devices, gather_by_doubling(): other = lax.ppermute(held, 'req', [(i, i ^ bit) for i in range(devices)])  7.97 us
    pallas_call x1, Pallas kernels, on_device(): pl.pallas_call(functools.partial(attend, devices, parts), out_shape=(jax....  2.61 us
    ppermute x4, waiting for transfers between devices, gather_by_doubling(): other = lax.ppermute(held, 'req', [(i, i ^ bit) for i in range(devices)])  2.31 us
    pallas_call x1, Pallas kernels, turned(): pl.pallas_call(turn, out_shape=jax.ShapeDtypeStruct((width, pages * page)...  1.95 us
    ppermute x1, waiting for transfers between devices, integers(): return (lax.ppermute(slots, 'req', other_core), long[:, None])  1.25 us
    ppermute x1, waiting for transfers between devices, on_device(): lax.ppermute(theirs, 'req', other_core)  1.15 us
  transfers between devices with their start and end apart: 6, of which 5 were waited for; matrix products, arithmetic and copies ran while one was open for 7% of the time, Pallas kernels for 5%

profile of v8, /device:TPU:0, one launch (start us, length us, event | category | flops | bytes accessed | tf_op | source)
XLA Modules:
  0.0 37.1 jit_solution(18329609826135443016)
XLA Ops:
  0.6 0.7 %maximum_bitcast_fusion.own_ref = bf16[1,4,3072]{2,1,0:T(4,128)(2,1)S(1)} fusion(bf16[4,1024]{1,0:T(4,128)(2,1)} %param.14, bf16[4,1024]{1,0:T(4,128)(2,1)} %param.13, bf16[4,1024]{1,0:T(4,128)(2,1)} %param.12), kind=kLoop, calls=%fused_computation.1 | loop fusion | flops 73728 | bytes 49152 | tf_op jit(solution)/shard_map/broadcast_in_dim | solution.py:38
  1.4 4.1 %collective-permute-start = (bf16[1,4,3072]{2,1,0:T(4,128)(2,1)S(1)}, bf16[1,4,3072]{2,1,0:T(4,128)(2,1)S(1)}, u32[]{:S(2)}, u32[]{:S(2)}) collective-permute-start(bf16[1,4,3072]{2,1,0:T(4,128)(2,1)S(1)} %maximum_bitcast_fusion.own_ref), channel_id=1, source_target_pairs={{0,16},{2,18},{4,20},{6,22},{8,24},{10,26},{12,28},{14,30},{16,0},... | collective-permute-start | bytes 73736 | tf_op jit(solution)/shard_map/ppermute | solution.py:42
  5.5 0.7 %convert_element_type.3 = f32[4]{0:T(128)S(1)} convert(s32[4]{0:T(128)} %param.21) | non-fusion elementwise | flops 4 | bytes 32 | tf_op jit(solution)/shard_map/convert_element_type | solution.py:80
  6.2 0.1 pad.11.clone
  6.2 0.1 pad.8.clone
  6.3 0.1 multiply_cosine_fusion
  6.4 0.1 maximum_maximum_fusion.1
  6.6 0.7 %fusion.4 = (s32[1,4]{1,0:T(1,128)S(1)}, s32[1,4]{1,0:T(1,128)S(1)}) fusion(s32[4]{0:T(128)} %param.23, s32[]{:T(128)S(6)} %axis_index.19), kind=kLoop, calls=%fused_computation.29 | loop fusion | flops 140 | bytes 52 | tf_op jit(solution)/shard_map/stack | solution.py:59
  7.3 0.0 collective-permute-done.other_ref
  7.3 1.9 %collective-permute-start.2 = (bf16[2,4,3072]{2,1,0:T(4,128)(2,1)S(1)}, bf16[2,4,3072]{2,1,0:T(4,128)(2,1)S(1)}, u32[]{:S(2)}, u32[]{:S(2)}) collective-permute-start(bf16[2,4,3072]{2,1,0:T(4,128)(2,1)S(1)} %shard_map.139.own_ref), channel_id=1, source_target_pairs={{0,8},{2,10},{4,12},{6,14},{8,0},{10,2},{12,4},{14,6},{16,24},{18,... | collective-permute-start | bytes 147464 | tf_op jit(solution)/shard_map/ppermute | solution.py:42
  9.2 0.1 pad.16.clone
  9.3 0.7 %copy.15.rest_1_.lengths_ref = s32[4,1]{1,0:T(4,128)S(1)} copy(s32[4,1]{0,1:T(1,128)} %bitcast.13) | data formatting | bytes 32 | tf_op jit(solution)/shard_map/broadcast_in_dim | solution.py:219
  10.0 0.0 copy-start.4
  10.0 0.0 collective-permute-start.1
  10.0 1.3 %collective-permute-done.1.rest_0_ = s32[4]{0:T(128)S(1)} collective-permute-done((s32[4]{0:T(128)}, s32[4]{0:T(128)S(1)}, u32[]{:S(2)}, u32[]{:S(2)}) %collective-permute-start.1) | collective-permute-done | bytes 48 | tf_op jit(solution)/shard_map/ppermute | solution.py:219
  11.3 0.2 collective-permute-done.2.other_ref
  11.5 0.0 slice-start
  11.5 0.0 slice-start.1
  11.5 1.9 %collective-permute-start.3 = (bf16[4,4,3072]{2,1,0:T(4,128)(2,1)S(1)}, bf16[4,4,3072]{2,1,0:T(4,128)(2,1)S(1)}, u32[]{:S(2)}, u32[]{:S(2)}) collective-permute-start(bf16[4,4,3072]{2,1,0:T(4,128)(2,1)S(1)} %shard_map.140.after_ref.own_ref), channel_id=1, source_target_pairs={{0,4},{2,6},{4,0},{6,2},{8,12},{10,14},{12,8},{14,10},{16,20},{18,... | collective-permute-start | bytes 294920 | tf_op jit(solution)/shard_map/ppermute | solution.py:42
  13.4 0.0 copy-done.4
  13.4 1.9 %shard_map.141.rest_0_.keys_ref = bf16[1024,3072]{1,0:T(8,128)(2,1)S(1)} custom-call(bf16[24,128,1024]{2,1,0:T(8,128)(2,1)S(1)} %copy-done.4, bf16[4,4,3072]{2,1,0:T(4,128)(2,1)S(1)} %shard_map.140.after_ref.own_ref), custom_call_target="tpu_custom_call" | custom-call | flops 4294967296 | bytes 1048576 | tf_op jit(solution)/shard_map/pallas_call | solution.py:99
  15.4 0.0 copy-start.5
  15.4 0.0 copy-start
  15.4 0.0 copy-start.2
  15.4 0.9 %collective-permute-done.3.other_ref = bf16[4,4,3072]{2,1,0:T(4,128)(2,1)S(1)} collective-permute-done((bf16[4,4,3072]{2,1,0:T(4,128)(2,1)S(1)}, bf16[4,4,3072]{2,1,0:T(4,128)(2,1)S(1)}, u32[]{:S(2)}, u32[]{:S(2)}) %collective-permute-start.3) | collective-permute-done | bytes 98336 | tf_op jit(solution)/shard_map/ppermute | solution.py:42
  16.3 0.1 collective-permute-start.4
  16.4 0.0 copy-done.5
  16.4 0.1 and_select_fusion.3
  16.5 0.1 add_add_fusion.where_ref
  16.6 0.0 copy-start.1
  16.6 0.0 copy-start.3
  16.6 1.3 %collective-permute-done.4.far_ref = bf16[8,4,3072]{2,1,0:T(4,128)(2,1)S(1)} collective-permute-done((bf16[8,4,3072]{2,1,0:T(4,128)(2,1)S(1)}, bf16[8,4,3072]{2,1,0:T(4,128)(2,1)S(1)}, u32[]{:S(2)}, u32[]{:S(2)}) %collective-permute-start.4) | collective-permute-done | bytes 196640 | tf_op jit(solution)/shard_map/ppermute | solution.py:42
  17.8 0.0 slice-done
  17.8 0.0 slice-done.1
  17.8 0.0 copy-done
  17.8 0.0 copy-done.2
  17.8 2.6 %shard_map.143 = (bf16[32,4,512]{2,1,0:T(4,128)(2,1)S(1)}, bf16[4,1024]{1,0:T(4,128)(2,1)}, bf16[4,1024]{1,0:T(4,128)(2,1)}) custom-call(s32[2,4]{1,0:T(2,128)S(1)} %pad_add_fusion.places_ref, bf16[8,4,3072]{2,1,0:T(4,128)(2,1)S(1)} %shard_map.142.near_ref, bf16[8,4,3072]{2,1,0:T(4,128)(2,1)S(1)} %collective-permute-done.4.far_ref, ...), custom_call_target="tpu_custom_call" | custom-call | tf_op jit(solution)/shard_map/pallas_call | solution.py:233
  20.5 14.6 %all_to_all.5.terms_ref = bf16[32,4,512]{2,1,0:T(4,128)(2,1)S(1)} all-to-all(bf16[32,4,512]{2,1,0:T(4,128)(2,1)S(1)} %get-tuple-element.16), channel_id=1, replica_groups=mesh['req'=16,'tp'=2] {'req','tp'}, dimensions={0} | all-to-all | bytes 262144 | tf_op jit(solution)/shard_map/all_to_all | solution.py:246
  35.0 0.2 shard_map.144
  35.2 0.1 collective-permute-start.5
  35.3 1.2 %collective-permute-done.5.other_ref = bf16[4,512]{1,0:T(4,128)(2,1)S(1)} collective-permute-done((bf16[4,512]{1,0:T(4,128)(2,1)S(1)}, bf16[4,512]{1,0:T(4,128)(2,1)S(1)}, u32[]{:S(2)}, u32[]{:S(2)}) %collective-permute-start.5) | collective-permute-done | bytes 4128 | tf_op jit(solution)/shard_map/ppermute | solution.py:260
  36.4 0.0 copy-done.1
  36.4 0.0 copy-done.3
  36.4 0.6 %shard_map.145 = bf16[4,1024]{1,0:T(4,128)(2,1)} custom-call(s32[3,8]{1,0:T(4,128)S(1)} %add_add_fusion.where_ref, bf16[4,512]{1,0:T(4,128)(2,1)S(1)} %get-tuple-element.17.mine_ref, bf16[4,512]{1,0:T(4,128)(2,1)S(1)} %collective-permute-done.5.other_ref, bf16[4,1024]{1,0:T(4,128)(2,1)S(1)} %copy-done.1, bf16[1024]{0:T(1024)(128)(2,1)S(1)} %copy-done.3), custom_call_target="tpu_custom_call" | custom-call | tf_op jit(solution)/shard_map/pallas_call | solution.py:254
  (17 shorter events, 0.1 us)
Async XLA Ops:
  1.4 5.9 %collective-permute-start = (bf16[1,4,3072]{2,1,0:T(4,128)(2,1)S(1)}, bf16[1,4,3072]{2,1,0:T(4,128)(2,1)S(1)}, u32[]{:S(2)}, u32[]{:S(2)}) collective-permute-start(bf16[1,4,3072]{2,1,0:T(4,128)(2,1)S(1)} %maximum_bitcast_fusion.own_ref), channel_id=1, source_target_pairs={{0,16},{2,18},{4,20},{6,22},{8,24},{10,26},{12,28},{14,30},{16,0},... | collective-permute-start | bytes 73736 | tf_op jit(solution)/shard_map/ppermute | solution.py:42
  7.3 4.2 %collective-permute-start.2 = (bf16[2,4,3072]{2,1,0:T(4,128)(2,1)S(1)}, bf16[2,4,3072]{2,1,0:T(4,128)(2,1)S(1)}, u32[]{:S(2)}, u32[]{:S(2)}) collective-permute-start(bf16[2,4,3072]{2,1,0:T(4,128)(2,1)S(1)} %shard_map.139.own_ref), channel_id=1, source_target_pairs={{0,8},{2,10},{4,12},{6,14},{8,0},{10,2},{12,4},{14,6},{16,24},{18,... | collective-permute-start | bytes 147464 | tf_op jit(solution)/shard_map/ppermute | solution.py:42
  10.0 3.4 %copy-start.4 = (bf16[24,128,1024]{2,1,0:T(8,128)(2,1)S(1)}, bf16[24,128,1024]{2,1,0:T(8,128)(2,1)}, u32[]{:S(2)}) copy-start(bf16[24,128,1024]{2,1,0:T(8,128)(2,1)} %pages_ref.1) | copy-start | bytes 18874372
  10.0 1.3 %collective-permute-start.1 = (s32[4]{0:T(128)}, s32[4]{0:T(128)S(1)}, u32[]{:S(2)}, u32[]{:S(2)}) collective-permute-start(s32[4]{0:T(128)} %param.22), channel_id=1, source_target_pairs={{0,2},{2,0},{4,6},{6,4},{8,10},{10,8},{12,14},{14,12},{16,18},{18,... | collective-permute-start | bytes 56 | tf_op jit(solution)/shard_map/ppermute | solution.py:219
  11.5 6.3 %slice-start = ((s8[6291456]{0:T(1024)(128)(4,1)}), s8[4194304]{0:T(1024)(128)(4,1)S(1)}, s32[]{:S(2)}) async-start(s8[6291456]{0:T(1024)(128)(4,1)} %bitcast.10), calls=%async_computation.1 | async-start | bytes 8388608
  11.5 6.3 %slice-start.1 = ((s8[6291456]{0:T(1024)(128)(4,1)}), s8[2097152]{0:T(1024)(128)(4,1)S(1)}, s32[]{:S(2)}) async-start(s8[6291456]{0:T(1024)(128)(4,1)} %bitcast.10), calls=%async_computation.2 | async-start | bytes 4194304
  11.5 4.8 %collective-permute-start.3 = (bf16[4,4,3072]{2,1,0:T(4,128)(2,1)S(1)}, bf16[4,4,3072]{2,1,0:T(4,128)(2,1)S(1)}, u32[]{:S(2)}, u32[]{:S(2)}) collective-permute-start(bf16[4,4,3072]{2,1,0:T(4,128)(2,1)S(1)} %shard_map.140.after_ref.own_ref), channel_id=1, source_target_pairs={{0,4},{2,6},{4,0},{6,2},{8,12},{10,14},{12,8},{14,10},{16,20},{18,... | collective-permute-start | bytes 294920 | tf_op jit(solution)/shard_map/ppermute | solution.py:42
  15.4 1.0 %copy-start.5 = (s32[4]{0:T(128)S(1)}, s32[4]{0:T(128)}, u32[]{:S(2)}) copy-start(s32[4]{0:T(128)} %param.22) | copy-start | bytes 52
  15.4 2.4 %copy-start = (bf16[1024,2048]{1,0:T(8,128)(2,1)S(1)}, bf16[1024,2048]{1,0:T(8,128)(2,1)}, u32[]{:S(2)}) copy-start(bf16[1024,2048]{1,0:T(8,128)(2,1)} %weight_ref.1) | copy-start | bytes 12582916
  15.4 2.4 %copy-start.2 = (s32[4,8]{1,0:T(4,128)S(1)}, s32[4,8]{1,0:T(4,128)}, u32[]{:S(2)}) copy-start(s32[4,8]{1,0:T(4,128)} %table_ref.1) | copy-start | bytes 388
  16.3 1.5 %collective-permute-start.4 = (bf16[8,4,3072]{2,1,0:T(4,128)(2,1)S(1)}, bf16[8,4,3072]{2,1,0:T(4,128)(2,1)S(1)}, u32[]{:S(2)}, u32[]{:S(2)}) collective-permute-start(bf16[8,4,3072]{2,1,0:T(4,128)(2,1)S(1)} %shard_map.142.near_ref), channel_id=1, source_target_pairs={{0,2},{2,0},{4,6},{6,4},{8,10},{10,8},{12,14},{14,12},{16,18},{18,... | collective-permute-start | bytes 589832 | tf_op jit(solution)/shard_map/ppermute | solution.py:42
  16.6 19.9 %copy-start.1 = (bf16[4,1024]{1,0:T(4,128)(2,1)S(1)}, bf16[4,1024]{1,0:T(4,128)(2,1)}, u32[]{:S(2)}) copy-start(bf16[4,1024]{1,0:T(4,128)(2,1)} %residual_ref.1) | copy-start | bytes 24580
  16.6 19.9 %copy-start.3 = (bf16[1024]{0:T(1024)(128)(2,1)S(1)}, bf16[1024]{0:T(1024)(128)(2,1)}, u32[]{:S(2)}) copy-start(bf16[1024]{0:T(1024)(128)(2,1)} %bias_ref.1) | copy-start | bytes 6148
  35.2 1.2 %collective-permute-start.5 = (bf16[4,512]{1,0:T(4,128)(2,1)S(1)}, bf16[4,512]{1,0:T(4,128)(2,1)S(1)}, u32[]{:S(2)}, u32[]{:S(2)}) collective-permute-start(bf16[4,512]{1,0:T(4,128)(2,1)S(1)} %get-tuple-element.18), channel_id=1, source_target_pairs={{0,2},{2,0},{4,6},{6,4},{8,10},{10,8},{12,14},{14,12},{16,18},{18,... | collective-permute-start | bytes 12296 | tf_op jit(solution)/shard_map/ppermute | solution.py:260

commit v9 on v8

--- a/solution.py
+++ b/solution.py
@@ -152,13 +152,13 @@
 
     def score(first):
         spread = [jnp.concatenate([x[:, first:first + lanes]] * together, axis=0) for x in (query, key.astype(F32), value)]
-        queries = jnp.where(mine, spread[0], 0.0)
-        own_score = jnp.sum(queries * spread[1], axis=1, keepdims=True) * scale
+        queries = jnp.where(mine, spread[0] * scale, 0.0)
+        own_score = jnp.sum(queries * spread[1], axis=1, keepdims=True)
         return jnp.dot(queries.astype(BF16), keys_ref[first:first + lanes], preferred_element_type=F32), own_score, spread[2]
 
     def soften(scores, own_score, own_value):
         masked = jnp.concatenate(
-            [jnp.where(shown[p], scores[:, p * page:(p + 1) * page] * scale, -jnp.inf) for p in range(pages)], axis=1
+            [jnp.where(shown[p], scores[:, p * page:(p + 1) * page], -jnp.inf) for p in range(pages)], axis=1
         )
         top = jnp.maximum(jnp.max(masked, axis=1, keepdims=True), own_score)
         exps = jnp.exp(masked - top)

time: 37.4 us -> 37.4 us (level)
  no operation moved by 1% of the time
where the time goes in v9:
time: 37.4 us; the launch traced here: 37.1 us
  blocking collectives  14.6 us (39%)
  starting transfers between devices  8.04 us (21%)
  Pallas kernels  5.37 us (14%)
  waiting for transfers between devices  4.72 us (13%)
  other arithmetic  2.46 us (7%)
  local copies, waits for them, and re-layouts  1.09 us (3%)
  between operations  0.81 us (2%)
    all_to_all x1, blocking collectives, on_device(): terms = lax.all_to_all(sent, ('req', 'tp'), 0, 0, tiled=True)  14.6 us
    ppermute x4, starting transfers between devices, gather_by_doubling(): other = lax.ppermute(held, 'req', [(i, i ^ bit) for i in range(devices)])  7.97 us
    pallas_call x1, Pallas kernels, on_device(): pl.pallas_call(functools.partial(attend, devices, parts), out_shape=(jax....  2.6 us
    ppermute x4, waiting for transfers between devices, gather_by_doubling(): other = lax.ppermute(held, 'req', [(i, i ^ bit) for i in range(devices)])  2.31 us
    pallas_call x1, Pallas kernels, turned(): pl.pallas_call(turn, out_shape=jax.ShapeDtypeStruct((width, pages * page)...  1.95 us
    ppermute x1, waiting for transfers between devices, integers(): return (lax.ppermute(slots, 'req', other_core), long[:, None])  1.25 us
    ppermute x1, waiting for transfers between devices, on_device(): lax.ppermute(theirs, 'req', other_core)  1.15 us
  transfers between devices with their start and end apart: 6, of which 5 were waited for; matrix products, arithmetic and copies ran while one was open for 7% of the time, Pallas kernels for 5%

profile of v9, /device:TPU:0, one launch (start us, length us, event | category | flops | bytes accessed | tf_op | source)
XLA Modules:
  0.0 37.1 jit_solution(8532741508259966178)
XLA Ops:
  0.6 0.7 %maximum_bitcast_fusion.own_ref = bf16[1,4,3072]{2,1,0:T(4,128)(2,1)S(1)} fusion(bf16[4,1024]{1,0:T(4,128)(2,1)} %param.14, bf16[4,1024]{1,0:T(4,128)(2,1)} %param.13, bf16[4,1024]{1,0:T(4,128)(2,1)} %param.12), kind=kLoop, calls=%fused_computation.1 | loop fusion | flops 73728 | bytes 49152 | tf_op jit(solution)/shard_map/broadcast_in_dim | solution.py:38
  1.4 4.1 %collective-permute-start = (bf16[1,4,3072]{2,1,0:T(4,128)(2,1)S(1)}, bf16[1,4,3072]{2,1,0:T(4,128)(2,1)S(1)}, u32[]{:S(2)}, u32[]{:S(2)}) collective-permute-start(bf16[1,4,3072]{2,1,0:T(4,128)(2,1)S(1)} %maximum_bitcast_fusion.own_ref), channel_id=1, source_target_pairs={{0,16},{2,18},{4,20},{6,22},{8,24},{10,26},{12,28},{14,30},{16,0},... | collective-permute-start | bytes 73736 | tf_op jit(solution)/shard_map/ppermute | solution.py:42
  5.5 0.7 %convert_element_type.3 = f32[4]{0:T(128)S(1)} convert(s32[4]{0:T(128)} %param.21) | non-fusion elementwise | flops 4 | bytes 32 | tf_op jit(solution)/shard_map/convert_element_type | solution.py:80
  6.2 0.1 pad.11.clone
  6.2 0.1 pad.8.clone
  6.3 0.1 multiply_cosine_fusion
  6.4 0.1 maximum_maximum_fusion.1
  6.6 0.7 %fusion.4 = (s32[1,4]{1,0:T(1,128)S(1)}, s32[1,4]{1,0:T(1,128)S(1)}) fusion(s32[4]{0:T(128)} %param.23, s32[]{:T(128)S(6)} %axis_index.19), kind=kLoop, calls=%fused_computation.29 | loop fusion | flops 140 | bytes 52 | tf_op jit(solution)/shard_map/stack | solution.py:59
  7.3 0.0 collective-permute-done.other_ref
  7.3 1.9 %collective-permute-start.2 = (bf16[2,4,3072]{2,1,0:T(4,128)(2,1)S(1)}, bf16[2,4,3072]{2,1,0:T(4,128)(2,1)S(1)}, u32[]{:S(2)}, u32[]{:S(2)}) collective-permute-start(bf16[2,4,3072]{2,1,0:T(4,128)(2,1)S(1)} %shard_map.139.own_ref), channel_id=1, source_target_pairs={{0,8},{2,10},{4,12},{6,14},{8,0},{10,2},{12,4},{14,6},{16,24},{18,... | collective-permute-start | bytes 147464 | tf_op jit(solution)/shard_map/ppermute | solution.py:42
  9.2 0.1 pad.16.clone
  9.3 0.7 %copy.15.rest_1_.lengths_ref = s32[4,1]{1,0:T(4,128)S(1)} copy(s32[4,1]{0,1:T(1,128)} %bitcast.13) | data formatting | bytes 32 | tf_op jit(solution)/shard_map/broadcast_in_dim | solution.py:219
  10.0 0.0 copy-start.4
  10.0 0.0 collective-permute-start.1
  10.0 1.3 %collective-permute-done.1.rest_0_ = s32[4]{0:T(128)S(1)} collective-permute-done((s32[4]{0:T(128)}, s32[4]{0:T(128)S(1)}, u32[]{:S(2)}, u32[]{:S(2)}) %collective-permute-start.1) | collective-permute-done | bytes 48 | tf_op jit(solution)/shard_map/ppermute | solution.py:219
  11.3 0.2 collective-permute-done.2.other_ref
  11.5 0.0 slice-start
  11.5 0.0 slice-start.1
  11.5 1.9 %collective-permute-start.3 = (bf16[4,4,3072]{2,1,0:T(4,128)(2,1)S(1)}, bf16[4,4,3072]{2,1,0:T(4,128)(2,1)S(1)}, u32[]{:S(2)}, u32[]{:S(2)}) collective-permute-start(bf16[4,4,3072]{2,1,0:T(4,128)(2,1)S(1)} %shard_map.140.after_ref.own_ref), channel_id=1, source_target_pairs={{0,4},{2,6},{4,0},{6,2},{8,12},{10,14},{12,8},{14,10},{16,20},{18,... | collective-permute-start | bytes 294920 | tf_op jit(solution)/shard_map/ppermute | solution.py:42
  13.4 0.0 copy-done.4
  13.4 1.9 %shard_map.141.rest_0_.keys_ref = bf16[1024,3072]{1,0:T(8,128)(2,1)S(1)} custom-call(bf16[24,128,1024]{2,1,0:T(8,128)(2,1)S(1)} %copy-done.4, bf16[4,4,3072]{2,1,0:T(4,128)(2,1)S(1)} %shard_map.140.after_ref.own_ref), custom_call_target="tpu_custom_call" | custom-call | flops 4294967296 | bytes 1048576 | tf_op jit(solution)/shard_map/pallas_call | solution.py:99
  15.4 0.0 copy-start.5
  15.4 0.0 copy-start
  15.4 0.0 copy-start.2
  15.4 0.9 %collective-permute-done.3.other_ref = bf16[4,4,3072]{2,1,0:T(4,128)(2,1)S(1)} collective-permute-done((bf16[4,4,3072]{2,1,0:T(4,128)(2,1)S(1)}, bf16[4,4,3072]{2,1,0:T(4,128)(2,1)S(1)}, u32[]{:S(2)}, u32[]{:S(2)}) %collective-permute-start.3) | collective-permute-done | bytes 98336 | tf_op jit(solution)/shard_map/ppermute | solution.py:42
  16.3 0.1 collective-permute-start.4
  16.4 0.0 copy-done.5
  16.4 0.1 and_select_fusion.3
  16.5 0.1 add_add_fusion.where_ref
  16.6 0.0 copy-start.1
  16.6 0.0 copy-start.3
  16.6 1.3 %collective-permute-done.4.far_ref = bf16[8,4,3072]{2,1,0:T(4,128)(2,1)S(1)} collective-permute-done((bf16[8,4,3072]{2,1,0:T(4,128)(2,1)S(1)}, bf16[8,4,3072]{2,1,0:T(4,128)(2,1)S(1)}, u32[]{:S(2)}, u32[]{:S(2)}) %collective-permute-start.4) | collective-permute-done | bytes 196640 | tf_op jit(solution)/shard_map/ppermute | solution.py:42
  17.8 0.0 slice-done
  17.8 0.0 slice-done.1
  17.8 0.0 copy-done
  17.8 0.0 copy-done.2
  17.8 2.6 %shard_map.143 = (bf16[32,4,512]{2,1,0:T(4,128)(2,1)S(1)}, bf16[4,1024]{1,0:T(4,128)(2,1)}, bf16[4,1024]{1,0:T(4,128)(2,1)}) custom-call(s32[2,4]{1,0:T(2,128)S(1)} %pad_add_fusion.places_ref, bf16[8,4,3072]{2,1,0:T(4,128)(2,1)S(1)} %shard_map.142.near_ref, bf16[8,4,3072]{2,1,0:T(4,128)(2,1)S(1)} %collective-permute-done.4.far_ref, ...), custom_call_target="tpu_custom_call" | custom-call | tf_op jit(solution)/shard_map/pallas_call | solution.py:233
  20.5 14.6 %all_to_all.5.terms_ref = bf16[32,4,512]{2,1,0:T(4,128)(2,1)S(1)} all-to-all(bf16[32,4,512]{2,1,0:T(4,128)(2,1)S(1)} %get-tuple-element.16), channel_id=1, replica_groups=mesh['req'=16,'tp'=2] {'req','tp'}, dimensions={0} | all-to-all | bytes 262144 | tf_op jit(solution)/shard_map/all_to_all | solution.py:246
  35.0 0.2 shard_map.144
  35.2 0.1 collective-permute-start.5
  35.3 1.2 %collective-permute-done.5.other_ref = bf16[4,512]{1,0:T(4,128)(2,1)S(1)} collective-permute-done((bf16[4,512]{1,0:T(4,128)(2,1)S(1)}, bf16[4,512]{1,0:T(4,128)(2,1)S(1)}, u32[]{:S(2)}, u32[]{:S(2)}) %collective-permute-start.5) | collective-permute-done | bytes 4128 | tf_op jit(solution)/shard_map/ppermute | solution.py:260
  36.4 0.0 copy-done.1
  36.4 0.0 copy-done.3
  36.4 0.6 %shard_map.145 = bf16[4,1024]{1,0:T(4,128)(2,1)} custom-call(s32[3,8]{1,0:T(4,128)S(1)} %add_add_fusion.where_ref, bf16[4,512]{1,0:T(4,128)(2,1)S(1)} %get-tuple-element.17.mine_ref, bf16[4,512]{1,0:T(4,128)(2,1)S(1)} %collective-permute-done.5.other_ref, bf16[4,1024]{1,0:T(4,128)(2,1)S(1)} %copy-done.1, bf16[1024]{0:T(1024)(128)(2,1)S(1)} %copy-done.3), custom_call_target="tpu_custom_call" | custom-call | tf_op jit(solution)/shard_map/pallas_call | solution.py:254
  (17 shorter events, 0.1 us)
Async XLA Ops:
  1.4 5.9 %collective-permute-start = (bf16[1,4,3072]{2,1,0:T(4,128)(2,1)S(1)}, bf16[1,4,3072]{2,1,0:T(4,128)(2,1)S(1)}, u32[]{:S(2)}, u32[]{:S(2)}) collective-permute-start(bf16[1,4,3072]{2,1,0:T(4,128)(2,1)S(1)} %maximum_bitcast_fusion.own_ref), channel_id=1, source_target_pairs={{0,16},{2,18},{4,20},{6,22},{8,24},{10,26},{12,28},{14,30},{16,0},... | collective-permute-start | bytes 73736 | tf_op jit(solution)/shard_map/ppermute | solution.py:42
  7.3 4.2 %collective-permute-start.2 = (bf16[2,4,3072]{2,1,0:T(4,128)(2,1)S(1)}, bf16[2,4,3072]{2,1,0:T(4,128)(2,1)S(1)}, u32[]{:S(2)}, u32[]{:S(2)}) collective-permute-start(bf16[2,4,3072]{2,1,0:T(4,128)(2,1)S(1)} %shard_map.139.own_ref), channel_id=1, source_target_pairs={{0,8},{2,10},{4,12},{6,14},{8,0},{10,2},{12,4},{14,6},{16,24},{18,... | collective-permute-start | bytes 147464 | tf_op jit(solution)/shard_map/ppermute | solution.py:42
  10.0 3.4 %copy-start.4 = (bf16[24,128,1024]{2,1,0:T(8,128)(2,1)S(1)}, bf16[24,128,1024]{2,1,0:T(8,128)(2,1)}, u32[]{:S(2)}) copy-start(bf16[24,128,1024]{2,1,0:T(8,128)(2,1)} %pages_ref.1) | copy-start | bytes 18874372
  10.0 1.3 %collective-permute-start.1 = (s32[4]{0:T(128)}, s32[4]{0:T(128)S(1)}, u32[]{:S(2)}, u32[]{:S(2)}) collective-permute-start(s32[4]{0:T(128)} %param.22), channel_id=1, source_target_pairs={{0,2},{2,0},{4,6},{6,4},{8,10},{10,8},{12,14},{14,12},{16,18},{18,... | collective-permute-start | bytes 56 | tf_op jit(solution)/shard_map/ppermute | solution.py:219
  11.5 6.3 %slice-start = ((s8[6291456]{0:T(1024)(128)(4,1)}), s8[4194304]{0:T(1024)(128)(4,1)S(1)}, s32[]{:S(2)}) async-start(s8[6291456]{0:T(1024)(128)(4,1)} %bitcast.10), calls=%async_computation.1 | async-start | bytes 8388608
  11.5 6.3 %slice-start.1 = ((s8[6291456]{0:T(1024)(128)(4,1)}), s8[2097152]{0:T(1024)(128)(4,1)S(1)}, s32[]{:S(2)}) async-start(s8[6291456]{0:T(1024)(128)(4,1)} %bitcast.10), calls=%async_computation.2 | async-start | bytes 4194304
  11.5 4.8 %collective-permute-start.3 = (bf16[4,4,3072]{2,1,0:T(4,128)(2,1)S(1)}, bf16[4,4,3072]{2,1,0:T(4,128)(2,1)S(1)}, u32[]{:S(2)}, u32[]{:S(2)}) collective-permute-start(bf16[4,4,3072]{2,1,0:T(4,128)(2,1)S(1)} %shard_map.140.after_ref.own_ref), channel_id=1, source_target_pairs={{0,4},{2,6},{4,0},{6,2},{8,12},{10,14},{12,8},{14,10},{16,20},{18,... | collective-permute-start | bytes 294920 | tf_op jit(solution)/shard_map/ppermute | solution.py:42
  15.4 1.0 %copy-start.5 = (s32[4]{0:T(128)S(1)}, s32[4]{0:T(128)}, u32[]{:S(2)}) copy-start(s32[4]{0:T(128)} %param.22) | copy-start | bytes 52
  15.4 2.4 %copy-start = (bf16[1024,2048]{1,0:T(8,128)(2,1)S(1)}, bf16[1024,2048]{1,0:T(8,128)(2,1)}, u32[]{:S(2)}) copy-start(bf16[1024,2048]{1,0:T(8,128)(2,1)} %weight_ref.1) | copy-start | bytes 12582916
  15.4 2.4 %copy-start.2 = (s32[4,8]{1,0:T(4,128)S(1)}, s32[4,8]{1,0:T(4,128)}, u32[]{:S(2)}) copy-start(s32[4,8]{1,0:T(4,128)} %table_ref.1) | copy-start | bytes 388
  16.3 1.5 %collective-permute-start.4 = (bf16[8,4,3072]{2,1,0:T(4,128)(2,1)S(1)}, bf16[8,4,3072]{2,1,0:T(4,128)(2,1)S(1)}, u32[]{:S(2)}, u32[]{:S(2)}) collective-permute-start(bf16[8,4,3072]{2,1,0:T(4,128)(2,1)S(1)} %shard_map.142.near_ref), channel_id=1, source_target_pairs={{0,2},{2,0},{4,6},{6,4},{8,10},{10,8},{12,14},{14,12},{16,18},{18,... | collective-permute-start | bytes 589832 | tf_op jit(solution)/shard_map/ppermute | solution.py:42
  16.6 19.9 %copy-start.1 = (bf16[4,1024]{1,0:T(4,128)(2,1)S(1)}, bf16[4,1024]{1,0:T(4,128)(2,1)}, u32[]{:S(2)}) copy-start(bf16[4,1024]{1,0:T(4,128)(2,1)} %residual_ref.1) | copy-start | bytes 24580
  16.6 19.9 %copy-start.3 = (bf16[1024]{0:T(1024)(128)(2,1)S(1)}, bf16[1024]{0:T(1024)(128)(2,1)}, u32[]{:S(2)}) copy-start(bf16[1024]{0:T(1024)(128)(2,1)} %bias_ref.1) | copy-start | bytes 6148
  35.2 1.2 %collective-permute-start.5 = (bf16[4,512]{1,0:T(4,128)(2,1)S(1)}, bf16[4,512]{1,0:T(4,128)(2,1)S(1)}, u32[]{:S(2)}, u32[]{:S(2)}) collective-permute-start(bf16[4,512]{1,0:T(4,128)(2,1)S(1)} %get-tuple-element.18), channel_id=1, source_target_pairs={{0,2},{2,0},{4,6},{6,4},{8,10},{10,8},{12,14},{14,12},{16,18},{18,... | collective-permute-start | bytes 12296 | tf_op jit(solution)/shard_map/ppermute | solution.py:260

commit v10 on v9

--- a/solution.py
+++ b/solution.py
@@ -167,7 +167,14 @@
         return exps.astype(BF16), own_exp * own_value, 1.0 / total
 
     def gather_values(first, exps, own, share):
-        seen = jnp.dot(exps, values_ref[:, :, first:first + lanes].reshape(tokens, lanes), preferred_element_type=F32)
+        seen = sum(
+            jnp.dot(
+                exps[:, p * page:(p + pages // 2) * page],
+                values_ref[p:p + pages // 2, :, first:first + lanes].reshape(tokens // 2, lanes),
+                preferred_element_type=F32,
+            )
+            for p in (0, pages // 2)
+        )
         seen = jnp.where(mine, (seen + own) * share, 0.0)
         return sum(seen[h * slots:(h + 1) * slots] for h in range(together))
 

time: 37.4 us -> 37.3 us (level)
  no operation moved by 1% of the time
where the time goes in v10:
time: 37.3 us; the launch traced here: 37 us
  blocking collectives  14.6 us (39%)
  starting transfers between devices  8.04 us (22%)
  Pallas kernels  5.35 us (14%)
  waiting for transfers between devices  4.72 us (13%)
  other arithmetic  2.46 us (7%)
  local copies, waits for them, and re-layouts  1.09 us (3%)
  between operations  0.81 us (2%)
    all_to_all x1, blocking collectives, on_device(): terms = lax.all_to_all(sent, ('req', 'tp'), 0, 0, tiled=True)  14.6 us
    ppermute x4, starting transfers between devices, gather_by_doubling(): other = lax.ppermute(held, 'req', [(i, i ^ bit) for i in range(devices)])  7.97 us
    pallas_call x1, Pallas kernels, on_device(): pl.pallas_call(functools.partial(attend, devices, parts), out_shape=(jax....  2.58 us
    ppermute x4, waiting for transfers between devices, gather_by_doubling(): other = lax.ppermute(held, 'req', [(i, i ^ bit) for i in range(devices)])  2.31 us
    pallas_call x1, Pallas kernels, turned(): pl.pallas_call(turn, out_shape=jax.ShapeDtypeStruct((width, pages * page)...  1.95 us
    ppermute x1, waiting for transfers between devices, integers(): return (lax.ppermute(slots, 'req', other_core), long[:, None])  1.25 us
    ppermute x1, waiting for transfers between devices, on_device(): lax.ppermute(theirs, 'req', other_core)  1.15 us
  transfers between devices with their start and end apart: 6, of which 5 were waited for; matrix products, arithmetic and copies ran while one was open for 7% of the time, Pallas kernels for 5%

profile of v10, /device:TPU:0, one launch (start us, length us, event | category | flops | bytes accessed | tf_op | source)
XLA Modules:
  0.0 37.0 jit_solution(4561100935269481416)
XLA Ops:
  0.6 0.7 %maximum_bitcast_fusion.own_ref = bf16[1,4,3072]{2,1,0:T(4,128)(2,1)S(1)} fusion(bf16[4,1024]{1,0:T(4,128)(2,1)} %param.14, bf16[4,1024]{1,0:T(4,128)(2,1)} %param.13, bf16[4,1024]{1,0:T(4,128)(2,1)} %param.12), kind=kLoop, calls=%fused_computation.1 | loop fusion | flops 73728 | bytes 49152 | tf_op jit(solution)/shard_map/broadcast_in_dim | solution.py:38
  1.4 4.1 %collective-permute-start = (bf16[1,4,3072]{2,1,0:T(4,128)(2,1)S(1)}, bf16[1,4,3072]{2,1,0:T(4,128)(2,1)S(1)}, u32[]{:S(2)}, u32[]{:S(2)}) collective-permute-start(bf16[1,4,3072]{2,1,0:T(4,128)(2,1)S(1)} %maximum_bitcast_fusion.own_ref), channel_id=1, source_target_pairs={{0,16},{2,18},{4,20},{6,22},{8,24},{10,26},{12,28},{14,30},{16,0},... | collective-permute-start | bytes 73736 | tf_op jit(solution)/shard_map/ppermute | solution.py:42
  5.5 0.7 %convert_element_type.3 = f32[4]{0:T(128)S(1)} convert(s32[4]{0:T(128)} %param.21) | non-fusion elementwise | flops 4 | bytes 32 | tf_op jit(solution)/shard_map/convert_element_type | solution.py:80
  6.2 0.1 pad.11.clone
  6.2 0.1 pad.8.clone
  6.3 0.1 multiply_cosine_fusion
  6.4 0.1 maximum_maximum_fusion.1
  6.6 0.7 %fusion.4 = (s32[1,4]{1,0:T(1,128)S(1)}, s32[1,4]{1,0:T(1,128)S(1)}) fusion(s32[4]{0:T(128)} %param.23, s32[]{:T(128)S(6)} %axis_index.19), kind=kLoop, calls=%fused_computation.29 | loop fusion | flops 140 | bytes 52 | tf_op jit(solution)/shard_map/stack | solution.py:59
  7.3 0.0 collective-permute-done.other_ref
  7.3 1.9 %collective-permute-start.2 = (bf16[2,4,3072]{2,1,0:T(4,128)(2,1)S(1)}, bf16[2,4,3072]{2,1,0:T(4,128)(2,1)S(1)}, u32[]{:S(2)}, u32[]{:S(2)}) collective-permute-start(bf16[2,4,3072]{2,1,0:T(4,128)(2,1)S(1)} %shard_map.139.own_ref), channel_id=1, source_target_pairs={{0,8},{2,10},{4,12},{6,14},{8,0},{10,2},{12,4},{14,6},{16,24},{18,... | collective-permute-start | bytes 147464 | tf_op jit(solution)/shard_map/ppermute | solution.py:42
  9.2 0.1 pad.16.clone
  9.3 0.7 %copy.15.rest_1_.lengths_ref = s32[4,1]{1,0:T(4,128)S(1)} copy(s32[4,1]{0,1:T(1,128)} %bitcast.13) | data formatting | bytes 32 | tf_op jit(solution)/shard_map/broadcast_in_dim | solution.py:226
  10.0 0.0 copy-start.4
  10.0 0.0 collective-permute-start.1
  10.0 1.3 %collective-permute-done.1.rest_0_ = s32[4]{0:T(128)S(1)} collective-permute-done((s32[4]{0:T(128)}, s32[4]{0:T(128)S(1)}, u32[]{:S(2)}, u32[]{:S(2)}) %collective-permute-start.1) | collective-permute-done | bytes 48 | tf_op jit(solution)/shard_map/ppermute | solution.py:226
  11.3 0.2 collective-permute-done.2.other_ref
  11.5 0.0 slice-start
  11.5 0.0 slice-start.1
  11.5 1.9 %collective-permute-start.3 = (bf16[4,4,3072]{2,1,0:T(4,128)(2,1)S(1)}, bf16[4,4,3072]{2,1,0:T(4,128)(2,1)S(1)}, u32[]{:S(2)}, u32[]{:S(2)}) collective-permute-start(bf16[4,4,3072]{2,1,0:T(4,128)(2,1)S(1)} %shard_map.140.after_ref.own_ref), channel_id=1, source_target_pairs={{0,4},{2,6},{4,0},{6,2},{8,12},{10,14},{12,8},{14,10},{16,20},{18,... | collective-permute-start | bytes 294920 | tf_op jit(solution)/shard_map/ppermute | solution.py:42
  13.4 0.0 copy-done.4
  13.4 1.9 %shard_map.141.rest_0_.keys_ref = bf16[1024,3072]{1,0:T(8,128)(2,1)S(1)} custom-call(bf16[24,128,1024]{2,1,0:T(8,128)(2,1)S(1)} %copy-done.4, bf16[4,4,3072]{2,1,0:T(4,128)(2,1)S(1)} %shard_map.140.after_ref.own_ref), custom_call_target="tpu_custom_call" | custom-call | flops 4294967296 | bytes 1048576 | tf_op jit(solution)/shard_map/pallas_call | solution.py:99
  15.4 0.0 copy-start.5
  15.4 0.0 copy-start
  15.4 0.0 copy-start.2
  15.4 0.9 %collective-permute-done.3.other_ref = bf16[4,4,3072]{2,1,0:T(4,128)(2,1)S(1)} collective-permute-done((bf16[4,4,3072]{2,1,0:T(4,128)(2,1)S(1)}, bf16[4,4,3072]{2,1,0:T(4,128)(2,1)S(1)}, u32[]{:S(2)}, u32[]{:S(2)}) %collective-permute-start.3) | collective-permute-done | bytes 98336 | tf_op jit(solution)/shard_map/ppermute | solution.py:42
  16.3 0.1 collective-permute-start.4
  16.4 0.0 copy-done.5
  16.4 0.1 and_select_fusion.3
  16.5 0.1 add_add_fusion.where_ref
  16.6 0.0 copy-start.1
  16.6 0.0 copy-start.3
  16.6 1.3 %collective-permute-done.4.far_ref = bf16[8,4,3072]{2,1,0:T(4,128)(2,1)S(1)} collective-permute-done((bf16[8,4,3072]{2,1,0:T(4,128)(2,1)S(1)}, bf16[8,4,3072]{2,1,0:T(4,128)(2,1)S(1)}, u32[]{:S(2)}, u32[]{:S(2)}) %collective-permute-start.4) | collective-permute-done | bytes 196640 | tf_op jit(solution)/shard_map/ppermute | solution.py:42
  17.8 0.0 slice-done
  17.8 0.0 slice-done.1
  17.8 0.0 copy-done
  17.8 0.0 copy-done.2
  17.8 2.6 %shard_map.143 = (bf16[32,4,512]{2,1,0:T(4,128)(2,1)S(1)}, bf16[4,1024]{1,0:T(4,128)(2,1)}, bf16[4,1024]{1,0:T(4,128)(2,1)}) custom-call(s32[2,4]{1,0:T(2,128)S(1)} %pad_add_fusion.places_ref, bf16[8,4,3072]{2,1,0:T(4,128)(2,1)S(1)} %shard_map.142.near_ref, bf16[8,4,3072]{2,1,0:T(4,128)(2,1)S(1)} %collective-permute-done.4.far_ref, ...), custom_call_target="tpu_custom_call" | custom-call | tf_op jit(solution)/shard_map/pallas_call | solution.py:240
  20.4 14.6 %all_to_all.5.terms_ref = bf16[32,4,512]{2,1,0:T(4,128)(2,1)S(1)} all-to-all(bf16[32,4,512]{2,1,0:T(4,128)(2,1)S(1)} %get-tuple-element.16), channel_id=1, replica_groups=mesh['req'=16,'tp'=2] {'req','tp'}, dimensions={0} | all-to-all | bytes 262144 | tf_op jit(solution)/shard_map/all_to_all | solution.py:253
  35.0 0.2 shard_map.144
  35.2 0.1 collective-permute-start.5
  35.2 1.2 %collective-permute-done.5.other_ref = bf16[4,512]{1,0:T(4,128)(2,1)S(1)} collective-permute-done((bf16[4,512]{1,0:T(4,128)(2,1)S(1)}, bf16[4,512]{1,0:T(4,128)(2,1)S(1)}, u32[]{:S(2)}, u32[]{:S(2)}) %collective-permute-start.5) | collective-permute-done | bytes 4128 | tf_op jit(solution)/shard_map/ppermute | solution.py:267
  36.4 0.0 copy-done.1
  36.4 0.0 copy-done.3
  36.4 0.6 %shard_map.145 = bf16[4,1024]{1,0:T(4,128)(2,1)} custom-call(s32[3,8]{1,0:T(4,128)S(1)} %add_add_fusion.where_ref, bf16[4,512]{1,0:T(4,128)(2,1)S(1)} %get-tuple-element.17.mine_ref, bf16[4,512]{1,0:T(4,128)(2,1)S(1)} %collective-permute-done.5.other_ref, bf16[4,1024]{1,0:T(4,128)(2,1)S(1)} %copy-done.1, bf16[1024]{0:T(1024)(128)(2,1)S(1)} %copy-done.3), custom_call_target="tpu_custom_call" | custom-call | tf_op jit(solution)/shard_map/pallas_call | solution.py:261
  (17 shorter events, 0.1 us)
Async XLA Ops:
  1.4 5.9 %collective-permute-start = (bf16[1,4,3072]{2,1,0:T(4,128)(2,1)S(1)}, bf16[1,4,3072]{2,1,0:T(4,128)(2,1)S(1)}, u32[]{:S(2)}, u32[]{:S(2)}) collective-permute-start(bf16[1,4,3072]{2,1,0:T(4,128)(2,1)S(1)} %maximum_bitcast_fusion.own_ref), channel_id=1, source_target_pairs={{0,16},{2,18},{4,20},{6,22},{8,24},{10,26},{12,28},{14,30},{16,0},... | collective-permute-start | bytes 73736 | tf_op jit(solution)/shard_map/ppermute | solution.py:42
  7.3 4.2 %collective-permute-start.2 = (bf16[2,4,3072]{2,1,0:T(4,128)(2,1)S(1)}, bf16[2,4,3072]{2,1,0:T(4,128)(2,1)S(1)}, u32[]{:S(2)}, u32[]{:S(2)}) collective-permute-start(bf16[2,4,3072]{2,1,0:T(4,128)(2,1)S(1)} %shard_map.139.own_ref), channel_id=1, source_target_pairs={{0,8},{2,10},{4,12},{6,14},{8,0},{10,2},{12,4},{14,6},{16,24},{18,... | collective-permute-start | bytes 147464 | tf_op jit(solution)/shard_map/ppermute | solution.py:42
  10.0 3.4 %copy-start.4 = (bf16[24,128,1024]{2,1,0:T(8,128)(2,1)S(1)}, bf16[24,128,1024]{2,1,0:T(8,128)(2,1)}, u32[]{:S(2)}) copy-start(bf16[24,128,1024]{2,1,0:T(8,128)(2,1)} %pages_ref.1) | copy-start | bytes 18874372
  10.0 1.3 %collective-permute-start.1 = (s32[4]{0:T(128)}, s32[4]{0:T(128)S(1)}, u32[]{:S(2)}, u32[]{:S(2)}) collective-permute-start(s32[4]{0:T(128)} %param.22), channel_id=1, source_target_pairs={{0,2},{2,0},{4,6},{6,4},{8,10},{10,8},{12,14},{14,12},{16,18},{18,... | collective-permute-start | bytes 56 | tf_op jit(solution)/shard_map/ppermute | solution.py:226
  11.5 6.3 %slice-start = ((s8[6291456]{0:T(1024)(128)(4,1)}), s8[4194304]{0:T(1024)(128)(4,1)S(1)}, s32[]{:S(2)}) async-start(s8[6291456]{0:T(1024)(128)(4,1)} %bitcast.10), calls=%async_computation.1 | async-start | bytes 8388608
  11.5 6.3 %slice-start.1 = ((s8[6291456]{0:T(1024)(128)(4,1)}), s8[2097152]{0:T(1024)(128)(4,1)S(1)}, s32[]{:S(2)}) async-start(s8[6291456]{0:T(1024)(128)(4,1)} %bitcast.10), calls=%async_computation.2 | async-start | bytes 4194304
  11.5 4.8 %collective-permute-start.3 = (bf16[4,4,3072]{2,1,0:T(4,128)(2,1)S(1)}, bf16[4,4,3072]{2,1,0:T(4,128)(2,1)S(1)}, u32[]{:S(2)}, u32[]{:S(2)}) collective-permute-start(bf16[4,4,3072]{2,1,0:T(4,128)(2,1)S(1)} %shard_map.140.after_ref.own_ref), channel_id=1, source_target_pairs={{0,4},{2,6},{4,0},{6,2},{8,12},{10,14},{12,8},{14,10},{16,20},{18,... | collective-permute-start | bytes 294920 | tf_op jit(solution)/shard_map/ppermute | solution.py:42
  15.4 1.0 %copy-start.5 = (s32[4]{0:T(128)S(1)}, s32[4]{0:T(128)}, u32[]{:S(2)}) copy-start(s32[4]{0:T(128)} %param.22) | copy-start | bytes 52
  15.4 2.4 %copy-start = (bf16[1024,2048]{1,0:T(8,128)(2,1)S(1)}, bf16[1024,2048]{1,0:T(8,128)(2,1)}, u32[]{:S(2)}) copy-start(bf16[1024,2048]{1,0:T(8,128)(2,1)} %weight_ref.1) | copy-start | bytes 12582916
  15.4 2.4 %copy-start.2 = (s32[4,8]{1,0:T(4,128)S(1)}, s32[4,8]{1,0:T(4,128)}, u32[]{:S(2)}) copy-start(s32[4,8]{1,0:T(4,128)} %table_ref.1) | copy-start | bytes 388
  16.3 1.5 %collective-permute-start.4 = (bf16[8,4,3072]{2,1,0:T(4,128)(2,1)S(1)}, bf16[8,4,3072]{2,1,0:T(4,128)(2,1)S(1)}, u32[]{:S(2)}, u32[]{:S(2)}) collective-permute-start(bf16[8,4,3072]{2,1,0:T(4,128)(2,1)S(1)} %shard_map.142.near_ref), channel_id=1, source_target_pairs={{0,2},{2,0},{4,6},{6,4},{8,10},{10,8},{12,14},{14,12},{16,18},{18,... | collective-permute-start | bytes 589832 | tf_op jit(solution)/shard_map/ppermute | solution.py:42
  16.6 19.8 %copy-start.1 = (bf16[4,1024]{1,0:T(4,128)(2,1)S(1)}, bf16[4,1024]{1,0:T(4,128)(2,1)}, u32[]{:S(2)}) copy-start(bf16[4,1024]{1,0:T(4,128)(2,1)} %residual_ref.1) | copy-start | bytes 24580
  16.6 19.8 %copy-start.3 = (bf16[1024]{0:T(1024)(128)(2,1)S(1)}, bf16[1024]{0:T(1024)(128)(2,1)}, u32[]{:S(2)}) copy-start(bf16[1024]{0:T(1024)(128)(2,1)} %bias_ref.1) | copy-start | bytes 6148
  35.2 1.2 %collective-permute-start.5 = (bf16[4,512]{1,0:T(4,128)(2,1)S(1)}, bf16[4,512]{1,0:T(4,128)(2,1)S(1)}, u32[]{:S(2)}, u32[]{:S(2)}) collective-permute-start(bf16[4,512]{1,0:T(4,128)(2,1)S(1)} %get-tuple-element.18), channel_id=1, source_target_pairs={{0,2},{2,0},{4,6},{6,4},{8,10},{10,8},{12,14},{14,12},{16,18},{18,... | collective-permute-start | bytes 12296 | tf_op jit(solution)/shard_map/ppermute | solution.py:267
